TPU v7x, 512 devices: a whole 4x8x8 slice. The times are simulated.
512 devices in a mesh: group: 8 (over y), dev: 64 (over x, z, core).
Axes of the slice: x: 4, y: 8, z: 8, core: 2. Of those that a mesh axis runs over, the one named last changes fastest.
Arguments:
- displacement: float32 [3, 131072], P(None, ('group', 'dev')), may hold values from -6 to 6
- connectivity: int32 [8, 32768], P(None, ('group', 'dev')), may hold values from 0 to 1279, as said below
- face_nodes: int32 [512, 64, 16], P(('group', 'dev')), may hold values from 0 to 255, as said below
- strain_map: float32 [6, 24, 32768], P(None, None, ('group', 'dev')), may hold values from -1.25 to 1.25
- assignment: int32 [32768], P(('group', 'dev')), may hold values from -1 to 1023, as said below
- phases: int32 [8, 64, 3072], P('group', None, 'dev'), may hold values 0 or 1
- load_map: float32 [6, 64, 3072], P(None, None, 'dev'), may hold values from -0.013671875 to 0.013671875
- stiff_root: float32 [64, 64], replicated, may hold values from -0.75 to 0.75
- chain_map: float32 [64, 64], replicated, may hold values from -0.75 to 0.75
- bridge_map: float32 [16, 16], replicated, may hold values from -1.5 to 1.5
- elastic: float32 [6, 6], replicated, may hold values from -2.5 to 2.5
Outputs:
- stress: float32 [6, 32768], P(None, ('group', 'dev'))
- fluctuation: float32 [8, 64, 3072, 128], P('group', None, 'dev')
Inputs may be any that keep to these rules, and one draw needn't show every extreme that they name: `connectivity`: an entry below 256 names an own node; 256 + p * 16 + j names slot j from partner p. Each partition has exactly 6 partners in its section, each with 1 to 16 live slots (its first partner exactly 16); only live slots are named and every live slot is named. `face_nodes`: slots that the receiver does not name hold arbitrary own nodes. `assignment`: each value 0 to 1023 appears exactly once; all others are -1. At most 8 non-negative entries lie on one partition, reached in every section. Among the Gauss points of one section at most 32 values lie in [h * 128, (h + 1) * 128) for any h, reached in every draw.
All inputs are finite; a program needn't handle non-finite values. No bound on the sum of `phases` on one device may be relied on, other than what follows from the above.
Results may differ from a plain program's by a relative error of at most 0.00022.
Values sent between devices are 32-bit elements; how exact they have to be, the bound alone decides.
No kernel may reach another device: no remote copies, remote signals or barrier semaphores. Data moves between devices by JAX's collectives and lax.ppermute only.
A program may use at most 128 MiB of HBM per device.

v0:
```python
import math

import jax
import jax.numpy as jnp
from jax import lax
from jax.sharding import PartitionSpec as P

BLOCK = 64
IFACE = 16
BLOCKS = 48
POINTS = 128
PLASTIC_CAP = 8
ITERS = 4


ridge = 0.5


def shifted(shard, axis, by):
    devices = lax.axis_size(axis)
    return lax.ppermute(shard, axis, [(i, (i + by) % devices) for i in range(devices)])


def apply_block(field, weights, stiff_root, chain_map, bridge_map):
    highest = lax.Precision.HIGHEST
    top = BLOCK - IFACE
    lower = shifted(field[top:], "dev", 1)
    upper = shifted(field[:IFACE], "dev", -1)
    shape = field.shape
    lifted = jnp.dot(stiff_root, field.reshape(BLOCK, -1), precision=highest).reshape(shape)
    core = jnp.dot(
        stiff_root.T, (weights[:, :, None] * lifted).reshape(BLOCK, -1), precision=highest
    ).reshape(shape)
    following = jnp.roll(field, -1, axis=1)
    edge = field - jnp.dot(chain_map, following.reshape(BLOCK, -1), precision=highest).reshape(
        shape
    )
    behind = jnp.dot(chain_map.T, edge.reshape(BLOCK, -1), precision=highest).reshape(shape)
    result = ridge * field + core + edge - jnp.roll(behind, 1, axis=1)
    face = field[top:] - jnp.einsum("ij,jks->iks", bridge_map, upper, precision=highest)
    below = lower - jnp.einsum("ij,jks->iks", bridge_map, field[:IFACE], precision=highest)
    pull = jnp.einsum("ji,jks->iks", bridge_map, below, precision=highest)
    return jnp.concatenate([result[:IFACE] - pull, result[IFACE:top], result[top:] + face], axis=0)


def spread(values):
    return values[None, None, :]


def squares(residual):
    return lax.psum(jnp.sum(residual * residual, axis=(0, 1)), "dev")


def local(
    displacement,
    connectivity,
    face_nodes,
    strain_map,
    assignment,
    phases,
    load_map,
    stiff_root,
    chain_map,
    bridge_map,
    elastic,
):
    highest = lax.Precision.HIGHEST
    outgoing = displacement[:, face_nodes[0]]
    arrived = lax.all_to_all(outgoing, "dev", split_axis=1, concat_axis=1, tiled=True)
    table = jnp.concatenate([displacement, arrived.reshape(3, -1)], axis=1)
    nodal = table[:, connectivity]
    nodal = jnp.transpose(nodal, (1, 0, 2)).reshape(24, -1)
    strain = jnp.sum(strain_map * nodal[None], axis=1)
    plastic = assignment >= 0
    rank = jnp.cumsum(plastic.astype(jnp.int32)) - 1
    select = plastic[:, None] & (rank[:, None] == jnp.arange(PLASTIC_CAP, dtype=jnp.int32)[None])
    pick = select.astype(jnp.float32)
    cand_strain = jnp.dot(strain, pick, precision=highest)
    cand_target = jnp.where(
        jnp.any(select, axis=0), jnp.sum(jnp.where(select, assignment[:, None], 0), axis=0), -1
    )
    sec_strain, sec_target = (
        lax.all_gather(cand_strain, "dev", axis=1, tiled=True),
        lax.all_gather(cand_target, "dev", axis=0, tiled=True),
    )
    groups = lax.axis_size("group")
    devs = lax.axis_size("dev")
    route_cap = 2 * POINTS // groups
    dest = jnp.where(sec_target >= 0, sec_target // POINTS, groups)
    member = dest[:, None] == jnp.arange(groups, dtype=jnp.int32)[None]
    position = jnp.sum(
        jnp.where(member, jnp.cumsum(member.astype(jnp.int32), axis=0) - 1, 0), axis=1
    )
    slot_index = jnp.where(dest < groups, dest * route_cap + position, groups * route_cap).astype(
        jnp.int32
    )
    send_strain = (
        jnp.zeros((6, groups * route_cap + 1), jnp.float32).at[:, slot_index].set(sec_strain)
    )
    send_strain = send_strain[:, : groups * route_cap].reshape(6, groups, route_cap)
    send_slot = (
        jnp.full((groups * route_cap + 1,), POINTS, jnp.int32)
        .at[slot_index]
        .set(sec_target % POINTS)
    )
    send_slot = send_slot[: groups * route_cap].reshape(1, groups, route_cap)
    got_strain, got_slot = (
        lax.all_to_all(send_strain, "group", split_axis=1, concat_axis=1, tiled=True),
        lax.all_to_all(send_slot, "group", split_axis=1, concat_axis=1, tiled=True),
    )
    placed = (got_slot.reshape(-1)[:, None] == jnp.arange(POINTS, dtype=jnp.int32)[None]).astype(
        jnp.float32
    )
    point_strain = jnp.dot(got_strain.reshape(6, -1), placed, precision=highest)
    rhs = jnp.einsum("cik,cs->iks", load_map, point_strain, precision=highest)
    weights = 1.0 + 2.0 * phases[0].astype(jnp.float32)
    solution = jnp.zeros_like(rhs)
    residual = rhs
    direction = rhs
    norm_now = squares(residual)
    for step in range(ITERS):
        image = apply_block(direction, weights, stiff_root, chain_map, bridge_map)
        alpha = norm_now / lax.psum(jnp.sum(direction * image, axis=(0, 1)), "dev")
        solution = solution + spread(alpha) * direction
        residual = residual - spread(alpha) * image
        if step + 1 < ITERS:
            norm_next = squares(residual)
            direction = residual + spread(norm_next / norm_now) * direction
            norm_now = norm_next
    scale_out = math.sqrt(BLOCK * devs * BLOCKS)
    fluctuation = (scale_out * solution)[None]
    partial_stress = jnp.einsum("cik,iks->cs", load_map, solution, precision=highest)
    point_stress = jnp.dot(elastic, point_strain, precision=highest) + lax.psum(
        partial_stress, "dev"
    )
    outgoing_stress = jnp.dot(point_stress, placed.T, precision=highest).reshape(
        6, groups, route_cap
    )
    returned = lax.all_to_all(outgoing_stress, "group", split_axis=1, concat_axis=1, tiled=True)
    flat_back = jnp.concatenate([returned.reshape(6, -1), jnp.zeros((6, 1), jnp.float32)], axis=1)
    mine = lax.dynamic_slice_in_dim(slot_index, lax.axis_index("dev") * PLASTIC_CAP, PLASTIC_CAP)
    own_stress = flat_back[:, mine]
    plastic_stress = jnp.dot(own_stress, pick.T, precision=highest)
    stress = jnp.where(plastic[None], plastic_stress, jnp.dot(elastic, strain, precision=highest))
    return (stress, fluctuation)


def solution(mesh):
    in_specs = (
        P(None, ("group", "dev")),
        P(None, ("group", "dev")),
        P(("group", "dev"), None, None),
        P(None, None, ("group", "dev")),
        P(("group", "dev")),
        P("group", None, "dev"),
        P(None, None, "dev"),
        P(),
        P(),
        P(),
        P(),
    )
    out_specs = (P(None, ("group", "dev")), P("group", None, "dev", None))
    return jax.shard_map(local, mesh=mesh, in_specs=in_specs, out_specs=out_specs, check_vma=False)
```

profile of v0, /device:TPU:1, one launch (start us, length us, event | category | flops | bytes accessed | tf_op | source)
XLA Modules:
  0.0 1268.1 jit_solution(18290428097510317588)
XLA Ops:
  2.4 2.8 gather_fusion
  6.4 14.8 %all-to-all-start = ((f32[3,64,16]{2,0,1:T(4,128)}), f32[3,64,16]{2,0,1:T(4,128)S(1)}, u32[]{:S(2)}, u32[]{:S(2)}) async-start(f32[3,64,16]{2,0,1:T(4,128)} %bitcast.7), calls=%async_computation | async-start | bytes 262144 | tf_op jit(solution)/shard_map/all_to_all | solution.py:69
  23.8 17.2 %all-reduce.1 = s32[512]{0:T(512)S(1)} all-reduce(s32[512]{0:T(512)S(1)} %select_dynamic-update-slice_fusion), channel_id=1, replica_groups=mesh['group'=8,'dev'=64] {'dev'}, use_global_device_ids=true, to_apply=%add.1 | all-reduce | flops 512 | bytes 4096
  42.7 2.4 scatter_custom_fusion.1
  45.8 6.8 all-to-all-start.2
  54.4 46.6 %all_gather.7 = f32[6,512]{0,1:T(8,128)S(1)} all-gather(f32[6,8]{0,1:T(8,128)S(1)} %fusion.119), channel_id=1, replica_groups=mesh['group'=8,'dev'=64] {'dev'}, dimensions={1}, use_global_device_ids=true | all-gather | bytes 12480 | tf_op jit(solution)/shard_map/all_gather | solution.py:83
  103.5 7.1 all-to-all-start.1
  112.1 5.1 all-to-all-done.1
  118.8 2.7 fusion.94
  125.6 4.0 collective-permute-start
  135.1 2.1 collective-permute-start.1
  138.3 5.9 collective-permute-done.1
  145.3 126.3 %all-reduce.2 = (f32[128]{0:T(128)S(1)}, f32[128]{0:T(128)S(1)}) all-reduce(f32[128]{0:T(128)S(1)} %get-tuple-element.13, f32[128]{0:T(128)S(1)} %get-tuple-element.12), channel_id=1, replica_groups=mesh['group'=8,'dev'=64] {'dev'}, use_global_device_ids=true, to_apply=%region_10.11 | all-reduce | flops 256 | bytes 2048 | tf_op jit(solution)/shard_map/psum | solution.py:51
  272.0 129.1 %psum.65 = f32[128]{0:T(128)S(1)} all-reduce(f32[128]{0:T(128)S(1)} %multiply_reduce_fusion.4), channel_id=1, replica_groups=mesh['group'=8,'dev'=64] {'dev'}, use_global_device_ids=true, to_apply=%region_14.15 | all-reduce | flops 128 | bytes 1024 | tf_op jit(solution)/shard_map/psum | solution.py:51
  414.4 3.0 collective-permute-start.3
  418.4 5.1 collective-permute-done.3
  425.2 127.4 %psum.66 = f32[128]{0:T(128)S(1)} all-reduce(f32[128]{0:T(128)S(1)} %multiply_reduce_fusion.3), channel_id=1, replica_groups=mesh['group'=8,'dev'=64] {'dev'}, use_global_device_ids=true, to_apply=%region_16.17 | all-reduce | flops 128 | bytes 1024 | tf_op jit(solution)/shard_map/psum | solution.py:123
  552.6 3.4 multiply_reduce_fusion.2
  555.9 129.1 %psum.67 = f32[128]{0:T(128)S(1)} all-reduce(f32[128]{0:T(128)S(1)} %get-tuple-element.18), channel_id=1, replica_groups=mesh['group'=8,'dev'=64] {'dev'}, use_global_device_ids=true, to_apply=%region_18.19 | all-reduce | flops 128 | bytes 1024 | tf_op jit(solution)/shard_map/psum | solution.py:51
  698.9 2.7 collective-permute-start.5
  702.6 5.4 collective-permute-done.5
  709.7 127.4 %psum.68 = f32[128]{0:T(128)S(1)} all-reduce(f32[128]{0:T(128)S(1)} %multiply_reduce_fusion.1), channel_id=1, replica_groups=mesh['group'=8,'dev'=64] {'dev'}, use_global_device_ids=true, to_apply=%region_20.21 | all-reduce | flops 128 | bytes 1024 | tf_op jit(solution)/shard_map/psum | solution.py:123
  837.0 2.3 multiply_reduce_fusion
  839.3 129.1 %psum.69 = f32[128]{0:T(128)S(1)} all-reduce(f32[128]{0:T(128)S(1)} %multiply_reduce_fusion), channel_id=1, replica_groups=mesh['group'=8,'dev'=64] {'dev'}, use_global_device_ids=true, to_apply=%region_22.23 | all-reduce | flops 128 | bytes 1024 | tf_op jit(solution)/shard_map/psum | solution.py:51
  968.4 2.8 multiply_add_fusion.1
  983.2 2.8 collective-permute-start.7
  987.0 5.3 collective-permute-done.7
  993.3 127.4 %psum.70 = f32[128]{0:T(128)S(1)} all-reduce(f32[128]{0:T(128)S(1)} %fusion.44), channel_id=1, replica_groups=mesh['group'=8,'dev'=64] {'dev'}, use_global_device_ids=true, to_apply=%region_24.25 | all-reduce | flops 128 | bytes 1024 | tf_op jit(solution)/shard_map/psum | solution.py:123
  1120.6 3.8 multiply_bitcast_fusion
  1125.4 129.1 %psum.71 = f32[6,128]{1,0:T(8,128)S(1)} all-reduce(f32[6,128]{1,0:T(8,128)S(1)} %convolution_bitcast_fusion.21), channel_id=1, replica_groups=mesh['group'=8,'dev'=64] {'dev'}, use_global_device_ids=true, to_apply=%region_25.26 | all-reduce | flops 768 | bytes 6144 | tf_op jit(solution)/shard_map/psum | solution.py:133
  1255.7 3.3 all-to-all-start.3
  1261.1 4.4 all-to-all-done.3
  (204 shorter events, 79.0 us)
Async XLA Ops:
  0.6 118.2 %copy-start = (f32[6,64,48]{1,2,0:T(8,128)S(1)}, f32[6,64,48]{1,2,0:T(8,128)}, u32[]{:S(2)}) copy-start(f32[6,64,48]{1,2,0:T(8,128)} %param.17) | copy-start | bytes 221188
  0.6 52.1 %copy-start.22 = (f32[3,256]{1,0:T(4,128)S(1)}, f32[3,256]{1,0:T(4,128)}, u32[]{:S(2)}) copy-start(f32[3,256]{1,0:T(4,128)} %param.11) | copy-start | bytes 9220
  0.7 20.6 %copy-start.25 = (s32[64]{0:T(128)S(1)}, s32[64]{0:T(128)}, u32[]{:S(2)}) copy-start(s32[64]{0:T(128)} %param.15) | copy-start | bytes 772
  0.7 41.9 %copy-start.24 = (s32[8,64]{1,0:T(8,128)S(1)}, s32[8,64]{1,0:T(8,128)}, u32[]{:S(2)}) copy-start(s32[8,64]{1,0:T(8,128)} %param.12) | copy-start | bytes 6148
  0.7 42.0 %copy-start.21 = (s32[1,64,48]{1,2,0:T(8,128)S(1)}, s32[1,64,48]{1,2,0:T(8,128)}, u32[]{:S(2)}) copy-start(s32[1,64,48]{1,2,0:T(8,128)} %param.16) | copy-start | bytes 36868
  5.3 49.0 %copy-start.20 = (f32[6,24,64]{2,1,0:T(8,128)S(1)}, f32[6,24,64]{2,1,0:T(8,128)}, u32[]{:S(2)}) copy-start(f32[6,24,64]{2,1,0:T(8,128)} %param.14) | copy-start | bytes 110596
  6.4 39.5 %all-to-all-start = ((f32[3,64,16]{2,0,1:T(4,128)}), f32[3,64,16]{2,0,1:T(4,128)S(1)}, u32[]{:S(2)}, u32[]{:S(2)}) async-start(f32[3,64,16]{2,0,1:T(4,128)} %bitcast.7), calls=%async_computation | async-start | bytes 262144 | tf_op jit(solution)/shard_map/all_to_all | solution.py:69
  45.8 57.7 %all-to-all-start.2 = ((s32[1,8,32]{2,0,1:T(1,128)}), s32[1,8,32]{2,0,1:T(1,128)S(1)}, u32[]{:S(2)}, u32[]{:S(2)}) async-start(s32[1,8,32]{2,0,1:T(1,128)} %reshape.206), calls=%async_computation.2 | async-start | bytes 8192 | tf_op jit(solution)/shard_map/all_to_all | solution.py:109
  103.5 13.7 %all-to-all-start.1 = ((f32[8,1,192]{2,1,0:T(1,128)}), f32[8,1,192]{2,1,0:T(1,128)S(1)}, u32[]{:S(2)}, u32[]{:S(2)}) async-start(f32[8,1,192]{2,1,0:T(1,128)} %reshape.307), calls=%async_computation.1 | async-start | bytes 16384 | tf_op jit(solution)/shard_map/all_to_all | solution.py:108
  125.6 4.5 copy-start.18
  125.6 11.6 collective-permute-start
  130.1 2.0 copy-start.3
  135.0 2.2 copy-start.19
  135.1 136.5 %copy-start.7 = (f32[32,48,128]{2,0,1:T(8,128)}, f32[32,48,128]{2,0,1:T(8,128)S(1)}, u32[]{:S(2)}) copy-start(f32[32,48,128]{2,0,1:T(8,128)S(1)} %slice.187) | copy-start | bytes 2359300
  135.1 9.1 collective-permute-start.1
  138.3 133.3 %copy-start.9 = (f32[16,48,128]{2,0,1:T(8,128)}, f32[16,48,128]{2,0,1:T(8,128)S(1)}, u32[]{:S(2)}) copy-start(f32[16,48,128]{2,0,1:T(8,128)S(1)} %fusion.79) | copy-start | bytes 1179652
  144.7 126.9 %copy-start.10 = (f32[16,48,128]{2,0,1:T(8,128)}, f32[16,48,128]{2,0,1:T(8,128)S(1)}, u32[]{:S(2)}) copy-start(f32[16,48,128]{2,0,1:T(8,128)S(1)} %fusion.81) | copy-start | bytes 1179652
  406.3 11.1 collective-permute-start.2
  414.4 9.6 copy-start.11
  414.4 9.1 collective-permute-start.3
  418.4 5.6 copy-start.15
  686.7 21.7 %copy-start.1 = (f32[64,48,128]{2,0,1:T(8,128)}, f32[64,48,128]{2,0,1:T(8,128)S(1)}, u32[]{:S(2)}) copy-start(f32[64,48,128]{2,0,1:T(8,128)S(1)} %multiply_add_fusion.2) | copy-start | bytes 4718596
  690.7 10.9 collective-permute-start.4
  698.9 9.6 copy-start.8
  698.9 9.1 collective-permute-start.5
  702.6 5.9 copy-start.13
  971.1 21.7 %copy-start.2 = (f32[64,48,128]{2,0,1:T(8,128)}, f32[64,48,128]{2,0,1:T(8,128)S(1)}, u32[]{:S(2)}) copy-start(f32[64,48,128]{2,0,1:T(8,128)S(1)} %multiply_add_fusion.1) | copy-start | bytes 4718596
  975.1 10.9 collective-permute-start.6
  983.2 9.1 collective-permute-start.7
  1124.4 130.1 %copy-start.23 = (f32[6,6]{1,0:T(8,128)S(1)}, f32[6,6]{1,0:T(8,128)}, u32[]{:S(2)}) copy-start(f32[6,6]{1,0:T(8,128)} %param.21) | copy-start | bytes 436
  1124.4 134.6 %copy-start.12 = (f32[1,64,48,128]{3,1,2,0:T(8,128)S(1)}, f32[1,64,48,128]{3,1,2,0:T(8,128)}, u32[]{:S(2)}) copy-start(f32[1,64,48,128]{3,1,2,0:T(8,128)} %get-tuple-element.16) | copy-start | bytes 4718596
  1255.7 9.9 all-to-all-start.3
  (6 other events, 7.5 us)
where the time goes:
time: 1270 us
  blocking collectives  1090 us (86%)
  starting transfers between devices  52.4 us (4%)
  matrix products  37.9 us (3%)
  waiting for transfers between devices  31.3 us (2%)
  local copies, waits for them, and re-layouts  30.6 us (2%)
  other arithmetic  24.8 us (2%)
    psum x4, blocking collectives, squares(): return lax.psum(jnp.sum(residual * residual, axis=(0, 1)), 'dev')  514 us
    psum x3, blocking collectives, local(): alpha = norm_now / lax.psum(jnp.sum(direction * image, axis=(0, 1)), 'dev')  382 us
    psum x1, blocking collectives, local(): lax.psum(partial_stress, 'dev')  129 us
    all_gather x1, blocking collectives, local(): lax.all_gather(cand_strain, 'dev', axis=1, tiled=True)  46.6 us
  transfers between devices with their start and end apart: 12, of which 6 were waited for; matrix products, arithmetic and copies ran while one was open for 3% of the time, Pallas kernels for 0%

commit v1 on v0

v1 whole, which is shorter than its diff:
```python
import math

import jax
import jax.numpy as jnp
from jax import lax
from jax.experimental import pallas as pl
from jax.experimental.pallas import tpu as pltpu
from jax.sharding import PartitionSpec as P

BLOCK = 64
IFACE = 16
BLOCKS = 48
POINTS = 128
PLASTIC_CAP = 8
HALF = BLOCKS // 2
ROWS = HALF * 8
LANES = 128

ridge = 0.5
F32 = jnp.float32
BF16 = jnp.bfloat16
HIGHEST = lax.Precision.HIGHEST


def iota(shape, dim):
    return lax.broadcasted_iota(jnp.int32, shape, dim)


def dot(a, b):
    return jnp.dot(a, b, precision=HIGHEST, preferred_element_type=F32)


def dot_nt(a, b):
    return lax.dot_general(
        a, b, (((1,), (1,)), ((), ())), precision=HIGHEST, preferred_element_type=F32
    )


def dot_tn(a, b):
    return lax.dot_general(
        a, b, (((0,), (0,)), ((), ())), precision=HIGHEST, preferred_element_type=F32
    )


def bdot(a, b):
    return jnp.dot(a, b, preferred_element_type=F32)


def bdot_nt(a, b):
    return lax.dot_general(a, b, (((1,), (1,)), ((), ())), preferred_element_type=F32)


def split2(x):
    high = x.astype(BF16)
    return high, (x - high.astype(F32)).astype(BF16)


def split3(x):
    high = x.astype(BF16).astype(F32)
    rest = x - high
    middle = rest.astype(BF16).astype(F32)
    return high, middle, rest - middle


def spread_rows(values):
    n = values.shape[1]
    rows = []
    for part in split3(values):
        for c in range(3):
            rows.append(jnp.broadcast_to(part[c : c + 1], (16, n)))
        rows.append(jnp.zeros((16, n), F32))
    return jnp.concatenate(rows, axis=0)


def pack_kernel(load_ref, phase_ref, out_ref, even):
    for c in range(8):
        if c < 6:
            value = load_ref[c]
        elif c == 6:
            value = 1.0 + 2.0 * phase_ref[0].astype(F32)
        else:
            out_ref[pl.ds(c, HALF, stride=8), :] = jnp.zeros((HALF, LANES), F32)
            continue
        padded = jnp.concatenate([value, jnp.zeros((BLOCK, LANES - BLOCKS), F32)], axis=1)
        turned = jnp.transpose(jnp.concatenate([padded, padded], axis=0))
        even[...] = turned
        first = even[pl.ds(0, HALF, stride=2), :]
        second = even[pl.ds(1, HALF, stride=2), :]
        out_ref[pl.ds(c, HALF, stride=8), :] = jnp.where(
            iota((HALF, LANES), 1) < BLOCK, first, second
        )


def face_kernel(disp_ref, face_ref, out_ref):
    devs = face_ref.shape[1]
    nodes = disp_ref.shape[1]
    faces = face_ref[0]
    spread = spread_rows(disp_ref[...])
    spread = jnp.concatenate([spread, jnp.zeros((64, nodes), F32)], axis=0).astype(BF16)
    place = iota((devs, nodes), 1)
    hot = jnp.concatenate(
        [jnp.where(faces[:, j : j + 1] == place, 1.0, 0.0) for j in range(16)], axis=0
    ).astype(BF16)
    found = bdot_nt(hot, spread)
    lane = iota((devs, 256), 1) % 16
    total = jnp.zeros((devs, 256), F32)
    for j in range(16):
        total = total + jnp.where(lane == j, found[j * devs : (j + 1) * devs], 0.0)
    near = total[:, :LANES]
    out_ref[:, 0, :] = (near + pltpu.roll(near, 64, 1)) + total[:, LANES:]


def weight_kernel(root_ref, chain_ref, bridge_ref, w1h, w1l, wbh, wbl, w2h, w2l, basis_ref):
    root, chain, bridge = root_ref[...], chain_ref[...], bridge_ref[...]

    zero = jnp.zeros((BLOCK, BLOCK), F32)

    def straight(m):
        return jnp.concatenate(
            [jnp.concatenate([m, zero], axis=1), jnp.concatenate([zero, m], axis=1)], axis=0
        )

    def crossed(m):
        return jnp.concatenate(
            [jnp.concatenate([zero, m], axis=1), jnp.concatenate([m, zero], axis=1)], axis=0
        )

    gap = BLOCK - IFACE
    wide = jnp.concatenate([bridge, jnp.zeros((IFACE, gap), F32)], axis=1)
    upper = jnp.concatenate([jnp.zeros((gap, BLOCK), F32), wide], axis=0)
    eye = jnp.where(iota((BLOCK, BLOCK), 0) == iota((BLOCK, BLOCK), 1), 1.0, 0.0)
    root_t = dot_nt(eye, root)
    chain_t = dot_nt(eye, chain)
    lower = dot_nt(eye, upper)
    first = jnp.concatenate([straight(root_t), crossed(chain_t)], axis=1)
    w1h[...], w1l[...] = split2(first)
    wbh[...], wbl[...] = split2(straight(lower))
    second = jnp.concatenate([straight(root), -crossed(chain), -straight(upper)], axis=0)
    w2h[...], w2l[...] = split2(second)

    size = 2 * BLOCK
    diagonal = iota((size, size), 0) == iota((size, size), 1)
    edge = jnp.where(diagonal, 1.0, 0.0) - crossed(chain)
    face = straight(jnp.where(iota((BLOCK, BLOCK), 0) >= gap, eye, 0.0) - upper)
    model = 2.0 * dot_tn(straight(root), straight(root)) + dot_tn(edge, edge) + dot_tn(face, face)
    model = model + jnp.where(diagonal, ridge, 0.0)

    def inner(p, q):
        return jnp.sum(jnp.sum(p * q, axis=1, keepdims=True), axis=0, keepdims=True)

    now = jnp.where(diagonal, size**-0.5, 0.0)
    past, image = None, size**-0.5 * model
    centres, steps = [], []
    for n in range(3):
        if n:
            image = dot(model, now)
        centre = inner(now, image)
        rest = image - centre * now
        if n:
            rest = rest - steps[-1] * past
        step = jnp.maximum(jnp.sqrt(inner(rest, rest)), 0.01 * centres[0] if n else 0.01 * centre)
        centres.append(centre)
        steps.append(step)
        past, now = now, rest / step
    row = iota((8, LANES), 0)
    table = jnp.zeros((8, LANES), F32)
    for n, value in enumerate(centres + steps):
        table = jnp.where(row == n, value, table)
    basis_ref[...] = table


def krylov_kernel(
    own_ref, m1_ref, m2_ref, p1_ref, p2_ref, w1h, w1l, wbh, wbl, w2h, w2l, basis_ref, u_ref, gram_ref
):
    centre = [basis_ref[n : n + 1, :] for n in range(3)]
    step = [basis_ref[n + 3 : n + 4, :] for n in range(3)]
    inverse = [1.0 / v for v in step]
    lane = iota((ROWS, LANES), 1)
    early = lane < BLOCK
    top = (lane % BLOCK) >= BLOCK - IFACE

    def weights_of(x):
        w = x.reshape(HALF, 8, LANES)[:, 6:7, :]
        return jnp.broadcast_to(w, (HALF, 8, LANES)).reshape(ROWS, LANES)

    def stage(x, high, low):
        xh, xl = split2(x)
        return bdot(xh, high) + (bdot(xl, high) + bdot(xh, low))

    def up(x):
        return jnp.concatenate([x[8:], x[:8]], axis=0)

    def down(x):
        return jnp.concatenate([x[ROWS - 8 :], x[: ROWS - 8]], axis=0)

    def halves(x, w):
        both = stage(x, w1h[...], w1l[...])
        lifted = both[:, :LANES]
        mixed = both[:, LANES:]
        edge = x - jnp.where(early, mixed, up(mixed))
        return lifted, w * lifted, edge

    def bridged(x):
        return stage(x, wbh[...], wbl[...])

    def face(x, following):
        return jnp.where(top, x, 0.0) - following

    def apply(x, w, f, f_before):
        _, weighted, edge = halves(x, w)
        shifted = jnp.where(early, edge, down(edge))
        left = jnp.concatenate([weighted, shifted, f_before], axis=1)
        return ridge * x + edge + f + stage(left, w2h[...], w2l[...])

    x0 = [m1_ref[...], own_ref[...], p1_ref[...], p2_ref[...]]
    w = [weights_of(x) for x in x0]
    zero = jnp.zeros((ROWS, LANES), F32)

    b0 = [bridged(x) for x in x0]
    f0 = [face(m2_ref[...], b0[0])] + [face(x0[p], b0[p + 1]) for p in range(3)] + [zero]
    x1 = []
    for p in range(4):
        image = apply(x0[p], w[p], f0[p + 1], f0[p])
        x1.append(inverse[0] * (image - centre[0] * x0[p]))

    b1 = [None] + [bridged(x1[p]) for p in range(1, 4)]
    f1 = [zero] + [face(x1[p], b1[p + 1]) for p in range(3)]
    x2 = []
    for p in range(3):
        image = apply(x1[p], w[p], f1[p + 1], f1[p])
        x2.append(inverse[1] * (image - centre[1] * x1[p] - step[0] * x0[p]))

    b2 = [None] + [bridged(x2[p]) for p in range(1, 3)]
    f2 = [face(x2[p], b2[p + 1]) for p in range(2)] + [zero]
    x3 = [None]
    for p in range(1, 3):
        image = apply(x2[p], w[p], f2[p], f2[p - 1])
        x3.append(inverse[2] * (image - centre[2] * x2[p] - step[1] * x1[p]))

    lifted, weighted, edge = halves(x3[1], w[1])
    f3 = face(x3[1], bridged(x3[2]))

    basis = [x0[1], x1[1], x2[1], x3[1]]
    for n in range(4):
        u_ref[n] = basis[n]

    def long(x):
        return jnp.concatenate([x[8 * k : 8 * k + 8] for k in range(HALF)], axis=1)

    tall = jnp.concatenate([long(x) for x in basis + [lifted, weighted, edge, f3]], axis=0)
    high = tall.astype(BF16).astype(F32)
    both = jnp.concatenate([high, tall - high], axis=0).astype(BF16)
    product = bdot_nt(both, both)
    product = product[:64] + product[64:]
    product = product + pltpu.roll(product, 64, 1)

    def pair(a, b, to):
        return pltpu.roll(product[8 * a : 8 * a + 8], (8 * (to - b)) % LANES, 1)

    at = iota((8, LANES), 1) // 8
    energy = 0.5 * pair(3, 3, 7) + (pair(4, 5, 7) + pair(6, 6, 7) + pair(7, 7, 7))
    moments = jnp.where(at < 4, product[:8], 0.0)
    moments = jnp.where(at == 4, pair(2, 2, 4), moments)
    moments = jnp.where(at == 5, pair(2, 3, 5), moments)
    moments = jnp.where(at == 6, pair(3, 3, 6), moments)
    moments = jnp.where(at == 7, energy, moments)
    for t in range(3):
        gram_ref[:, t * LANES : (t + 1) * LANES] = moments[2 * t : 2 * t + 1] + pltpu.roll(
            moments[2 * t + 1 : 2 * t + 2], 64, 1
        )


def turn_kernel(u_ref, out_ref, wide):
    for k in range(HALF):
        rows = jnp.concatenate([u_ref[n, 8 * k : 8 * k + 8, :] for n in range(4)], axis=0)
        high = rows.astype(BF16).astype(F32)
        stack = jnp.concatenate([high, rows - high, high, jnp.zeros_like(high)], axis=0)
        turned = jnp.transpose(stack)
        wide[pl.ds(2 * k, BLOCK, stride=BLOCKS), :] = turned[:BLOCK]
        wide[pl.ds(2 * k + 1, BLOCK, stride=BLOCKS), :] = turned[BLOCK:]
    out_ref[...] = wide[...].astype(BF16)


def strain_kernel(
    disp_ref, arrived_ref, conn_ref, map_ref, assign_ref, gram_ref, send_ref, strain_ref
):
    devs = arrived_ref.shape[0]
    nodes = disp_ref.shape[1]
    points = conn_ref.shape[1]
    conn = conn_ref[...]
    index = jnp.concatenate([conn[a : a + 1] for a in range(8)], axis=1)
    refs = 8 * points
    own = jnp.where(iota((nodes, refs), 0) == index, 1.0, 0.0).astype(BF16)
    partner = (index - nodes) >> 4
    other = jnp.where(iota((devs, refs), 0) == partner, 1.0, 0.0).astype(BF16)
    ghost = jnp.transpose(arrived_ref[:, 0, :])[:64]
    ghost = jnp.concatenate(split3(ghost), axis=0).astype(BF16)
    table = spread_rows(disp_ref[...]).astype(BF16)
    found = bdot(table, own) + bdot(ghost, other)
    found = (found[:64] + found[64:128]) + found[128:]
    found = jnp.where(iota((64, refs), 0) % 16 == index % 16, found, 0.0)
    sums = [jnp.sum(found[16 * c : 16 * c + 16], axis=0, keepdims=True) for c in range(3)]
    nodal = jnp.concatenate(
        [sums[c][:, a * points : (a + 1) * points] for a in range(8) for c in range(3)], axis=0
    )
    strain = jnp.concatenate(
        [jnp.sum(map_ref[c] * nodal, axis=0, keepdims=True) for c in range(6)], axis=0
    )
    strain_ref[...] = jnp.concatenate([strain, jnp.zeros((2, points), F32)], axis=0)

    assign = assign_ref[...]
    plastic = assign >= 0
    flags = jnp.where(plastic, 1.0, 0.0)
    before = jnp.where(iota((points, points), 0) < iota((points, points), 1), 1.0, 0.0)
    rank = bdot(jnp.broadcast_to(flags, (8, points)).astype(BF16), before.astype(BF16))
    pick = jnp.where(plastic & (rank == iota((8, points), 0).astype(F32)), 1.0, 0.0)
    values = jnp.concatenate(
        [
            strain,
            (assign + 1).astype(F32),
            jnp.zeros((LANES - 7, points), F32),
        ],
        axis=0,
    )
    chosen = dot_nt(pick, values)
    line = chosen[0:1]
    for slot in range(1, PLASTIC_CAP):
        line = line + pltpu.roll(chosen[slot : slot + 1], 8 * slot, 1)
    line = jnp.concatenate([gram_ref[...], line], axis=1)
    send_ref[:, 0, :] = jnp.broadcast_to(line, (devs, 4 * LANES))


def section_kernel(arrived_ref, send_ref, own_ref):
    devs = arrived_ref.shape[0]
    groups = send_ref.shape[0]
    arrived = arrived_ref[:, 0, :]
    total = jnp.sum(arrived[:, : 3 * LANES], axis=0, keepdims=True)
    low = iota((1, LANES), 1) < 64
    rows = []
    for t in range(3):
        tile = total[:, t * LANES : (t + 1) * LANES]
        rows.append(jnp.where(low, tile, 0.0))
        rows.append(jnp.where(low, pltpu.roll(tile, 64, 1), 0.0))
    rows.append(jnp.zeros((2, LANES), F32))
    moments = jnp.concatenate(rows, axis=0)
    own_ref[...] = moments

    cand = arrived[:, 3 * LANES :]
    entry = iota((LANES, 4 * LANES), 1)
    copies = jnp.where(
        iota((LANES, 4 * LANES), 0) == (entry // 64) * 8 + entry % 8, 1.0, 0.0
    )
    tiled = dot(cand, copies)
    spot = iota((devs, LANES), 1)
    column = iota((devs, 64), 1)
    left, right = [], []
    for slot in range(PLASTIC_CAP):
        target = cand[:, 8 * slot + 6 : 8 * slot + 7].astype(jnp.int32) - 1
        right.append(jnp.where((target & (POINTS - 1)) == spot, 1.0, 0.0))
        keep = ((target >> 7) == column // 8) & (column % 8 < 6)
        left.append(jnp.where(keep, tiled[:, 64 * slot : 64 * slot + 64], 0.0))
    dense = dot_tn(jnp.concatenate(left, axis=0), jnp.concatenate(right, axis=0))
    for h in range(groups):
        send_ref[h, 0:8, :] = dense[8 * h : 8 * h + 8]
        send_ref[h, 8:16, :] = moments


def coefficients(m, centre, step):
    m00, m01, m02, m03, m22, m23, m33, energy = m
    m11 = m00 + (step[1] * m02 + (centre[1] - centre[0]) * m01) / step[0]
    m12 = (step[2] * m03 + (centre[2] - centre[0]) * m02 + step[1] * m01) / step[0]
    m13 = (step[1] * (m22 - m11) + (centre[1] - centre[2]) * m12 + step[0] * m02) / step[2]
    products = [
        [m00, m01, m02, m03],
        [m01, m11, m12, m13],
        [m02, m12, m22, m23],
        [m03, m13, m23, m33],
    ]

    def gram(a, b):
        return products[a][b]

    def image(a, b):
        a, b = max(a, b), min(a, b)
        if b == 3:
            return energy
        value = step[b] * products[a][b + 1] + centre[b] * products[a][b]
        return value + step[b - 1] * products[a][b - 1] if b else value

    def inner(p, form):
        total = None
        for a in range(len(p)):
            for b in range(a, len(p)):
                term = p[a] * p[b] * form(a, b)
                if a != b:
                    term = 2.0 * term
                total = term if total is None else total + term
        return total

    def times(p):
        out = [jnp.zeros_like(p[0]) for _ in range(len(p) + 1)]
        for b, v in enumerate(p):
            out[b + 1] = out[b + 1] + step[b] * v
            out[b] = out[b] + centre[b] * v
            if b:
                out[b - 1] = out[b - 1] + step[b - 1] * v
        return out

    one = jnp.ones_like(m00)
    answer = []
    residual = [one]
    direction = [one]
    norm = m00
    for turn in range(4):
        alpha = norm / inner(direction, image)
        answer = answer + [jnp.zeros_like(one)]
        answer = [x + alpha * p for x, p in zip(answer, direction)]
        if turn < 3:
            stepped = times(direction)
            residual = residual + [jnp.zeros_like(one)]
            residual = [r - alpha * v for r, v in zip(residual, stepped)]
            later = inner(residual, gram)
            beta = later / norm
            direction = direction + [jnp.zeros_like(one)]
            direction = [r + beta * p for r, p in zip(residual, direction)]
            norm = later
    return answer


def final_kernel(
    scale, arrived_ref, own_ref, strain_ref, assign_ref, elastic_ref, basis_ref, u_ref, stress_ref, out_ref
):
    groups = arrived_ref.shape[0]
    points = strain_ref.shape[1]
    centre = [basis_ref[n : n + 1, :] for n in range(3)]
    step = [basis_ref[n + 3 : n + 4, :] for n in range(3)]
    field = arrived_ref[0, 0:8, :]
    for h in range(1, groups):
        field = field + arrived_ref[h, 0:8, :]
    diagonal = (iota((64, LANES), 0) // 8) == (iota((64, LANES), 1) // 8)

    def tall(x):
        return jnp.concatenate([x] * 8, axis=0)

    def opened(moments):
        return jnp.where(diagonal, tall(moments), 0.0)[:, :64]

    strain = strain_ref[...]
    padded = jnp.concatenate([strain, jnp.zeros((8, LANES - points), F32)], axis=1)
    assign = jnp.concatenate(
        [assign_ref[...], jnp.full((1, LANES - points), -1, jnp.int32)], axis=1
    )
    forces = dot(opened(own_ref[...]), tall(field))
    every = jnp.concatenate([opened(arrived_ref[h, 8:16, :]) for h in range(groups)], axis=0)
    products = dot(every, tall(padded))
    group_of = assign >> 7
    local = jnp.zeros((64, LANES), F32)
    for h in range(groups):
        local = local + jnp.where(group_of == h, products[64 * h : 64 * h + 64], 0.0)

    m = []
    for n in range(8):
        first = jnp.sum(forces[8 * n : 8 * n + 8] * field, axis=0, keepdims=True)
        second = jnp.sum(local[8 * n : 8 * n + 8] * padded, axis=0, keepdims=True)
        m.append(jnp.concatenate([first, second], axis=0))
    answer = coefficients(m, centre, step)

    extra = jnp.zeros((8, LANES), F32)
    for n in range(4):
        extra = extra + answer[n][1:2] * local[8 * n : 8 * n + 8]
    elastic_stress = dot(elastic_ref[...], strain[:6])
    plastic = assign_ref[...] >= 0
    stress_ref[...] = elastic_stress + jnp.where(plastic, extra[:6, :points], 0.0)

    right = jnp.concatenate([(scale * answer[n][0:1]) * field for n in range(4)], axis=0)
    high = right.astype(BF16).astype(F32)
    right = jnp.concatenate([high, high, right - high, jnp.zeros_like(high)], axis=0).astype(BF16)
    for part in range(6):
        rows = slice(512 * part, 512 * part + 512)
        out_ref[rows, :] = bdot(u_ref[rows, :], right)


def call(kernel, outs, *args, scratch=()):
    vmem = pl.BlockSpec(memory_space=pltpu.VMEM)
    many = isinstance(outs, list)
    return pl.pallas_call(
        kernel,
        out_shape=outs,
        in_specs=[vmem] * len(args),
        out_specs=[vmem] * len(outs) if many else vmem,
        scratch_shapes=list(scratch),
        compiler_params=pltpu.CompilerParams(vmem_limit_bytes=32 * 1024 * 1024),
    )(*args)


def arr(*shape, dtype=F32):
    return jax.ShapeDtypeStruct(shape, dtype)


def shifted(x, by):
    devices = lax.axis_size("dev")
    return lax.ppermute(x, "dev", [(i, (i + by) % devices) for i in range(devices)])


def exchange(x, axis):
    return lax.all_to_all(x, axis, split_axis=0, concat_axis=0, tiled=True)


def local(
    displacement,
    connectivity,
    face_nodes,
    strain_map,
    assignment,
    phases,
    load_map,
    stiff_root,
    chain_map,
    bridge_map,
    elastic,
):
    groups = lax.axis_size("group")
    devs = lax.axis_size("dev")
    points = connectivity.shape[1]
    assign = assignment.reshape(1, -1)

    packed = call(
        pack_kernel,
        arr(ROWS, LANES),
        load_map,
        phases,
        scratch=[pltpu.VMEM((LANES, LANES), F32)],
    )
    near = [shifted(packed, 1), shifted(packed, 2), shifted(packed, -1), shifted(packed, -2)]
    faces = call(face_kernel, arr(devs, 1, LANES), displacement, face_nodes)
    arrived = exchange(faces, "dev")

    *weights, terms = call(
        weight_kernel,
        [
            arr(LANES, 2 * LANES, dtype=BF16),
            arr(LANES, 2 * LANES, dtype=BF16),
            arr(LANES, LANES, dtype=BF16),
            arr(LANES, LANES, dtype=BF16),
            arr(3 * LANES, LANES, dtype=BF16),
            arr(3 * LANES, LANES, dtype=BF16),
            arr(8, LANES),
        ],
        stiff_root,
        chain_map,
        bridge_map,
    )
    vectors, gram = call(
        krylov_kernel,
        [arr(4, ROWS, LANES), arr(1, 3 * LANES)],
        packed,
        *near,
        *weights,
        terms,
    )
    send, strain = call(
        strain_kernel,
        [arr(devs, 1, 4 * LANES), arr(8, points)],
        displacement,
        arrived,
        connectivity,
        strain_map,
        assign,
        gram,
    )
    section = exchange(send, "dev")
    turned = call(
        turn_kernel,
        arr(BLOCK * BLOCKS, LANES, dtype=BF16),
        vectors,
        scratch=[pltpu.VMEM((BLOCK * BLOCKS, LANES), F32)],
    )
    across, own = call(section_kernel, [arr(groups, 16, LANES), arr(8, LANES)], section)
    gathered = exchange(across, "group")
    scale = math.sqrt(BLOCK * devs * BLOCKS)
    stress, fluctuation = call(
        lambda *refs: final_kernel(scale, *refs),
        [arr(6, points), arr(BLOCK * BLOCKS, POINTS)],
        gathered,
        own,
        strain,
        assign,
        elastic,
        terms,
        turned,
    )
    return stress, fluctuation.reshape(1, BLOCK, BLOCKS, POINTS)


def solution(mesh):
    in_specs = (
        P(None, ("group", "dev")),
        P(None, ("group", "dev")),
        P(("group", "dev"), None, None),
        P(None, None, ("group", "dev")),
        P(("group", "dev")),
        P("group", None, "dev"),
        P(None, None, "dev"),
        P(),
        P(),
        P(),
        P(),
    )
    out_specs = (P(None, ("group", "dev")), P("group", None, "dev", None))
    return jax.shard_map(local, mesh=mesh, in_specs=in_specs, out_specs=out_specs, check_vma=False)
```

time: 1270 us -> 84.5 us (0.07)
  blocking collectives: 1090 us -> 20.3 us
  matrix products: 37.9 us -> 0 us
  local copies, waits for them, and re-layouts: 30.6 us -> 5.58 us
  other arithmetic: 24.8 us -> 0 us
  waiting for transfers between devices: 31.3 us -> 6.89 us
  starting transfers between devices: 52.4 us -> 35.7 us
  Pallas kernels: 0 us -> 14.6 us
    psum x8 -> x0, blocking collectives: 1020 us -> none  [the longest x4 514 us: squares(): return lax.psum(jnp.sum(residual * residual, axis=(0, 1)), 'dev')]
    all_gather x1 -> x0, blocking collectives: 46.6 us -> none  [local(): lax.all_gather(cand_strain, 'dev', axis=1, tiled=True)]
    dot_general x36 -> x0, matrix products: 37.9 us -> none  [the longest x4 7.99 us: apply_block(): jnp.dot(stiff_root, field.reshape(BLOCK, -1), precision=highest)]
    ppermute x8 -> x4, waiting for transfers between devices: 21.7 us -> 0.01 us  [shifted(): lax.ppermute(x, 'dev', [(i, (i + by) % devices) for i in range(devices)])]
    all_to_all x0 -> x1, blocking collectives: none -> 20.3 us  [exchange(): return lax.all_to_all(x, axis, split_axis=0, concat_axis=0, tiled=True)]
    all_to_all x4 -> x2, starting transfers between devices: 32.1 us -> 14.4 us  [exchange(): return lax.all_to_all(x, axis, split_axis=0, concat_axis=0, tiled=True)]
    unnamed x1 -> x0, blocking collectives: 17.2 us -> none
    pallas_call x0 -> x8, Pallas kernels: none -> 14.6 us  [call(): pl.pallas_call(kernel, out_shape=outs, in_specs=[vmem] * len(args), out_s...]
  transfers between devices with their start and end apart: 12 -> 6, of which waited for: 6 -> 2; matrix products, arithmetic and copies ran while one was open for 3% -> 1% of each run, Pallas kernels for 0% -> 10%
where the time goes in v1:
time: 84.5 us; the launch traced here: 83.8 us
  starting transfers between devices  35.7 us (42%)
  blocking collectives  20.3 us (24%)
  Pallas kernels  14.6 us (17%)
  waiting for transfers between devices  6.89 us (8%)
  local copies, waits for them, and re-layouts  5.58 us (7%)
    ppermute x4, starting transfers between devices, shifted(): lax.ppermute(x, 'dev', [(i, (i + by) % devices) for i in range(devices)])  21.3 us
    all_to_all x1, blocking collectives, exchange(): return lax.all_to_all(x, axis, split_axis=0, concat_axis=0, tiled=True)  20.3 us
    pallas_call x8, Pallas kernels, call(): pl.pallas_call(kernel, out_shape=outs, in_specs=[vmem] * len(args), out_s...  14.6 us
    all_to_all x2, starting transfers between devices, exchange(): return lax.all_to_all(x, axis, split_axis=0, concat_axis=0, tiled=True)  14.4 us
    all_to_all x2, waiting for transfers between devices, exchange(): return lax.all_to_all(x, axis, split_axis=0, concat_axis=0, tiled=True)  6.88 us
    unnamed x21, local copies, waits for them, and re-layouts  5.58 us
  transfers between devices with their start and end apart: 6, of which 2 were waited for; matrix products, arithmetic and copies ran while one was open for 1% of the time, Pallas kernels for 10%

profile of v1, /device:TPU:1, one launch (start us, length us, event | category | flops | bytes accessed | tf_op | source)
XLA Modules:
  0.0 83.8 jit_solution(2834523547198973712)
XLA Ops:
  0.6 0.0 copy-start.4
  0.7 0.9 %copy.15.phase_ref = s32[1,64,48]{2,1,0:T(8,128)S(1)} copy(s32[1,64,48]{1,2,0:T(8,128)} %param.16) | data formatting | bytes 24576 | tf_op args[5]
  1.5 1.0 %copy.14.load_ref = f32[6,64,48]{2,1,0:T(8,128)S(1)} copy(f32[6,64,48]{1,2,0:T(8,128)} %param.17) | data formatting | bytes 147456 | tf_op args[6]
  2.6 0.2 shard_map.123.own_ref
  2.8 0.0 copy-start.6
  2.8 13.8 %collective-permute-start.3 = (f32[192,128]{1,0:T(8,128)S(1)}, f32[192,128]{1,0:T(8,128)S(1)}, u32[]{:S(2)}, u32[]{:S(2)}) collective-permute-start(f32[192,128]{1,0:T(8,128)S(1)} %shard_map.123.own_ref), channel_id=1, source_target_pairs={{0,62},{1,63},{2,0},{3,1},{4,2},{5,3},{6,4},{7,5},{8,6},{9,7},{10,... | collective-permute-start | bytes 294920 | tf_op jit(solution)/shard_map/ppermute | solution.py:502
  16.6 2.9 %collective-permute-start.2 = (f32[192,128]{1,0:T(8,128)S(1)}, f32[192,128]{1,0:T(8,128)S(1)}, u32[]{:S(2)}, u32[]{:S(2)}) collective-permute-start(f32[192,128]{1,0:T(8,128)S(1)} %shard_map.123.own_ref), channel_id=1, source_target_pairs={{0,63},{1,0},{2,1},{3,2},{4,3},{5,4},{6,5},{7,6},{8,7},{9,8},{10,9... | collective-permute-start | bytes 294920 | tf_op jit(solution)/shard_map/ppermute | solution.py:502
  19.5 1.9 %collective-permute-start.1 = (f32[192,128]{1,0:T(8,128)S(1)}, f32[192,128]{1,0:T(8,128)S(1)}, u32[]{:S(2)}, u32[]{:S(2)}) collective-permute-start(f32[192,128]{1,0:T(8,128)S(1)} %shard_map.123.own_ref), channel_id=1, source_target_pairs={{0,2},{1,3},{2,4},{3,5},{4,6},{5,7},{6,8},{7,9},{8,10},{9,11},{10,... | collective-permute-start | bytes 294920 | tf_op jit(solution)/shard_map/ppermute | solution.py:502
  21.4 2.7 %collective-permute-start = (f32[192,128]{1,0:T(8,128)S(1)}, f32[192,128]{1,0:T(8,128)S(1)}, u32[]{:S(2)}, u32[]{:S(2)}) collective-permute-start(f32[192,128]{1,0:T(8,128)S(1)} %shard_map.123.own_ref), channel_id=1, source_target_pairs={{0,1},{1,2},{2,3},{3,4},{4,5},{5,6},{6,7},{7,8},{8,9},{9,10},{10,1... | collective-permute-start | bytes 294920 | tf_op jit(solution)/shard_map/ppermute | solution.py:502
  24.1 0.8 copy.13.face_ref
  24.9 0.7 copy-done.3
  25.6 1.1 %shard_map.122 = f32[64,1,128]{2,1,0:T(1,128)} custom-call(f32[3,256]{1,0:T(4,128)S(1)} %copy-done.3, s32[1,64,16]{2,1,0:T(8,128)S(1)} %copy.13.face_ref), custom_call_target="tpu_custom_call" | custom-call | tf_op jit(solution)/shard_map/pallas_call | solution.py:486
  26.7 7.6 %all-to-all-start = ((f32[64,1,128]{2,1,0:T(1,128)}), f32[64,1,128]{2,1,0:T(1,128)S(1)}, u32[]{:S(2)}, u32[]{:S(2)}) async-start(f32[64,1,128]{2,1,0:T(1,128)} %shard_map.122), calls=%async_computation | async-start | bytes 65536 | tf_op jit(solution)/shard_map/all_to_all | solution.py:506
  34.3 0.0 copy-start.1
  34.3 0.7 copy-done.1
  35.0 0.8 copy-done.2
  35.8 0.7 copy-done.5
  36.5 1.6 %shard_map.124 = (bf16[128,256]{1,0:T(8,128)(2,1)S(1)}, bf16[128,256]{1,0:T(8,128)(2,1)S(1)}, bf16[128,128]{1,0:T(8,128)(2,1)S(1)}, bf16[128,128]{1,0:T(8,128)(2...) custom-call(f32[64,64]{1,0:T(8,128)S(1)} %copy-done.1, ...), custom_call_target="tpu_custom_call" | custom-call | tf_op jit(solution)/shard_map/pallas_call | solution.py:486
  38.1 0.0 collective-permute-done.3.p2_ref
  38.1 0.0 collective-permute-done.2.p1_ref
  38.1 0.0 collective-permute-done.1.m2_ref
  38.2 0.0 collective-permute-done.m1_ref
  38.2 5.0 %shard_map.125 = (f32[4,192,128]{2,1,0:T(8,128)S(1)}, f32[1,384]{1,0:T(1,128)S(1)}) custom-call(f32[192,128]{1,0:T(8,128)S(1)} %shard_map.123.own_ref, f32[192,128]{1,0:T(8,128)S(1)} %collective-permute-done.m1_ref, f32[192,128]{1,0:T(8,128)S(1)} %collective-permute-done.1.m2_ref, f32[192,128]{1,0:T(8,128)S(1)} %collective-permute-done.2.p1_ref, ...), custom_call_target="tpu_custom_call" | custom-call | tf_op jit(solution)/shard_map/pallas_call | solution.py:486
  43.2 0.3 all-to-all-done.arrived_ref
  43.5 0.0 copy-done
  43.5 0.7 shard_map.126
  44.2 20.3 %all_to_all.15.arrived_ref = f32[64,1,512]{2,1,0:T(1,128)S(1)} all-to-all(f32[64,1,512]{2,1,0:T(1,128)S(1)} %get-tuple-element.25), channel_id=1, replica_groups=mesh['group'=8,'dev'=64] {'dev'}, dimensions={0} | all-to-all | bytes 262144 | tf_op jit(solution)/shard_map/all_to_all | solution.py:506
  64.4 3.1 %shard_map.127 = (f32[8,16,128]{2,1,0:T(8,128)}, f32[8,128]{1,0:T(8,128)S(1)}) custom-call(f32[64,1,512]{2,1,0:T(1,128)S(1)} %all_to_all.15.arrived_ref), custom_call_target="tpu_custom_call" | custom-call | tf_op jit(solution)/shard_map/pallas_call | solution.py:486
  67.5 6.8 %all-to-all-start.2 = ((f32[8,16,128]{2,1,0:T(8,128)}), f32[8,16,128]{2,1,0:T(8,128)S(1)}, u32[]{:S(2)}, u32[]{:S(2)}) async-start(f32[8,16,128]{2,1,0:T(8,128)} %get-tuple-element.26), calls=%async_computation.2 | async-start | bytes 131072 | tf_op jit(solution)/shard_map/all_to_all | solution.py:506
  74.4 0.6 shard_map.128.refs_6_
  75.0 6.6 %all-to-all-done.2.refs_0_ = f32[8,16,128]{2,1,0:T(8,128)S(1)} async-done(((f32[8,16,128]{2,1,0:T(8,128)}), f32[8,16,128]{2,1,0:T(8,128)S(1)}, u32[]{:S(2)}, u32[]{:S(2)}) %all-to-all-start.2) | async-done | bytes 65568 | tf_op jit(solution)/shard_map/all_to_all | solution.py:506
  81.6 2.2 %shard_map.129 = (f32[6,64]{1,0:T(8,128)}, f32[3072,128]{1,0:T(8,128)}) custom-call(f32[8,16,128]{2,1,0:T(8,128)S(1)} %all-to-all-done.2.refs_0_, f32[8,128]{1,0:T(8,128)S(1)} %get-tuple-element.27.refs_1_, f32[8,64]{1,0:T(8,128)S(1)} %get-tuple-element.28.refs_2_, s32[1,64]{1,0:T(1,128)S(1)} %bitcast.3, f32[6,6]{1,0:T(8,128)S(1)} %copy-done.6, ...), custom_call_target="tpu_custom_call" | custom-call | tf_op jit(solution)/shard_map/pallas_call | solution.py:486
  (10 shorter events, 0.0 us)
Async XLA Ops:
  0.6 42.9 %copy-start.4 = (f32[3,256]{1,0:T(4,128)S(1)}, f32[3,256]{1,0:T(4,128)}, u32[]{:S(2)}) copy-start(f32[3,256]{1,0:T(4,128)} %disp_ref.3) | copy-start | bytes 9220
  0.6 42.8 %copy-start.8 = (s32[64]{0:T(128)S(1)}, s32[64]{0:T(128)}, u32[]{:S(2)}) copy-start(s32[64]{0:T(128)} %param.15) | copy-start | bytes 772
  0.7 42.8 %copy-start = (f32[6,24,64]{2,1,0:T(8,128)S(1)}, f32[6,24,64]{2,1,0:T(8,128)}, u32[]{:S(2)}) copy-start(f32[6,24,64]{2,1,0:T(8,128)} %map_ref.1) | copy-start | bytes 110596
  0.7 42.8 %copy-start.7 = (s32[8,64]{1,0:T(8,128)S(1)}, s32[8,64]{1,0:T(8,128)}, u32[]{:S(2)}) copy-start(s32[8,64]{1,0:T(8,128)} %conn_ref.1) | copy-start | bytes 6148
  2.8 78.8 %copy-start.6 = (f32[6,6]{1,0:T(8,128)S(1)}, f32[6,6]{1,0:T(8,128)}, u32[]{:S(2)}) copy-start(f32[6,6]{1,0:T(8,128)} %refs_4_.1) | copy-start | bytes 436
  2.8 35.3 %collective-permute-start.3 = (f32[192,128]{1,0:T(8,128)S(1)}, f32[192,128]{1,0:T(8,128)S(1)}, u32[]{:S(2)}, u32[]{:S(2)}) collective-permute-start(f32[192,128]{1,0:T(8,128)S(1)} %shard_map.123.own_ref), channel_id=1, source_target_pairs={{0,62},{1,63},{2,0},{3,1},{4,2},{5,3},{6,4},{7,5},{8,6},{9,7},{10,... | collective-permute-start | bytes 294920 | tf_op jit(solution)/shard_map/ppermute | solution.py:502
  16.6 21.5 %collective-permute-start.2 = (f32[192,128]{1,0:T(8,128)S(1)}, f32[192,128]{1,0:T(8,128)S(1)}, u32[]{:S(2)}, u32[]{:S(2)}) collective-permute-start(f32[192,128]{1,0:T(8,128)S(1)} %shard_map.123.own_ref), channel_id=1, source_target_pairs={{0,63},{1,0},{2,1},{3,2},{4,3},{5,4},{6,5},{7,6},{8,7},{9,8},{10,9... | collective-permute-start | bytes 294920 | tf_op jit(solution)/shard_map/ppermute | solution.py:502
  19.5 18.7 %collective-permute-start.1 = (f32[192,128]{1,0:T(8,128)S(1)}, f32[192,128]{1,0:T(8,128)S(1)}, u32[]{:S(2)}, u32[]{:S(2)}) collective-permute-start(f32[192,128]{1,0:T(8,128)S(1)} %shard_map.123.own_ref), channel_id=1, source_target_pairs={{0,2},{1,3},{2,4},{3,5},{4,6},{5,7},{6,8},{7,9},{8,10},{9,11},{10,... | collective-permute-start | bytes 294920 | tf_op jit(solution)/shard_map/ppermute | solution.py:502
  21.4 16.7 %collective-permute-start = (f32[192,128]{1,0:T(8,128)S(1)}, f32[192,128]{1,0:T(8,128)S(1)}, u32[]{:S(2)}, u32[]{:S(2)}) collective-permute-start(f32[192,128]{1,0:T(8,128)S(1)} %shard_map.123.own_ref), channel_id=1, source_target_pairs={{0,1},{1,2},{2,3},{3,4},{4,5},{5,6},{6,7},{7,8},{8,9},{9,10},{10,1... | collective-permute-start | bytes 294920 | tf_op jit(solution)/shard_map/ppermute | solution.py:502
  24.9 0.7 copy-start.3
  26.7 16.8 %all-to-all-start = ((f32[64,1,128]{2,1,0:T(1,128)}), f32[64,1,128]{2,1,0:T(1,128)S(1)}, u32[]{:S(2)}, u32[]{:S(2)}) async-start(f32[64,1,128]{2,1,0:T(1,128)} %shard_map.122), calls=%async_computation | async-start | bytes 65536 | tf_op jit(solution)/shard_map/all_to_all | solution.py:506
  34.3 0.8 copy-start.1
  35.0 0.8 copy-start.2
  35.8 0.7 copy-start.5
  67.5 14.1 %all-to-all-start.2 = ((f32[8,16,128]{2,1,0:T(8,128)}), f32[8,16,128]{2,1,0:T(8,128)S(1)}, u32[]{:S(2)}, u32[]{:S(2)}) async-start(f32[8,16,128]{2,1,0:T(8,128)} %get-tuple-element.26), calls=%async_computation.2 | async-start | bytes 131072 | tf_op jit(solution)/shard_map/all_to_all | solution.py:506

commit v2 on v1

v2 whole, which is shorter than its diff:
```python
import math

import jax
import jax.numpy as jnp
from jax import lax
from jax.experimental import pallas as pl
from jax.experimental.pallas import tpu as pltpu
from jax.sharding import PartitionSpec as P

BLOCK = 64
IFACE = 16
BLOCKS = 48
POINTS = 128
PLASTIC_CAP = 8
NODES = 256
HALF = BLOCKS // 2
ROWS = HALF * 8
LANES = 128

ridge = 0.5
F32 = jnp.float32
BF16 = jnp.bfloat16
HIGHEST = lax.Precision.HIGHEST


def iota(shape, dim):
    return lax.broadcasted_iota(jnp.int32, shape, dim)


def dot(a, b):
    return jnp.dot(a, b, precision=HIGHEST, preferred_element_type=F32)


def dot_nt(a, b):
    return lax.dot_general(
        a, b, (((1,), (1,)), ((), ())), precision=HIGHEST, preferred_element_type=F32
    )


def dot_tn(a, b):
    return lax.dot_general(
        a, b, (((0,), (0,)), ((), ())), precision=HIGHEST, preferred_element_type=F32
    )


def bdot(a, b):
    return jnp.dot(a, b, preferred_element_type=F32)


def bdot_nt(a, b):
    return lax.dot_general(a, b, (((1,), (1,)), ((), ())), preferred_element_type=F32)


def split2(x):
    high = x.astype(BF16)
    return high, (x - high.astype(F32)).astype(BF16)


def split3(x):
    high = x.astype(BF16).astype(F32)
    rest = x - high
    middle = rest.astype(BF16).astype(F32)
    return high, middle, rest - middle


def spread_rows(values):
    n = values.shape[1]
    rows = []
    for part in split3(values):
        for c in range(3):
            rows.append(jnp.broadcast_to(part[c : c + 1], (16, n)))
        rows.append(jnp.zeros((16, n), F32))
    return jnp.concatenate(rows, axis=0)


def stacked(ref, m):
    high, low = split2(m)
    rows = m.shape[0]
    ref[:rows] = high
    ref[rows : 2 * rows] = high
    ref[2 * rows :] = low


def rough(a, b):
    return bdot(a.astype(BF16), b.astype(BF16))


def pack(load, phase, out_ref):
    for c in range(6):
        out_ref[pl.ds(c, HALF, stride=8), :] = jnp.concatenate(
            [load[pl.ds(c, 1), pl.ds(par, HALF, stride=2), :][0] for par in range(2)], axis=1
        )
    labels = [phase[pl.ds(0, 1), pl.ds(par, HALF, stride=2), :][0] for par in range(2)]
    weights = 1.0 + 2.0 * jnp.concatenate(labels, axis=1).astype(F32)
    out_ref[pl.ds(6, HALF, stride=8), :] = weights
    out_ref[pl.ds(7, HALF, stride=8), :] = jnp.zeros((HALF, LANES), F32)


def faces(disp, listed, out_ref):
    devs = listed.shape[2]
    nodes = disp.shape[1]
    names = jnp.concatenate([listed[0].astype(F32), jnp.zeros((16, LANES - devs), F32)], axis=1)
    names = jnp.concatenate([names, jnp.zeros((LANES - 16, LANES), F32)], axis=0)
    names = jnp.transpose(names)[:devs]
    spread = spread_rows(disp[...])
    spread = jnp.concatenate([spread, jnp.zeros((64, nodes), F32)], axis=0).astype(BF16)
    place = iota((devs, nodes), 1).astype(F32)
    hot = jnp.concatenate(
        [jnp.where(names[:, j : j + 1] == place, 1.0, 0.0) for j in range(16)], axis=0
    ).astype(BF16)
    found = bdot_nt(hot, spread)
    lane = iota((devs, 256), 1) % 16
    total = jnp.zeros((devs, 256), F32)
    for j in range(16):
        total = total + jnp.where(lane == j, found[j * devs : (j + 1) * devs], 0.0)
    near = total[:, :LANES]
    out_ref[:, 0, :] = (near + pltpu.roll(near, 64, 1)) + total[:, LANES:]


def fetch(sources, targets, sems):
    copies = [
        pltpu.make_async_copy(a, b, sems.at[n]) for n, (a, b) in enumerate(zip(sources, targets))
    ]
    for copy in copies:
        copy.start()
    for copy in copies:
        copy.wait()


def own_nodes(disp, conn):
    nodes, points = disp.shape[1], conn.shape[1]
    index = side_by_side(conn[...])
    hot = jnp.where(iota((nodes, 8 * points), 0) == index, 1.0, 0.0).astype(BF16)
    parts = jnp.concatenate(split3(disp[...]) + (jnp.zeros((7, nodes), F32),), axis=0)
    found = bdot(parts.astype(BF16), hot)
    return by_node((found[0:3] + found[3:6]) + found[6:9], points)


def side_by_side(rows):
    return jnp.concatenate([rows[a : a + 1] for a in range(rows.shape[0])], axis=1)


def by_node(sums, points):
    return jnp.concatenate(
        [sums[:, a * points : (a + 1) * points] for a in range(8)],
        axis=0,
    )


def first_kernel(*refs):
    face_ref, pack_ref, carry_ref, disp, listed, load, phase, conn, maps, assign, sems = refs[7:]
    fetch(refs[:7], [disp, listed, load, phase, conn, maps, assign], sems)
    faces(disp, listed, face_ref)
    pack(load, phase, pack_ref)
    points = conn.shape[1]
    blank = jnp.zeros((7, points), F32)
    for c in range(6):
        carry_ref[24 * c : 24 * c + 24, :points] = maps[c]
    carry_ref[144:152, :points] = conn[...].astype(F32)
    carry_ref[152:160, :points] = jnp.concatenate([assign[...].astype(F32), blank], axis=0)
    carry_ref[160:184, :points] = own_nodes(disp, conn)
    carry_ref[:, points:] = jnp.zeros((184, LANES - points), F32)


def tables(root_ref, chain_ref, bridge_ref, w1, wb, w2, basis_ref):
    root, chain, bridge = root_ref[...], chain_ref[...], bridge_ref[...]
    zero = jnp.zeros((BLOCK, BLOCK), F32)

    def straight(m):
        return jnp.concatenate(
            [jnp.concatenate([m, zero], axis=1), jnp.concatenate([zero, m], axis=1)], axis=0
        )

    def crossed(m):
        return jnp.concatenate(
            [jnp.concatenate([zero, m], axis=1), jnp.concatenate([m, zero], axis=1)], axis=0
        )

    gap = BLOCK - IFACE
    wide = jnp.concatenate([bridge, jnp.zeros((IFACE, gap), F32)], axis=1)
    upper = jnp.concatenate([jnp.zeros((gap, BLOCK), F32), wide], axis=0)
    roots, chains, bridges = straight(root), crossed(chain), straight(upper)
    stacked(w1, jnp.concatenate([jnp.transpose(roots), jnp.transpose(chains)], axis=1))
    stacked(wb, jnp.transpose(bridges))
    stacked(w2, jnp.concatenate([roots, -chains, -bridges], axis=0))

    size = 2 * BLOCK
    diagonal = iota((size, size), 0) == iota((size, size), 1)
    edge = jnp.where(diagonal, 1.0, 0.0) - chains
    face = jnp.where(diagonal & (iota((size, size), 0) % BLOCK >= gap), 1.0, 0.0) - bridges
    tall = jnp.concatenate([2.0**0.5 * roots, edge, face], axis=0)
    model = rough(jnp.transpose(tall), tall)
    model = model + jnp.where(diagonal, ridge, 0.0)

    def inner(p, q):
        return jnp.sum(jnp.sum(p * q, axis=1, keepdims=True), axis=0, keepdims=True)

    now = jnp.where(diagonal, size**-0.5, 0.0)
    past, image = None, size**-0.5 * model
    centres, steps = [], []
    for n in range(3):
        if n:
            image = rough(model, now)
        centre = inner(now, image)
        rest = image - centre * now
        if n:
            rest = rest - steps[-1] * past
        step = jnp.maximum(jnp.sqrt(inner(rest, rest)), 0.01 * centres[0] if n else 0.01 * centre)
        centres.append(centre)
        steps.append(step)
        past, now = now, rest / step
    row = iota((8, LANES), 0)
    table = jnp.zeros((8, LANES), F32)
    for n, value in enumerate(centres + steps):
        table = jnp.where(row == n, value, table)
    basis_ref[...] = table


def krylov_kernel(
    own_ref, m1_ref, m2_ref, p1_ref, p2_ref, w1, wb, w2, basis_ref, u_ref, gram_ref
):
    centre = [basis_ref[n : n + 1, :] for n in range(3)]
    step = [basis_ref[n + 3 : n + 4, :] for n in range(3)]
    inverse = [1.0 / v for v in step]

    def lanes(x):
        return iota(x.shape, 1)

    def weights_of(x):
        w = x.reshape(HALF, 8, LANES)[:, 6:7, :]
        return jnp.broadcast_to(w, (HALF, 8, LANES)).reshape(ROWS, LANES)

    def stage(x, w):
        high, low = split2(x)
        return bdot(jnp.concatenate([high, low, high], axis=1), w[...])

    def blocks(x):
        return [x[n : n + ROWS] for n in range(0, x.shape[0], ROWS)]

    def up(x):
        parts = [p for v in blocks(x) for p in (v[8:], v[:8])]
        return jnp.concatenate(parts, axis=0)

    def down(x):
        parts = [p for v in blocks(x) for p in (v[ROWS - 8 :], v[: ROWS - 8])]
        return jnp.concatenate(parts, axis=0)

    def halves(x, w):
        both = stage(x, w1)
        lifted = both[:, :LANES]
        mixed = both[:, LANES:]
        edge = x - jnp.where(lanes(x) < BLOCK, mixed, up(mixed))
        return lifted, w * lifted, edge

    def face(x, following):
        return jnp.where(lanes(x) % BLOCK >= BLOCK - IFACE, x, 0.0) - following

    def apply(x, w, f, f_before):
        _, weighted, edge = halves(x, w)
        shifted = jnp.where(lanes(x) < BLOCK, edge, down(edge))
        left = jnp.concatenate([weighted, shifted, f_before], axis=1)
        return ridge * x + edge + f + stage(left, w2)

    zero = jnp.zeros((ROWS, LANES), F32)
    near = [m1_ref[...], own_ref[...], p1_ref[...], p2_ref[...]]
    w = jnp.concatenate([weights_of(x) for x in near], axis=0)

    x0 = jnp.concatenate(near, axis=0)
    known = jnp.concatenate([m2_ref[...], x0[: 3 * ROWS]], axis=0)
    f = jnp.concatenate([face(known, stage(x0, wb)), zero], axis=0)
    image = apply(x0, w, f[ROWS:], f[: 4 * ROWS])
    x1 = inverse[0] * (image - centre[0] * x0)

    f = jnp.concatenate([zero, face(x1[: 3 * ROWS], stage(x1[ROWS:], wb))], axis=0)
    now, past = x1[: 3 * ROWS], x0[: 3 * ROWS]
    image = apply(now, w[: 3 * ROWS], f[ROWS:], f[: 3 * ROWS])
    x2 = inverse[1] * (image - centre[1] * now - step[0] * past)

    f = jnp.concatenate([face(x2[: 2 * ROWS], stage(x2[ROWS:], wb)), zero], axis=0)
    now, past = x2[ROWS:], x1[ROWS : 3 * ROWS]
    image = apply(now, w[ROWS : 3 * ROWS], f[ROWS:], f[: 2 * ROWS])
    x3 = inverse[2] * (image - centre[2] * now - step[1] * past)

    own = x3[:ROWS]
    lifted, weighted, edge = halves(own, w[ROWS : 2 * ROWS])
    f3 = face(own, stage(x3[ROWS:], wb))

    basis = [near[1], x1[ROWS : 2 * ROWS], x2[ROWS : 2 * ROWS], own]
    for n in range(4):
        u_ref[n] = basis[n]

    def long(x):
        return jnp.concatenate([x[8 * k : 8 * k + 8] for k in range(HALF)], axis=1)

    tall = jnp.concatenate([long(x) for x in basis + [lifted, weighted, edge, f3]], axis=0)
    high = tall.astype(BF16).astype(F32)
    both = jnp.concatenate([high, tall - high], axis=0).astype(BF16)
    product = bdot_nt(both, both)
    product = product[:64] + product[64:]
    product = product + pltpu.roll(product, 64, 1)

    def pair(a, b, to):
        return pltpu.roll(product[8 * a : 8 * a + 8], (8 * (to - b)) % LANES, 1)

    at = iota((8, LANES), 1) // 8
    energy = 0.5 * pair(3, 3, 7) + (pair(4, 5, 7) + pair(6, 6, 7) + pair(7, 7, 7))
    moments = jnp.where(at < 4, product[:8], 0.0)
    moments = jnp.where(at == 4, pair(2, 2, 4), moments)
    moments = jnp.where(at == 5, pair(2, 3, 5), moments)
    moments = jnp.where(at == 6, pair(3, 3, 6), moments)
    moments = jnp.where(at == 7, energy, moments)
    for t in range(3):
        gram_ref[:, t * LANES : (t + 1) * LANES] = moments[2 * t : 2 * t + 1] + pltpu.roll(
            moments[2 * t + 1 : 2 * t + 2], 64, 1
        )


def turn_kernel(u_ref, out_ref, wide):
    for k in range(HALF):
        rows = jnp.concatenate([u_ref[n, 8 * k : 8 * k + 8, :] for n in range(4)], axis=0)
        high = rows.astype(BF16).astype(F32)
        stack = jnp.concatenate([high, rows - high, high, jnp.zeros_like(high)], axis=0)
        turned = jnp.transpose(stack)
        wide[pl.ds(2 * k, BLOCK, stride=BLOCKS), :] = turned[:BLOCK]
        wide[pl.ds(2 * k + 1, BLOCK, stride=BLOCKS), :] = turned[BLOCK:]
    out_ref[...] = wide[...].astype(BF16)


def strain_kernel(carry_ref, arrived_ref, gram_ref, send_ref, strain_ref):
    devs = arrived_ref.shape[0]
    copies = send_ref.shape[0]
    points = strain_ref.shape[1]
    index = side_by_side(carry_ref[144:152, :points].astype(jnp.int32))
    refs = 8 * points
    partner = (index - NODES) >> 4
    other = jnp.where(iota((devs, refs), 0) == partner, 1.0, 0.0).astype(BF16)
    ghost = jnp.transpose(arrived_ref[:, 0, :])[:64]
    ghost = jnp.concatenate(split3(ghost), axis=0).astype(BF16)
    found = bdot(ghost, other)
    found = (found[:64] + found[64:128]) + found[128:]
    found = jnp.where(iota((64, refs), 0) % 16 == index % 16, found, 0.0)
    sums = [jnp.sum(found[16 * c : 16 * c + 16], axis=0, keepdims=True) for c in range(3)]
    nodal = by_node(jnp.concatenate(sums, axis=0), points) + carry_ref[160:184, :points]
    strain = jnp.concatenate(
        [
            jnp.sum(carry_ref[24 * c : 24 * c + 24, :points] * nodal, axis=0, keepdims=True)
            for c in range(6)
        ],
        axis=0,
    )
    strain_ref[...] = jnp.concatenate([strain, jnp.zeros((2, points), F32)], axis=0)

    assign = carry_ref[152:153, :points]
    plastic = assign >= 0.0
    flags = jnp.where(plastic, 1.0, 0.0)
    before = jnp.where(iota((points, points), 0) < iota((points, points), 1), 1.0, 0.0)
    rank = bdot(jnp.broadcast_to(flags, (8, points)).astype(BF16), before.astype(BF16))
    pick = jnp.where(plastic & (rank == iota((8, points), 0).astype(F32)), 1.0, 0.0)
    values = jnp.concatenate(
        [
            strain,
            assign + 1.0,
            jnp.zeros((LANES - 7, points), F32),
        ],
        axis=0,
    )
    chosen = dot_nt(pick, values)
    line = chosen[0:1]
    for slot in range(1, PLASTIC_CAP):
        line = line + pltpu.roll(chosen[slot : slot + 1], 8 * slot, 1)
    line = jnp.concatenate([gram_ref[...], line], axis=1)
    send_ref[:, 0, :] = jnp.broadcast_to(line, (copies, 4 * LANES))


def section_kernel(arrived_ref, send_ref):
    devs = arrived_ref.shape[0]
    groups = send_ref.shape[0] // 2
    total = jnp.sum(arrived_ref[:, 0, : 3 * LANES], axis=0, keepdims=True)
    cand = arrived_ref[:, 0, 3 * LANES :]
    turned = jnp.transpose(jnp.concatenate([cand] * (LANES // devs), axis=0))
    line = jnp.concatenate([turned[8 * n : 8 * n + 8, :devs] for n in range(PLASTIC_CAP)], axis=1)
    width = PLASTIC_CAP * devs
    target = line[6:7].astype(jnp.int32) - 1
    row = iota((64, width), 0)
    keep = ((target >> 7) == row // 8) & (row % 8 < 6)
    left = [
        jnp.where(keep, jnp.concatenate([part] * 8, axis=0), 0.0).astype(BF16)
        for part in split3(line)
    ]
    hot = jnp.where(iota((POINTS, width), 0) == (target & (POINTS - 1)), 1.0, 0.0).astype(BF16)
    dense = bdot_nt(jnp.concatenate(left, axis=0), hot)
    dense = (dense[:64] + dense[64:128]) + dense[128:]
    for h in range(groups):
        for core in range(2):
            for c in range(6):
                lanes = slice(c * LANES, (c + 1) * LANES)
                send_ref[2 * h + core, :, lanes] = dense[8 * h + c : 8 * h + c + 1]
            send_ref[2 * h + core, :, 6 * LANES :] = total


def coefficients(m, centre, step):
    m00, m01, m02, m03, m22, m23, m33, energy = m
    m11 = m00 + (step[1] * m02 + (centre[1] - centre[0]) * m01) / step[0]
    m12 = (step[2] * m03 + (centre[2] - centre[0]) * m02 + step[1] * m01) / step[0]
    m13 = (step[1] * (m22 - m11) + (centre[1] - centre[2]) * m12 + step[0] * m02) / step[2]
    products = [
        [m00, m01, m02, m03],
        [m01, m11, m12, m13],
        [m02, m12, m22, m23],
        [m03, m13, m23, m33],
    ]

    def gram(a, b):
        return products[a][b]

    def image(a, b):
        a, b = max(a, b), min(a, b)
        if b == 3:
            return energy
        value = step[b] * products[a][b + 1] + centre[b] * products[a][b]
        return value + step[b - 1] * products[a][b - 1] if b else value

    def inner(p, form):
        total = None
        for a in range(len(p)):
            for b in range(a, len(p)):
                term = p[a] * p[b] * form(a, b)
                if a != b:
                    term = 2.0 * term
                total = term if total is None else total + term
        return total

    def times(p):
        out = [jnp.zeros_like(p[0]) for _ in range(len(p) + 1)]
        for b, v in enumerate(p):
            out[b + 1] = out[b + 1] + step[b] * v
            out[b] = out[b] + centre[b] * v
            if b:
                out[b - 1] = out[b - 1] + step[b - 1] * v
        return out

    one = jnp.ones_like(m00)
    answer = []
    residual = [one]
    direction = [one]
    norm = m00
    for turn in range(4):
        alpha = norm / inner(direction, image)
        answer = answer + [jnp.zeros_like(one)]
        answer = [x + alpha * p for x, p in zip(answer, direction)]
        if turn < 3:
            stepped = times(direction)
            residual = residual + [jnp.zeros_like(one)]
            residual = [r - alpha * v for r, v in zip(residual, stepped)]
            later = inner(residual, gram)
            beta = later / norm
            direction = direction + [jnp.zeros_like(one)]
            direction = [r + beta * p for r, p in zip(residual, direction)]
            norm = later
    return answer


def final_kernel(
    scale,
    arrived_ref,
    strain_ref,
    assign_ref,
    elastic_ref,
    basis_ref,
    u_ref,
    stress_ref,
    out_hbm,
    out_ref,
    sems,
):
    groups = arrived_ref.shape[0] // 2
    points = strain_ref.shape[1]
    mine = lax.axis_index("group")
    centre = [basis_ref[n : n + 1, :] for n in range(3)]
    step = [basis_ref[n + 3 : n + 4, :] for n in range(3)]
    both = jnp.sum(arrived_ref[:, 0, : 6 * LANES], axis=0, keepdims=True)
    field = [both[:, c * LANES : (c + 1) * LANES] for c in range(6)]
    field = jnp.concatenate(field + [jnp.zeros((2, LANES), F32)], axis=0)

    def unfold(lines):
        tiles = []
        for t in range(3):
            tile = lines[:, t * LANES : (t + 1) * LANES]
            low = iota(tile.shape, 1) < 64
            tiles.append(jnp.where(low, tile, 0.0))
            tiles.append(jnp.where(low, pltpu.roll(tile, 64, 1), 0.0))
        blank = jnp.zeros((2, LANES), F32)
        return [
            jnp.concatenate([v[h : h + 1] for v in tiles] + [blank], axis=0)
            for h in range(lines.shape[0])
        ]

    lane = iota((8, LANES), 1)
    diagonal = (iota((64, LANES), 0) // 8) == (iota((64, LANES), 1) % 64) // 8

    def tall(x):
        return jnp.concatenate([x] * 8, axis=0)

    def opened(moments):
        high, middle, low = split3(moments + pltpu.roll(moments, 64, 1))
        first = jnp.where(diagonal, tall(jnp.where(lane < 64, high, middle)), 0.0).astype(BF16)
        second = jnp.where(diagonal, tall(jnp.where(lane < 64, high, low)), 0.0).astype(BF16)
        return jnp.concatenate([first, first, second], axis=1)

    def meeting(x):
        high, middle, low = (tall(part) for part in split3(x))
        parts = [high, high, middle, middle, low, high]
        return jnp.concatenate(parts, axis=0).astype(BF16)

    strain = strain_ref[...]
    padded = jnp.concatenate([strain, jnp.zeros((8, LANES - points), F32)], axis=1)
    assign = jnp.concatenate(
        [assign_ref[...], jnp.full((1, LANES - points), -1, jnp.int32)], axis=1
    )
    halves = arrived_ref[:, 0, 6 * LANES :]
    whole = [halves[2 * h : 2 * h + 1] + halves[2 * h + 1 : 2 * h + 2] for h in range(groups)]
    every = unfold(jnp.concatenate(whole, axis=0))
    own = jnp.zeros((8, LANES), F32)
    for h in range(groups):
        own = own + jnp.where(mine == h, every[h], 0.0)
    forces = bdot(opened(own), meeting(field))
    every = jnp.concatenate([opened(v) for v in every], axis=0)
    products = bdot(every, meeting(padded))
    group_of = assign >> 7
    local = jnp.zeros((64, LANES), F32)
    for h in range(groups):
        local = local + jnp.where(group_of == h, products[64 * h : 64 * h + 64], 0.0)

    m = []
    for n in range(8):
        first = jnp.sum(forces[8 * n : 8 * n + 8] * field, axis=0, keepdims=True)
        second = jnp.sum(local[8 * n : 8 * n + 8] * padded, axis=0, keepdims=True)
        m.append(jnp.concatenate([first, second], axis=0))
    answer = coefficients(m, centre, step)

    extra = jnp.zeros((8, LANES), F32)
    for n in range(4):
        extra = extra + answer[n][1:2] * local[8 * n : 8 * n + 8]
    elastic_stress = dot(elastic_ref[...], strain[:6])
    plastic = assign_ref[...] >= 0
    stress_ref[...] = elastic_stress + jnp.where(plastic, extra[:6, :points], 0.0)

    right = jnp.concatenate([(scale * answer[n][0:1]) * field for n in range(4)], axis=0)
    high = right.astype(BF16).astype(F32)
    right = jnp.concatenate([high, high, right - high, jnp.zeros_like(high)], axis=0).astype(BF16)
    copies = []
    for part in range(6):
        rows = pl.ds(512 * part, 512)
        out_ref[rows, :] = bdot(u_ref[rows, :], right)
        copy = pltpu.make_async_copy(out_ref.at[rows], out_hbm.at[rows], sems.at[part])
        copy.start()
        copies.append(copy)
    for copy in copies:
        copy.wait()


def call(kernel, outs, *args, scratch=(), own_copies=0, last_out=None):
    vmem = pl.BlockSpec(memory_space=pltpu.VMEM)
    many = isinstance(outs, list)
    out_specs = [vmem] * len(outs) if many else vmem
    if last_out:
        out_specs[-1] = pl.BlockSpec(memory_space=last_out)
    scratch = list(scratch)
    if own_copies:
        scratch += [pltpu.VMEM(x.shape, x.dtype) for x in args[:own_copies]]
        scratch += [pltpu.SemaphoreType.DMA((own_copies,))]
    spaces = [pl.BlockSpec(memory_space=pltpu.HBM)] * own_copies + [vmem] * len(args)
    limit = 60 if own_copies else 32
    return pl.pallas_call(
        kernel,
        out_shape=outs,
        in_specs=spaces[: len(args)],
        out_specs=out_specs,
        scratch_shapes=scratch,
        compiler_params=pltpu.CompilerParams(vmem_limit_bytes=limit * 1024 * 1024),
    )(*args)


def arr(*shape, dtype=F32):
    return jax.ShapeDtypeStruct(shape, dtype)


def shifted(x, by):
    devices = lax.axis_size("dev")
    return lax.ppermute(x, "dev", [(i, (i + by) % devices) for i in range(devices)])


def exchange(x, axis, members=None):
    return lax.all_to_all(
        x, axis, split_axis=0, concat_axis=0, tiled=True, axis_index_groups=members
    )


def local(
    displacement,
    connectivity,
    face_nodes,
    strain_map,
    assignment,
    phases,
    load_map,
    stiff_root,
    chain_map,
    bridge_map,
    elastic,
):
    groups = lax.axis_size("group")
    devs = lax.axis_size("dev")
    points = connectivity.shape[1]
    assign = assignment.reshape(1, -1)

    listed = jnp.transpose(face_nodes, (0, 2, 1))
    load = jnp.transpose(load_map, (0, 2, 1))
    labels = jnp.transpose(phases, (0, 2, 1))
    sources = [displacement, listed, load, labels, connectivity, strain_map, assign]
    outgoing, packed, carry = call(
        first_kernel,
        [arr(devs, 1, LANES), arr(ROWS, LANES), arr(184, LANES)],
        *sources,
        own_copies=len(sources),
    )
    *weights, terms = call(
        tables,
        [
            arr(3 * LANES, 2 * LANES, dtype=BF16),
            arr(3 * LANES, LANES, dtype=BF16),
            arr(9 * LANES, LANES, dtype=BF16),
            arr(8, LANES),
        ],
        stiff_root,
        chain_map,
        bridge_map,
    )
    arrived = exchange(outgoing, "dev")
    near = [shifted(packed, 1), shifted(packed, 2), shifted(packed, -1), shifted(packed, -2)]
    vectors, gram = call(
        krylov_kernel,
        [arr(4, ROWS, LANES), arr(1, 3 * LANES)],
        packed,
        *near,
        *weights,
        terms,
    )
    send, strain = call(
        strain_kernel,
        [arr(devs // 2, 1, 4 * LANES), arr(8, points)],
        carry,
        arrived,
        gram,
    )
    same_core = [list(range(core, devs, 2)) for core in range(2)]
    same_chip = [
        [g * devs + chip + core for g in range(groups) for core in range(2)]
        for chip in range(0, devs, 2)
    ]
    section = exchange(send, "dev", same_core)
    turned = call(
        turn_kernel,
        arr(BLOCK * BLOCKS, LANES, dtype=BF16),
        vectors,
        scratch=[pltpu.VMEM((BLOCK * BLOCKS, LANES), F32)],
    )
    across = call(section_kernel, arr(2 * groups, 1, 9 * LANES), section)
    gathered = exchange(across, ("group", "dev"), same_chip)
    scale = math.sqrt(BLOCK * devs * BLOCKS)
    stress, fluctuation = call(
        lambda *refs: final_kernel(scale, *refs),
        [arr(6, points), arr(BLOCK * BLOCKS, POINTS)],
        gathered,
        strain,
        assign,
        elastic,
        terms,
        turned,
        scratch=[
            pltpu.VMEM((BLOCK * BLOCKS, POINTS), F32),
            pltpu.SemaphoreType.DMA((6,)),
        ],
        last_out=pl.ANY,
    )
    return stress, fluctuation.reshape(1, BLOCK, BLOCKS, POINTS)


def solution(mesh):
    in_specs = (
        P(None, ("group", "dev")),
        P(None, ("group", "dev")),
        P(("group", "dev"), None, None),
        P(None, None, ("group", "dev")),
        P(("group", "dev")),
        P("group", None, "dev"),
        P(None, None, "dev"),
        P(),
        P(),
        P(),
        P(),
    )
    out_specs = (P(None, ("group", "dev")), P("group", None, "dev", None))
    return jax.shard_map(local, mesh=mesh, in_specs=in_specs, out_specs=out_specs, check_vma=False)
```

time: 84.5 us -> 81.2 us (0.961)
  blocking collectives: 20.3 us -> 17.7 us
  Pallas kernels: 14.6 us -> 12.6 us
  starting transfers between devices: 35.7 us -> 37.6 us
  local copies, waits for them, and re-layouts: 5.58 us -> 3.99 us
  waiting for transfers between devices: 6.89 us -> 8 us
    all_to_all x1, blocking collectives: 20.3 us -> 17.7 us  [exchange(): lax.all_to_all(x, axis, split_axis=0, concat_axis=0, tiled=True, axis_ind...]
    all_to_all x2, starting transfers between devices: 14.4 us -> 16.4 us  [exchange(): lax.all_to_all(x, axis, split_axis=0, concat_axis=0, tiled=True, axis_ind...]
    pallas_call x8 -> x7, Pallas kernels: 14.6 us -> 12.6 us  [call(): pl.pallas_call(kernel, out_shape=outs, in_specs=spaces[:len(args)], out_s...]
    unnamed x21 -> x14, local copies, waits for them, and re-layouts: 5.58 us -> 3.99 us
    all_to_all x2, waiting for transfers between devices: 6.88 us -> 7.99 us  [exchange(): lax.all_to_all(x, axis, split_axis=0, concat_axis=0, tiled=True, axis_ind...]
  transfers between devices with their start and end apart: 6 -> 6, of which waited for: 2 -> 2; matrix products, arithmetic and copies ran while one was open for 1% -> 0% of each run, Pallas kernels for 10% -> 8%
where the time goes in v2:
time: 81.2 us; the launch traced here: 80.6 us
  starting transfers between devices  37.6 us (46%)
  blocking collectives  17.7 us (22%)
  Pallas kernels  12.6 us (16%)
  waiting for transfers between devices  8 us (10%)
  local copies, waits for them, and re-layouts  3.99 us (5%)
    ppermute x4, starting transfers between devices, shifted(): lax.ppermute(x, 'dev', [(i, (i + by) % devices) for i in range(devices)])  21.2 us
    all_to_all x1, blocking collectives, exchange(): lax.all_to_all(x, axis, split_axis=0, concat_axis=0, tiled=True, axis_ind...  17.7 us
    all_to_all x2, starting transfers between devices, exchange(): lax.all_to_all(x, axis, split_axis=0, concat_axis=0, tiled=True, axis_ind...  16.4 us
    pallas_call x7, Pallas kernels, call(): pl.pallas_call(kernel, out_shape=outs, in_specs=spaces[:len(args)], out_s...  12.6 us
    all_to_all x2, waiting for transfers between devices, exchange(): lax.all_to_all(x, axis, split_axis=0, concat_axis=0, tiled=True, axis_ind...  7.99 us
    unnamed x14, local copies, waits for them, and re-layouts  3.99 us
  transfers between devices with their start and end apart: 6, of which 2 were waited for; matrix products, arithmetic and copies ran while one was open for 0% of the time, Pallas kernels for 8%

profile of v2, /device:TPU:1, one launch (start us, length us, event | category | flops | bytes accessed | tf_op | source)
XLA Modules:
  0.0 80.6 jit_solution(12362005707877423716)
XLA Ops:
  0.6 0.0 copy-start.5
  0.6 0.0 copy-start.6
  0.7 2.4 %shard_map.122 = (f32[64,1,128]{2,1,0:T(1,128)}, f32[192,128]{1,0:T(8,128)}, f32[184,128]{1,0:T(8,128)}) custom-call(f32[3,256]{1,0:T(4,128)} %refs_0_.1, s32[1,16,64]{2,1,0:T(8,128)} %bitcast.9, f32[6,48,64]{2,1,0:T(8,128)} %bitcast.7, s32[1,48,64]{2,1,0:T(8,128)} %bitcast.8, s32[8,64]{1,0:T(8,128)} %refs_4_.1, f32[6,24,64]{2,1,0:T(8,128)} %refs_5_.1, ...), custom_call_target="tpu_custom_call" | custom-call | tf_op jit(solution)/shard_map/pallas_call | solution.py:574
  3.0 13.7 %collective-permute-start.3 = (f32[192,128]{1,0:T(8,128)}, f32[192,128]{1,0:T(8,128)S(1)}, u32[]{:S(2)}, u32[]{:S(2)}) collective-permute-start(f32[192,128]{1,0:T(8,128)} %get-tuple-element.17.own_ref), channel_id=1, source_target_pairs={{0,62},{1,63},{2,0},{3,1},{4,2},{5,3},{6,4},{7,5},{8,6},{9,7},{10,... | collective-permute-start | bytes 294920 | tf_op jit(solution)/shard_map/ppermute | solution.py:590
  16.7 2.9 %collective-permute-start.2 = (f32[192,128]{1,0:T(8,128)}, f32[192,128]{1,0:T(8,128)S(1)}, u32[]{:S(2)}, u32[]{:S(2)}) collective-permute-start(f32[192,128]{1,0:T(8,128)} %get-tuple-element.17.own_ref), channel_id=1, source_target_pairs={{0,63},{1,0},{2,1},{3,2},{4,3},{5,4},{6,5},{7,6},{8,7},{9,8},{10,9... | collective-permute-start | bytes 294920 | tf_op jit(solution)/shard_map/ppermute | solution.py:590
  19.6 1.9 %collective-permute-start.1 = (f32[192,128]{1,0:T(8,128)}, f32[192,128]{1,0:T(8,128)S(1)}, u32[]{:S(2)}, u32[]{:S(2)}) collective-permute-start(f32[192,128]{1,0:T(8,128)} %get-tuple-element.17.own_ref), channel_id=1, source_target_pairs={{0,2},{1,3},{2,4},{3,5},{4,6},{5,7},{6,8},{7,9},{8,10},{9,11},{10,... | collective-permute-start | bytes 294920 | tf_op jit(solution)/shard_map/ppermute | solution.py:590
  21.5 2.7 %collective-permute-start = (f32[192,128]{1,0:T(8,128)}, f32[192,128]{1,0:T(8,128)S(1)}, u32[]{:S(2)}, u32[]{:S(2)}) collective-permute-start(f32[192,128]{1,0:T(8,128)} %get-tuple-element.17.own_ref), channel_id=1, source_target_pairs={{0,1},{1,2},{2,3},{3,4},{4,5},{5,6},{6,7},{7,8},{8,9},{9,10},{10,1... | collective-permute-start | bytes 294920 | tf_op jit(solution)/shard_map/ppermute | solution.py:590
  24.2 7.6 %all-to-all-start = ((f32[64,1,128]{2,1,0:T(1,128)}), f32[64,1,128]{2,1,0:T(1,128)S(1)}, u32[]{:S(2)}, u32[]{:S(2)}) async-start(f32[64,1,128]{2,1,0:T(1,128)} %get-tuple-element.16), calls=%async_computation | async-start | bytes 65536 | tf_op jit(solution)/shard_map/all_to_all | solution.py:594
  31.8 0.0 copy-start.2
  31.8 0.7 copy-done.2
  32.6 0.8 copy-done.3
  33.3 0.0 copy-start.4
  33.3 0.7 copy-done.4
  34.0 1.2 %shard_map.123 = (bf16[384,256]{1,0:T(8,128)(2,1)S(1)}, bf16[384,128]{1,0:T(8,128)(2,1)S(1)}, bf16[1152,128]{1,0:T(8,128)(2,1)S(1)}, f32[8,128]{1,0:T(8,128)S(1)}) custom-call(f32[64,64]{1,0:T(8,128)S(1)} %copy-done.2, f32[64,64]{1,0:T(8,128)S(1)} %copy-done.3, f32[16,16]{1,0:T(8,128)S(1)} %copy-done.4), custom_call_target="tpu_custom_call" | custom-call | tf_op jit(solution)/shard_map/pallas_call | solution.py:574
  35.3 0.0 collective-permute-done.3.p2_ref
  35.3 0.0 collective-permute-done.2.p1_ref
  35.3 0.0 collective-permute-done.1.m2_ref
  35.3 0.0 collective-permute-done.m1_ref
  35.3 0.0 copy-start
  35.3 0.9 %copy-done = f32[192,128]{1,0:T(8,128)S(1)} copy-done((f32[192,128]{1,0:T(8,128)S(1)}, f32[192,128]{1,0:T(8,128)}, u32[]{:S(2)}) %copy-start) | copy-done | bytes 98328
  36.2 4.2 %shard_map.124 = (f32[4,192,128]{2,1,0:T(8,128)S(1)}, f32[1,384]{1,0:T(1,128)S(1)}) custom-call(f32[192,128]{1,0:T(8,128)S(1)} %copy-done, f32[192,128]{1,0:T(8,128)S(1)} %collective-permute-done.m1_ref, f32[192,128]{1,0:T(8,128)S(1)} %collective-permute-done.1.m2_ref, f32[192,128]{1,0:T(8,128)S(1)} %collective-permute-done.2.p1_ref, ...), custom_call_target="tpu_custom_call" | custom-call | tf_op jit(solution)/shard_map/pallas_call | solution.py:574
  40.4 0.7 all-to-all-done.arrived_ref
  41.1 0.9 %copy-done.1 = f32[184,128]{1,0:T(8,128)S(1)} copy-done((f32[184,128]{1,0:T(8,128)S(1)}, f32[184,128]{1,0:T(8,128)}, u32[]{:S(2)}) %copy-start.1) | copy-done | bytes 94232
  42.0 0.6 shard_map.125
  42.6 17.7 %all_to_all.15.arrived_ref = f32[32,1,512]{2,1,0:T(1,128)S(1)} all-to-all(f32[32,1,512]{2,1,0:T(1,128)S(1)} %get-tuple-element.23), channel_id=1, replica_groups={{0,2,4,6,8,10,12,14,16,18,20,22,24,26,28,30,32,34,36,38,40,42,44,46,48,..., dimensions={0} | all-to-all | bytes 131072 | tf_op jit(solution)/shard_map/all_to_all | solution.py:594
  60.2 1.0 %shard_map.126 = f32[16,1,1152]{2,1,0:T(1,128)} custom-call(f32[32,1,512]{2,1,0:T(1,128)S(1)} %all_to_all.15.arrived_ref), custom_call_target="tpu_custom_call" | custom-call | tf_op jit(solution)/shard_map/pallas_call | solution.py:574
  61.2 8.8 %all-to-all-start.2 = ((f32[16,1,1152]{2,1,0:T(1,128)}), f32[16,1,1152]{2,1,0:T(1,128)S(1)}, u32[]{:S(2)}, u32[]{:S(2)}) async-start(f32[16,1,1152]{2,1,0:T(1,128)} %shard_map.126), calls=%async_computation.2 | async-start | bytes 147456 | tf_op jit(solution)/shard_map/all_to_all | solution.py:594
  70.1 0.7 shard_map.127.refs_5_
  70.7 7.3 %all-to-all-done.2.refs_0_ = f32[16,1,1152]{2,1,0:T(1,128)S(1)} async-done(((f32[16,1,1152]{2,1,0:T(1,128)}), f32[16,1,1152]{2,1,0:T(1,128)S(1)}, u32[]{:S(2)}, u32[]{:S(2)}) %all-to-all-start.2) | async-done | bytes 73760 | tf_op jit(solution)/shard_map/all_to_all | solution.py:594
  78.0 0.0 copy-done.5
  78.0 0.0 copy-done.6
  78.0 2.6 %shard_map.128 = (f32[6,64]{1,0:T(8,128)}, f32[3072,128]{1,0:T(8,128)}) custom-call(f32[16,1,1152]{2,1,0:T(1,128)S(1)} %all-to-all-done.2.refs_0_, f32[8,64]{1,0:T(8,128)S(1)} %get-tuple-element.24.refs_1_, s32[1,64]{1,0:T(1,128)S(1)} %bitcast.6, f32[6,6]{1,0:T(8,128)S(1)} %copy-done.5, f32[8,128]{1,0:T(8,128)S(1)} %get-tuple-element.21.basis_ref.refs_4_, ...), custom_call_target="tpu_custom_call" | custom-call | tf_op jit(solution)/shard_map/pallas_call | solution.py:574
  (2 shorter events, 0.0 us)
Async XLA Ops:
  0.6 77.4 %copy-start.5 = (f32[6,6]{1,0:T(8,128)S(1)}, f32[6,6]{1,0:T(8,128)}, u32[]{:S(2)}) copy-start(f32[6,6]{1,0:T(8,128)} %refs_3_.1) | copy-start | bytes 436
  0.6 77.4 %copy-start.6 = (s32[64]{0:T(128)S(1)}, s32[64]{0:T(128)}, u32[]{:S(2)}) copy-start(s32[64]{0:T(128)} %param.15) | copy-start | bytes 772
  3.0 32.2 %collective-permute-start.3 = (f32[192,128]{1,0:T(8,128)}, f32[192,128]{1,0:T(8,128)S(1)}, u32[]{:S(2)}, u32[]{:S(2)}) collective-permute-start(f32[192,128]{1,0:T(8,128)} %get-tuple-element.17.own_ref), channel_id=1, source_target_pairs={{0,62},{1,63},{2,0},{3,1},{4,2},{5,3},{6,4},{7,5},{8,6},{9,7},{10,... | collective-permute-start | bytes 294920 | tf_op jit(solution)/shard_map/ppermute | solution.py:590
  16.7 18.6 %collective-permute-start.2 = (f32[192,128]{1,0:T(8,128)}, f32[192,128]{1,0:T(8,128)S(1)}, u32[]{:S(2)}, u32[]{:S(2)}) collective-permute-start(f32[192,128]{1,0:T(8,128)} %get-tuple-element.17.own_ref), channel_id=1, source_target_pairs={{0,63},{1,0},{2,1},{3,2},{4,3},{5,4},{6,5},{7,6},{8,7},{9,8},{10,9... | collective-permute-start | bytes 294920 | tf_op jit(solution)/shard_map/ppermute | solution.py:590
  19.6 15.7 %collective-permute-start.1 = (f32[192,128]{1,0:T(8,128)}, f32[192,128]{1,0:T(8,128)S(1)}, u32[]{:S(2)}, u32[]{:S(2)}) collective-permute-start(f32[192,128]{1,0:T(8,128)} %get-tuple-element.17.own_ref), channel_id=1, source_target_pairs={{0,2},{1,3},{2,4},{3,5},{4,6},{5,7},{6,8},{7,9},{8,10},{9,11},{10,... | collective-permute-start | bytes 294920 | tf_op jit(solution)/shard_map/ppermute | solution.py:590
  21.5 13.8 %collective-permute-start = (f32[192,128]{1,0:T(8,128)}, f32[192,128]{1,0:T(8,128)S(1)}, u32[]{:S(2)}, u32[]{:S(2)}) collective-permute-start(f32[192,128]{1,0:T(8,128)} %get-tuple-element.17.own_ref), channel_id=1, source_target_pairs={{0,1},{1,2},{2,3},{3,4},{4,5},{5,6},{6,7},{7,8},{8,9},{9,10},{10,1... | collective-permute-start | bytes 294920 | tf_op jit(solution)/shard_map/ppermute | solution.py:590
  24.2 16.9 %all-to-all-start = ((f32[64,1,128]{2,1,0:T(1,128)}), f32[64,1,128]{2,1,0:T(1,128)S(1)}, u32[]{:S(2)}, u32[]{:S(2)}) async-start(f32[64,1,128]{2,1,0:T(1,128)} %get-tuple-element.16), calls=%async_computation | async-start | bytes 65536 | tf_op jit(solution)/shard_map/all_to_all | solution.py:594
  31.8 0.8 copy-start.2
  32.6 0.8 copy-start.3
  33.3 0.7 copy-start.4
  35.3 0.9 %copy-start = (f32[192,128]{1,0:T(8,128)S(1)}, f32[192,128]{1,0:T(8,128)}, u32[]{:S(2)}) copy-start(f32[192,128]{1,0:T(8,128)} %get-tuple-element.17.own_ref) | copy-start | bytes 294916
  41.1 0.9 %copy-start.1 = (f32[184,128]{1,0:T(8,128)S(1)}, f32[184,128]{1,0:T(8,128)}, u32[]{:S(2)}) copy-start(f32[184,128]{1,0:T(8,128)} %get-tuple-element.15.carry_ref) | copy-start | bytes 282628
  61.2 16.8 %all-to-all-start.2 = ((f32[16,1,1152]{2,1,0:T(1,128)}), f32[16,1,1152]{2,1,0:T(1,128)S(1)}, u32[]{:S(2)}, u32[]{:S(2)}) async-start(f32[16,1,1152]{2,1,0:T(1,128)} %shard_map.126), calls=%async_computation.2 | async-start | bytes 147456 | tf_op jit(solution)/shard_map/all_to_all | solution.py:594

commit v3 on v2

--- a/solution.py
+++ b/solution.py
@@ -148,22 +148,28 @@
 
 
 def first_kernel(*refs):
-    face_ref, pack_ref, carry_ref, disp, listed, load, phase, conn, maps, assign, sems = refs[7:]
-    fetch(refs[:7], [disp, listed, load, phase, conn, maps, assign], sems)
+    face_ref, pack_ref, rest_ref, *held, sems = refs[10:]
+    fetch(refs[:10], held, sems)
+    disp, listed, load, phase, conn, maps, assign, root, chain, bridge = held
     faces(disp, listed, face_ref)
     pack(load, phase, pack_ref)
     points = conn.shape[1]
     blank = jnp.zeros((7, points), F32)
     for c in range(6):
-        carry_ref[24 * c : 24 * c + 24, :points] = maps[c]
-    carry_ref[144:152, :points] = conn[...].astype(F32)
-    carry_ref[152:160, :points] = jnp.concatenate([assign[...].astype(F32), blank], axis=0)
-    carry_ref[160:184, :points] = own_nodes(disp, conn)
-    carry_ref[:, points:] = jnp.zeros((184, LANES - points), F32)
-
-
-def tables(root_ref, chain_ref, bridge_ref, w1, wb, w2, basis_ref):
-    root, chain, bridge = root_ref[...], chain_ref[...], bridge_ref[...]
+        rest_ref[24 * c : 24 * c + 24, :points] = maps[c]
+    rest_ref[144:152, :points] = conn[...].astype(F32)
+    rest_ref[152:160, :points] = jnp.concatenate([assign[...].astype(F32), blank], axis=0)
+    rest_ref[160:184, :points] = own_nodes(disp, conn)
+    rest_ref[:184, points:] = jnp.zeros((184, LANES - points), F32)
+    rest_ref[184:248, :] = jnp.concatenate([root[...], chain[...]], axis=1)
+    wide = jnp.concatenate([bridge[...], jnp.zeros((IFACE, LANES - IFACE), F32)], axis=1)
+    rest_ref[248:264, :] = wide
+    rest_ref[264:, :] = pack_ref[...]
+
+
+def tables(rest_ref, w1, wb, w2, basis_ref):
+    root, chain = rest_ref[184:248, :BLOCK], rest_ref[184:248, BLOCK:]
+    bridge = rest_ref[248:264, :IFACE]
     zero = jnp.zeros((BLOCK, BLOCK), F32)
 
     def straight(m):
@@ -217,7 +223,7 @@
 
 
 def krylov_kernel(
-    own_ref, m1_ref, m2_ref, p1_ref, p2_ref, w1, wb, w2, basis_ref, u_ref, gram_ref
+    rest_ref, m1_ref, m2_ref, p1_ref, p2_ref, w1, wb, w2, basis_ref, cand_ref, u_ref, send_ref
 ):
     centre = [basis_ref[n : n + 1, :] for n in range(3)]
     step = [basis_ref[n + 3 : n + 4, :] for n in range(3)]
@@ -262,7 +268,7 @@
         return ridge * x + edge + f + stage(left, w2)
 
     zero = jnp.zeros((ROWS, LANES), F32)
-    near = [m1_ref[...], own_ref[...], p1_ref[...], p2_ref[...]]
+    near = [m1_ref[...], rest_ref[264:, :], p1_ref[...], p2_ref[...]]
     w = jnp.concatenate([weights_of(x) for x in near], axis=0)
 
     x0 = jnp.concatenate(near, axis=0)
@@ -309,10 +315,12 @@
     moments = jnp.where(at == 5, pair(2, 3, 5), moments)
     moments = jnp.where(at == 6, pair(3, 3, 6), moments)
     moments = jnp.where(at == 7, energy, moments)
-    for t in range(3):
-        gram_ref[:, t * LANES : (t + 1) * LANES] = moments[2 * t : 2 * t + 1] + pltpu.roll(
-            moments[2 * t + 1 : 2 * t + 2], 64, 1
-        )
+    line = [
+        moments[2 * t : 2 * t + 1] + pltpu.roll(moments[2 * t + 1 : 2 * t + 2], 64, 1)
+        for t in range(3)
+    ]
+    line = jnp.concatenate(line + [cand_ref[...]], axis=1)
+    send_ref[:, 0, :] = jnp.broadcast_to(line, (send_ref.shape[0], 4 * LANES))
 
 
 def turn_kernel(u_ref, out_ref, wide):
@@ -326,11 +334,10 @@
     out_ref[...] = wide[...].astype(BF16)
 
 
-def strain_kernel(carry_ref, arrived_ref, gram_ref, send_ref, strain_ref):
+def strain_kernel(rest_ref, arrived_ref, cand_ref, strain_ref):
     devs = arrived_ref.shape[0]
-    copies = send_ref.shape[0]
     points = strain_ref.shape[1]
-    index = side_by_side(carry_ref[144:152, :points].astype(jnp.int32))
+    index = side_by_side(rest_ref[144:152, :points].astype(jnp.int32))
     refs = 8 * points
     partner = (index - NODES) >> 4
     other = jnp.where(iota((devs, refs), 0) == partner, 1.0, 0.0).astype(BF16)
@@ -340,17 +347,17 @@
     found = (found[:64] + found[64:128]) + found[128:]
     found = jnp.where(iota((64, refs), 0) % 16 == index % 16, found, 0.0)
     sums = [jnp.sum(found[16 * c : 16 * c + 16], axis=0, keepdims=True) for c in range(3)]
-    nodal = by_node(jnp.concatenate(sums, axis=0), points) + carry_ref[160:184, :points]
+    nodal = by_node(jnp.concatenate(sums, axis=0), points) + rest_ref[160:184, :points]
     strain = jnp.concatenate(
         [
-            jnp.sum(carry_ref[24 * c : 24 * c + 24, :points] * nodal, axis=0, keepdims=True)
+            jnp.sum(rest_ref[24 * c : 24 * c + 24, :points] * nodal, axis=0, keepdims=True)
             for c in range(6)
         ],
         axis=0,
     )
     strain_ref[...] = jnp.concatenate([strain, jnp.zeros((2, points), F32)], axis=0)
 
-    assign = carry_ref[152:153, :points]
+    assign = rest_ref[152:153, :points]
     plastic = assign >= 0.0
     flags = jnp.where(plastic, 1.0, 0.0)
     before = jnp.where(iota((points, points), 0) < iota((points, points), 1), 1.0, 0.0)
@@ -368,8 +375,7 @@
     line = chosen[0:1]
     for slot in range(1, PLASTIC_CAP):
         line = line + pltpu.roll(chosen[slot : slot + 1], 8 * slot, 1)
-    line = jnp.concatenate([gram_ref[...], line], axis=1)
-    send_ref[:, 0, :] = jnp.broadcast_to(line, (copies, 4 * LANES))
+    cand_ref[...] = line
 
 
 def section_kernel(arrived_ref, send_ref):
@@ -469,9 +475,7 @@
     basis_ref,
     u_ref,
     stress_ref,
-    out_hbm,
     out_ref,
-    sems,
 ):
     groups = arrived_ref.shape[0] // 2
     points = strain_ref.shape[1]
@@ -548,23 +552,15 @@
     right = jnp.concatenate([(scale * answer[n][0:1]) * field for n in range(4)], axis=0)
     high = right.astype(BF16).astype(F32)
     right = jnp.concatenate([high, high, right - high, jnp.zeros_like(high)], axis=0).astype(BF16)
-    copies = []
     for part in range(6):
-        rows = pl.ds(512 * part, 512)
+        rows = slice(512 * part, 512 * part + 512)
         out_ref[rows, :] = bdot(u_ref[rows, :], right)
-        copy = pltpu.make_async_copy(out_ref.at[rows], out_hbm.at[rows], sems.at[part])
-        copy.start()
-        copies.append(copy)
-    for copy in copies:
-        copy.wait()
-
-
-def call(kernel, outs, *args, scratch=(), own_copies=0, last_out=None):
+
+
+def call(kernel, outs, *args, scratch=(), own_copies=0):
     vmem = pl.BlockSpec(memory_space=pltpu.VMEM)
     many = isinstance(outs, list)
     out_specs = [vmem] * len(outs) if many else vmem
-    if last_out:
-        out_specs[-1] = pl.BlockSpec(memory_space=last_out)
     scratch = list(scratch)
     if own_copies:
         scratch += [pltpu.VMEM(x.shape, x.dtype) for x in args[:own_copies]]
@@ -618,12 +614,15 @@
     load = jnp.transpose(load_map, (0, 2, 1))
     labels = jnp.transpose(phases, (0, 2, 1))
     sources = [displacement, listed, load, labels, connectivity, strain_map, assign]
-    outgoing, packed, carry = call(
+    sources += [stiff_root, chain_map, bridge_map]
+    outgoing, packed, rest = call(
         first_kernel,
-        [arr(devs, 1, LANES), arr(ROWS, LANES), arr(184, LANES)],
+        [arr(devs, 1, LANES), arr(ROWS, LANES), arr(264 + ROWS, LANES)],
         *sources,
         own_copies=len(sources),
     )
+    arrived = exchange(outgoing, "dev")
+    near = [shifted(packed, 1), shifted(packed, 2), shifted(packed, -1), shifted(packed, -2)]
     *weights, terms = call(
         tables,
         [
@@ -632,26 +631,17 @@
             arr(9 * LANES, LANES, dtype=BF16),
             arr(8, LANES),
         ],
-        stiff_root,
-        chain_map,
-        bridge_map,
-    )
-    arrived = exchange(outgoing, "dev")
-    near = [shifted(packed, 1), shifted(packed, 2), shifted(packed, -1), shifted(packed, -2)]
-    vectors, gram = call(
+        rest,
+    )
+    cand, strain = call(strain_kernel, [arr(1, LANES), arr(8, points)], rest, arrived)
+    vectors, send = call(
         krylov_kernel,
-        [arr(4, ROWS, LANES), arr(1, 3 * LANES)],
-        packed,
+        [arr(4, ROWS, LANES), arr(devs // 2, 1, 4 * LANES)],
+        rest,
         *near,
         *weights,
         terms,
-    )
-    send, strain = call(
-        strain_kernel,
-        [arr(devs // 2, 1, 4 * LANES), arr(8, points)],
-        carry,
-        arrived,
-        gram,
+        cand,
     )
     same_core = [list(range(core, devs, 2)) for core in range(2)]
     same_chip = [
@@ -677,11 +667,6 @@
         elastic,
         terms,
         turned,
-        scratch=[
-            pltpu.VMEM((BLOCK * BLOCKS, POINTS), F32),
-            pltpu.SemaphoreType.DMA((6,)),
-        ],
-        last_out=pl.ANY,
     )
     return stress, fluctuation.reshape(1, BLOCK, BLOCKS, POINTS)
 

time: 81.2 us -> 79.3 us (0.977)
  waiting for transfers between devices: 8 us -> 14.5 us
  blocking collectives: 17.7 us -> 11.8 us
  local copies, waits for them, and re-layouts: 3.99 us -> 1.88 us
    all_to_all x2, waiting for transfers between devices: 7.99 us -> 14.4 us  [exchange(): lax.all_to_all(x, axis, split_axis=0, concat_axis=0, tiled=True, axis_ind...]
    all_to_all x1, blocking collectives: 17.7 us -> 11.8 us  [exchange(): lax.all_to_all(x, axis, split_axis=0, concat_axis=0, tiled=True, axis_ind...]
    unnamed x14 -> x8, local copies, waits for them, and re-layouts: 3.99 us -> 1.88 us
  transfers between devices with their start and end apart: 6 -> 6, of which waited for: 2 -> 2; matrix products, arithmetic and copies ran while one was open for 0% -> 0% of each run, Pallas kernels for 8% -> 3%
where the time goes in v3:
time: 79.3 us; the launch traced here: 78.8 us
  starting transfers between devices  37.7 us (48%)
  waiting for transfers between devices  14.5 us (18%)
  Pallas kernels  12.2 us (15%)
  blocking collectives  11.8 us (15%)
  local copies, waits for them, and re-layouts  1.88 us (2%)
    ppermute x4, starting transfers between devices, shifted(): lax.ppermute(x, 'dev', [(i, (i + by) % devices) for i in range(devices)])  21.2 us
    all_to_all x2, starting transfers between devices, exchange(): lax.all_to_all(x, axis, split_axis=0, concat_axis=0, tiled=True, axis_ind...  16.6 us
    all_to_all x2, waiting for transfers between devices, exchange(): lax.all_to_all(x, axis, split_axis=0, concat_axis=0, tiled=True, axis_ind...  14.4 us
    pallas_call x7, Pallas kernels, call(): pl.pallas_call(kernel, out_shape=outs, in_specs=spaces[:len(args)], out_s...  12.2 us
    all_to_all x1, blocking collectives, exchange(): lax.all_to_all(x, axis, split_axis=0, concat_axis=0, tiled=True, axis_ind...  11.8 us
    unnamed x8, local copies, waits for them, and re-layouts  1.88 us
  transfers between devices with their start and end apart: 6, of which 2 were waited for; matrix products, arithmetic and copies ran while one was open for 0% of the time, Pallas kernels for 3%

profile of v3, /device:TPU:1, one launch (start us, length us, event | category | flops | bytes accessed | tf_op | source)
XLA Modules:
  0.0 78.8 jit_solution(14244032270553169958)
XLA Ops:
  0.6 2.4 %shard_map.122 = (f32[64,1,128]{2,1,0:T(1,128)}, f32[192,128]{1,0:T(8,128)}, f32[456,128]{1,0:T(8,128)}) custom-call(f32[3,256]{1,0:T(4,128)} %refs_0_.1, s32[1,16,64]{2,1,0:T(8,128)} %bitcast.9, f32[6,48,64]{2,1,0:T(8,128)} %bitcast.7, s32[1,48,64]{2,1,0:T(8,128)} %bitcast.8, s32[8,64]{1,0:T(8,128)} %refs_4_.1, f32[6,24,64]{2,1,0:T(8,128)} %refs_5_.1, ...), custom_call_target="tpu_custom_call" | custom-call | tf_op jit(solution)/shard_map/pallas_call | solution.py:570
  3.1 13.7 %collective-permute-start.3 = (f32[192,128]{1,0:T(8,128)}, f32[192,128]{1,0:T(8,128)S(1)}, u32[]{:S(2)}, u32[]{:S(2)}) collective-permute-start(f32[192,128]{1,0:T(8,128)} %get-tuple-element.16), channel_id=1, source_target_pairs={{0,62},{1,63},{2,0},{3,1},{4,2},{5,3},{6,4},{7,5},{8,6},{9,7},{10,... | collective-permute-start | bytes 294920 | tf_op jit(solution)/shard_map/ppermute | solution.py:586
  16.8 2.9 %collective-permute-start.2 = (f32[192,128]{1,0:T(8,128)}, f32[192,128]{1,0:T(8,128)S(1)}, u32[]{:S(2)}, u32[]{:S(2)}) collective-permute-start(f32[192,128]{1,0:T(8,128)} %get-tuple-element.16), channel_id=1, source_target_pairs={{0,63},{1,0},{2,1},{3,2},{4,3},{5,4},{6,5},{7,6},{8,7},{9,8},{10,9... | collective-permute-start | bytes 294920 | tf_op jit(solution)/shard_map/ppermute | solution.py:586
  19.6 1.9 %collective-permute-start.1 = (f32[192,128]{1,0:T(8,128)}, f32[192,128]{1,0:T(8,128)S(1)}, u32[]{:S(2)}, u32[]{:S(2)}) collective-permute-start(f32[192,128]{1,0:T(8,128)} %get-tuple-element.16), channel_id=1, source_target_pairs={{0,2},{1,3},{2,4},{3,5},{4,6},{5,7},{6,8},{7,9},{8,10},{9,11},{10,... | collective-permute-start | bytes 294920 | tf_op jit(solution)/shard_map/ppermute | solution.py:586
  21.6 2.7 %collective-permute-start = (f32[192,128]{1,0:T(8,128)}, f32[192,128]{1,0:T(8,128)S(1)}, u32[]{:S(2)}, u32[]{:S(2)}) collective-permute-start(f32[192,128]{1,0:T(8,128)} %get-tuple-element.16), channel_id=1, source_target_pairs={{0,1},{1,2},{2,3},{3,4},{4,5},{5,6},{6,7},{7,8},{8,9},{9,10},{10,1... | collective-permute-start | bytes 294920 | tf_op jit(solution)/shard_map/ppermute | solution.py:586
  24.3 7.6 %all-to-all-start = ((f32[64,1,128]{2,1,0:T(1,128)}), f32[64,1,128]{2,1,0:T(1,128)S(1)}, u32[]{:S(2)}, u32[]{:S(2)}) async-start(f32[64,1,128]{2,1,0:T(1,128)} %get-tuple-element.21), calls=%async_computation | async-start | bytes 65536 | tf_op jit(solution)/shard_map/all_to_all | solution.py:590
  31.9 0.0 copy-start
  31.9 0.9 %copy-done = f32[456,128]{1,0:T(8,128)S(1)} copy-done((f32[456,128]{1,0:T(8,128)S(1)}, f32[456,128]{1,0:T(8,128)}, u32[]{:S(2)}) %copy-start) | copy-done | bytes 233496
  32.8 1.2 %shard_map.123 = (bf16[384,256]{1,0:T(8,128)(2,1)S(1)}, bf16[384,128]{1,0:T(8,128)(2,1)S(1)}, bf16[1152,128]{1,0:T(8,128)(2,1)S(1)}, f32[8,128]{1,0:T(8,128)S(1)}) custom-call(f32[456,128]{1,0:T(8,128)S(1)} %copy-done), custom_call_target="tpu_custom_call" | custom-call | tf_op jit(solution)/shard_map/pallas_call | solution.py:570
  34.0 7.1 %all-to-all-done.arrived_ref = f32[64,1,128]{2,1,0:T(1,128)S(1)} async-done(((f32[64,1,128]{2,1,0:T(1,128)}), f32[64,1,128]{2,1,0:T(1,128)S(1)}, u32[]{:S(2)}, u32[]{:S(2)}) %all-to-all-start) | async-done | bytes 32800 | tf_op jit(solution)/shard_map/all_to_all | solution.py:590
  41.1 0.0 copy-start.1
  41.1 0.9 %copy-done.1 = f32[456,128]{1,0:T(8,128)S(1)} copy-done((f32[456,128]{1,0:T(8,128)S(1)}, f32[456,128]{1,0:T(8,128)}, u32[]{:S(2)}) %copy-start.1) | copy-done | bytes 233496
  42.1 0.0 copy-start.2
  42.1 0.0 copy-start.3
  42.1 0.5 shard_map.124
  42.6 0.0 collective-permute-done.3.p2_ref
  42.7 0.0 collective-permute-done.2.p1_ref
  42.7 0.0 collective-permute-done.1.m2_ref
  42.7 0.0 collective-permute-done.m1_ref
  42.7 4.2 %shard_map.125 = (f32[4,192,128]{2,1,0:T(8,128)S(1)}, f32[32,1,512]{2,1,0:T(1,128)S(1)}) custom-call(f32[456,128]{1,0:T(8,128)S(1)} %copy-done.1, f32[192,128]{1,0:T(8,128)S(1)} %collective-permute-done.m1_ref, f32[192,128]{1,0:T(8,128)S(1)} %collective-permute-done.1.m2_ref, f32[192,128]{1,0:T(8,128)S(1)} %collective-permute-done.2.p1_ref, ...), custom_call_target="tpu_custom_call" | custom-call | tf_op jit(solution)/shard_map/pallas_call | solution.py:570
  46.9 11.8 %all_to_all.15.arrived_ref = f32[32,1,512]{2,1,0:T(1,128)S(1)} all-to-all(f32[32,1,512]{2,1,0:T(1,128)S(1)} %get-tuple-element.23), channel_id=1, replica_groups={{0,2,4,6,8,10,12,14,16,18,20,22,24,26,28,30,32,34,36,38,40,42,44,46,48,..., dimensions={0} | all-to-all | bytes 131072 | tf_op jit(solution)/shard_map/all_to_all | solution.py:590
  58.8 1.0 %shard_map.126 = f32[16,1,1152]{2,1,0:T(1,128)} custom-call(f32[32,1,512]{2,1,0:T(1,128)S(1)} %all_to_all.15.arrived_ref), custom_call_target="tpu_custom_call" | custom-call | tf_op jit(solution)/shard_map/pallas_call | solution.py:570
  59.8 9.0 %all-to-all-start.2 = ((f32[16,1,1152]{2,1,0:T(1,128)}), f32[16,1,1152]{2,1,0:T(1,128)S(1)}, u32[]{:S(2)}, u32[]{:S(2)}) async-start(f32[16,1,1152]{2,1,0:T(1,128)} %shard_map.126), calls=%async_computation.2 | async-start | bytes 147456 | tf_op jit(solution)/shard_map/all_to_all | solution.py:590
  68.7 0.6 shard_map.127.refs_5_
  69.4 7.3 %all-to-all-done.2.refs_0_ = f32[16,1,1152]{2,1,0:T(1,128)S(1)} async-done(((f32[16,1,1152]{2,1,0:T(1,128)}), f32[16,1,1152]{2,1,0:T(1,128)S(1)}, u32[]{:S(2)}, u32[]{:S(2)}) %all-to-all-start.2) | async-done | bytes 73760 | tf_op jit(solution)/shard_map/all_to_all | solution.py:590
  76.7 0.0 copy-done.2
  76.7 0.0 copy-done.3
  76.7 2.1 %shard_map.128 = (f32[6,64]{1,0:T(8,128)}, f32[3072,128]{1,0:T(8,128)}) custom-call(f32[16,1,1152]{2,1,0:T(1,128)S(1)} %all-to-all-done.2.refs_0_, f32[8,64]{1,0:T(8,128)S(1)} %get-tuple-element.24.refs_1_, s32[1,64]{1,0:T(1,128)S(1)} %bitcast.6, f32[6,6]{1,0:T(8,128)S(1)} %copy-done.2, f32[8,128]{1,0:T(8,128)S(1)} %get-tuple-element.20.basis_ref.refs_4_, ...), custom_call_target="tpu_custom_call" | custom-call | tf_op jit(solution)/shard_map/pallas_call | solution.py:570
Async XLA Ops:
  3.1 39.6 %collective-permute-start.3 = (f32[192,128]{1,0:T(8,128)}, f32[192,128]{1,0:T(8,128)S(1)}, u32[]{:S(2)}, u32[]{:S(2)}) collective-permute-start(f32[192,128]{1,0:T(8,128)} %get-tuple-element.16), channel_id=1, source_target_pairs={{0,62},{1,63},{2,0},{3,1},{4,2},{5,3},{6,4},{7,5},{8,6},{9,7},{10,... | collective-permute-start | bytes 294920 | tf_op jit(solution)/shard_map/ppermute | solution.py:586
  16.8 25.9 %collective-permute-start.2 = (f32[192,128]{1,0:T(8,128)}, f32[192,128]{1,0:T(8,128)S(1)}, u32[]{:S(2)}, u32[]{:S(2)}) collective-permute-start(f32[192,128]{1,0:T(8,128)} %get-tuple-element.16), channel_id=1, source_target_pairs={{0,63},{1,0},{2,1},{3,2},{4,3},{5,4},{6,5},{7,6},{8,7},{9,8},{10,9... | collective-permute-start | bytes 294920 | tf_op jit(solution)/shard_map/ppermute | solution.py:586
  19.6 23.0 %collective-permute-start.1 = (f32[192,128]{1,0:T(8,128)}, f32[192,128]{1,0:T(8,128)S(1)}, u32[]{:S(2)}, u32[]{:S(2)}) collective-permute-start(f32[192,128]{1,0:T(8,128)} %get-tuple-element.16), channel_id=1, source_target_pairs={{0,2},{1,3},{2,4},{3,5},{4,6},{5,7},{6,8},{7,9},{8,10},{9,11},{10,... | collective-permute-start | bytes 294920 | tf_op jit(solution)/shard_map/ppermute | solution.py:586
  21.6 21.1 %collective-permute-start = (f32[192,128]{1,0:T(8,128)}, f32[192,128]{1,0:T(8,128)S(1)}, u32[]{:S(2)}, u32[]{:S(2)}) collective-permute-start(f32[192,128]{1,0:T(8,128)} %get-tuple-element.16), channel_id=1, source_target_pairs={{0,1},{1,2},{2,3},{3,4},{4,5},{5,6},{6,7},{7,8},{8,9},{9,10},{10,1... | collective-permute-start | bytes 294920 | tf_op jit(solution)/shard_map/ppermute | solution.py:586
  24.3 16.9 %all-to-all-start = ((f32[64,1,128]{2,1,0:T(1,128)}), f32[64,1,128]{2,1,0:T(1,128)S(1)}, u32[]{:S(2)}, u32[]{:S(2)}) async-start(f32[64,1,128]{2,1,0:T(1,128)} %get-tuple-element.21), calls=%async_computation | async-start | bytes 65536 | tf_op jit(solution)/shard_map/all_to_all | solution.py:590
  31.9 0.9 %copy-start = (f32[456,128]{1,0:T(8,128)S(1)}, f32[456,128]{1,0:T(8,128)}, u32[]{:S(2)}) copy-start(f32[456,128]{1,0:T(8,128)} %get-tuple-element.15.rest_ref) | copy-start | bytes 700420
  41.1 0.9 %copy-start.1 = (f32[456,128]{1,0:T(8,128)S(1)}, f32[456,128]{1,0:T(8,128)}, u32[]{:S(2)}) copy-start(f32[456,128]{1,0:T(8,128)} %get-tuple-element.15.rest_ref) | copy-start | bytes 700420
  42.1 34.6 %copy-start.2 = (f32[6,6]{1,0:T(8,128)S(1)}, f32[6,6]{1,0:T(8,128)}, u32[]{:S(2)}) copy-start(f32[6,6]{1,0:T(8,128)} %refs_3_.1) | copy-start | bytes 436
  42.1 34.6 %copy-start.3 = (s32[64]{0:T(128)S(1)}, s32[64]{0:T(128)}, u32[]{:S(2)}) copy-start(s32[64]{0:T(128)} %param.15) | copy-start | bytes 772
  59.8 17.0 %all-to-all-start.2 = ((f32[16,1,1152]{2,1,0:T(1,128)}), f32[16,1,1152]{2,1,0:T(1,128)S(1)}, u32[]{:S(2)}, u32[]{:S(2)}) async-start(f32[16,1,1152]{2,1,0:T(1,128)} %shard_map.126), calls=%async_computation.2 | async-start | bytes 147456 | tf_op jit(solution)/shard_map/all_to_all | solution.py:590

commit v4 on v3

--- a/solution.py
+++ b/solution.py
@@ -167,7 +167,9 @@
     rest_ref[264:, :] = pack_ref[...]
 
 
-def tables(rest_ref, w1, wb, w2, basis_ref):
+def tables(rest_ref, w1, wb, w2, basis_ref, strain_part, own_part):
+    strain_part[...] = rest_ref[:184]
+    own_part[...] = rest_ref[264:]
     root, chain = rest_ref[184:248, :BLOCK], rest_ref[184:248, BLOCK:]
     bridge = rest_ref[248:264, :IFACE]
     zero = jnp.zeros((BLOCK, BLOCK), F32)
@@ -223,7 +225,7 @@
 
 
 def krylov_kernel(
-    rest_ref, m1_ref, m2_ref, p1_ref, p2_ref, w1, wb, w2, basis_ref, cand_ref, u_ref, send_ref
+    own_ref, m1_ref, m2_ref, p1_ref, p2_ref, w1, wb, w2, basis_ref, cand_ref, u_ref, send_ref
 ):
     centre = [basis_ref[n : n + 1, :] for n in range(3)]
     step = [basis_ref[n + 3 : n + 4, :] for n in range(3)]
@@ -236,9 +238,12 @@
         w = x.reshape(HALF, 8, LANES)[:, 6:7, :]
         return jnp.broadcast_to(w, (HALF, 8, LANES)).reshape(ROWS, LANES)
 
+    def parts(x):
+        high, low = split2(x)
+        return jnp.concatenate([high, low, high], axis=1)
+
     def stage(x, w):
-        high, low = split2(x)
-        return bdot(jnp.concatenate([high, low, high], axis=1), w[...])
+        return bdot(parts(x), w[...])
 
     def blocks(x):
         return [x[n : n + ROWS] for n in range(0, x.shape[0], ROWS)]
@@ -251,8 +256,8 @@
         parts = [p for v in blocks(x) for p in (v[ROWS - 8 :], v[: ROWS - 8])]
         return jnp.concatenate(parts, axis=0)
 
-    def halves(x, w):
-        both = stage(x, w1)
+    def halves(x, w, split):
+        both = bdot(split, w1[...])
         lifted = both[:, :LANES]
         mixed = both[:, LANES:]
         edge = x - jnp.where(lanes(x) < BLOCK, mixed, up(mixed))
@@ -261,34 +266,37 @@
     def face(x, following):
         return jnp.where(lanes(x) % BLOCK >= BLOCK - IFACE, x, 0.0) - following
 
-    def apply(x, w, f, f_before):
-        _, weighted, edge = halves(x, w)
+    def apply(x, w, split, f, f_before):
+        _, weighted, edge = halves(x, w, split)
         shifted = jnp.where(lanes(x) < BLOCK, edge, down(edge))
         left = jnp.concatenate([weighted, shifted, f_before], axis=1)
         return ridge * x + edge + f + stage(left, w2)
 
     zero = jnp.zeros((ROWS, LANES), F32)
-    near = [m1_ref[...], rest_ref[264:, :], p1_ref[...], p2_ref[...]]
+    near = [m1_ref[...], own_ref[...], p1_ref[...], p2_ref[...]]
     w = jnp.concatenate([weights_of(x) for x in near], axis=0)
 
     x0 = jnp.concatenate(near, axis=0)
     known = jnp.concatenate([m2_ref[...], x0[: 3 * ROWS]], axis=0)
-    f = jnp.concatenate([face(known, stage(x0, wb)), zero], axis=0)
-    image = apply(x0, w, f[ROWS:], f[: 4 * ROWS])
+    split = parts(x0)
+    f = jnp.concatenate([face(known, bdot(split, wb[...])), zero], axis=0)
+    image = apply(x0, w, split, f[ROWS:], f[: 4 * ROWS])
     x1 = inverse[0] * (image - centre[0] * x0)
 
-    f = jnp.concatenate([zero, face(x1[: 3 * ROWS], stage(x1[ROWS:], wb))], axis=0)
+    split = parts(x1)
+    f = jnp.concatenate([zero, face(x1[: 3 * ROWS], bdot(split[ROWS:], wb[...]))], axis=0)
     now, past = x1[: 3 * ROWS], x0[: 3 * ROWS]
-    image = apply(now, w[: 3 * ROWS], f[ROWS:], f[: 3 * ROWS])
+    image = apply(now, w[: 3 * ROWS], split[: 3 * ROWS], f[ROWS:], f[: 3 * ROWS])
     x2 = inverse[1] * (image - centre[1] * now - step[0] * past)
 
-    f = jnp.concatenate([face(x2[: 2 * ROWS], stage(x2[ROWS:], wb)), zero], axis=0)
+    split = parts(x2[ROWS:])
+    f = jnp.concatenate([face(x2[: 2 * ROWS], bdot(split, wb[...])), zero], axis=0)
     now, past = x2[ROWS:], x1[ROWS : 3 * ROWS]
-    image = apply(now, w[ROWS : 3 * ROWS], f[ROWS:], f[: 2 * ROWS])
+    image = apply(now, w[ROWS : 3 * ROWS], split, f[ROWS:], f[: 2 * ROWS])
     x3 = inverse[2] * (image - centre[2] * now - step[1] * past)
 
     own = x3[:ROWS]
-    lifted, weighted, edge = halves(own, w[ROWS : 2 * ROWS])
+    lifted, weighted, edge = halves(own, w[ROWS : 2 * ROWS], parts(own))
     f3 = face(own, stage(x3[ROWS:], wb))
 
     basis = [near[1], x1[ROWS : 2 * ROWS], x2[ROWS : 2 * ROWS], own]
@@ -557,7 +565,7 @@
         out_ref[rows, :] = bdot(u_ref[rows, :], right)
 
 
-def call(kernel, outs, *args, scratch=(), own_copies=0):
+def call(kernel, outs, *args, scratch=(), own_copies=0, cost=None):
     vmem = pl.BlockSpec(memory_space=pltpu.VMEM)
     many = isinstance(outs, list)
     out_specs = [vmem] * len(outs) if many else vmem
@@ -573,6 +581,7 @@
         in_specs=spaces[: len(args)],
         out_specs=out_specs,
         scratch_shapes=scratch,
+        cost_estimate=cost,
         compiler_params=pltpu.CompilerParams(vmem_limit_bytes=limit * 1024 * 1024),
     )(*args)
 
@@ -623,21 +632,29 @@
     )
     arrived = exchange(outgoing, "dev")
     near = [shifted(packed, 1), shifted(packed, 2), shifted(packed, -1), shifted(packed, -2)]
-    *weights, terms = call(
+    *weights, terms, strain_part, own_part = call(
         tables,
         [
             arr(3 * LANES, 2 * LANES, dtype=BF16),
             arr(3 * LANES, LANES, dtype=BF16),
             arr(9 * LANES, LANES, dtype=BF16),
             arr(8, LANES),
+            arr(184, LANES),
+            arr(ROWS, LANES),
         ],
         rest,
     )
-    cand, strain = call(strain_kernel, [arr(1, LANES), arr(8, points)], rest, arrived)
+    cand, strain = call(
+        strain_kernel,
+        [arr(1, LANES), arr(8, points)],
+        strain_part,
+        arrived,
+        cost=pl.CostEstimate(flops=2 * 10**10, bytes_accessed=0, transcendentals=0),
+    )
     vectors, send = call(
         krylov_kernel,
         [arr(4, ROWS, LANES), arr(devs // 2, 1, 4 * LANES)],
-        rest,
+        own_part,
         *near,
         *weights,
         terms,

time: 79.3 us -> 76.1 us (0.960)
  waiting for transfers between devices: 14.5 us -> 8.47 us
  blocking collectives: 11.8 us -> 15.2 us
  local copies, waits for them, and re-layouts: 1.88 us -> 0.97 us
    all_to_all x2, waiting for transfers between devices: 14.4 us -> 7.32 us  [exchange(): lax.all_to_all(x, axis, split_axis=0, concat_axis=0, tiled=True, axis_ind...]
    all_to_all x2, starting transfers between devices: 16.6 us -> 23.7 us  [exchange(): lax.all_to_all(x, axis, split_axis=0, concat_axis=0, tiled=True, axis_ind...]
    ppermute x4, starting transfers between devices: 21.2 us -> 14.4 us  [shifted(): lax.ppermute(x, 'dev', [(i, (i + by) % devices) for i in range(devices)])]
    all_to_all x1, blocking collectives: 11.8 us -> 15.2 us  [exchange(): lax.all_to_all(x, axis, split_axis=0, concat_axis=0, tiled=True, axis_ind...]
    ppermute x4, waiting for transfers between devices: 0.03 us -> 1.15 us  [shifted(): lax.ppermute(x, 'dev', [(i, (i + by) % devices) for i in range(devices)])]
    unnamed x8 -> x6, local copies, waits for them, and re-layouts: 1.88 us -> 0.97 us
where the time goes in v4:
time: 76.1 us; the launch traced here: 75.7 us
  starting transfers between devices  38.1 us (50%)
  blocking collectives  15.2 us (20%)
  Pallas kernels  12.2 us (16%)
  waiting for transfers between devices  8.47 us (11%)
  local copies, waits for them, and re-layouts  0.97 us (1%)
    all_to_all x2, starting transfers between devices, exchange(): lax.all_to_all(x, axis, split_axis=0, concat_axis=0, tiled=True, axis_ind...  23.7 us
    all_to_all x1, blocking collectives, exchange(): lax.all_to_all(x, axis, split_axis=0, concat_axis=0, tiled=True, axis_ind...  15.2 us
    ppermute x4, starting transfers between devices, shifted(): lax.ppermute(x, 'dev', [(i, (i + by) % devices) for i in range(devices)])  14.4 us
    pallas_call x7, Pallas kernels, call(): pl.pallas_call(kernel, out_shape=outs, in_specs=spaces[:len(args)], out_s...  12.2 us
    all_to_all x2, waiting for transfers between devices, exchange(): lax.all_to_all(x, axis, split_axis=0, concat_axis=0, tiled=True, axis_ind...  7.32 us
  transfers between devices with their start and end apart: 6, of which 2 were waited for; matrix products, arithmetic and copies ran while one was open for 0% of the time, Pallas kernels for 3%

profile of v4, /device:TPU:1, one launch (start us, length us, event | category | flops | bytes accessed | tf_op | source)
XLA Modules:
  0.0 75.7 jit_solution(2095121832703542088)
XLA Ops:
  0.6 2.4 %shard_map.122 = (f32[64,1,128]{2,1,0:T(1,128)}, f32[192,128]{1,0:T(8,128)}, f32[456,128]{1,0:T(8,128)}) custom-call(f32[3,256]{1,0:T(4,128)} %refs_0_.1, s32[1,16,64]{2,1,0:T(8,128)} %bitcast.9, f32[6,48,64]{2,1,0:T(8,128)} %bitcast.7, s32[1,48,64]{2,1,0:T(8,128)} %bitcast.8, s32[8,64]{1,0:T(8,128)} %refs_4_.1, f32[6,24,64]{2,1,0:T(8,128)} %refs_5_.1, ...), custom_call_target="tpu_custom_call" | custom-call | tf_op jit(solution)/shard_map/pallas_call | solution.py:578
  3.1 14.8 %all-to-all-start = ((f32[64,1,128]{2,1,0:T(1,128)}), f32[64,1,128]{2,1,0:T(1,128)S(1)}, u32[]{:S(2)}, u32[]{:S(2)}) async-start(f32[64,1,128]{2,1,0:T(1,128)} %get-tuple-element.25), calls=%async_computation | async-start | bytes 65536 | tf_op jit(solution)/shard_map/all_to_all | solution.py:599
  17.9 6.9 %collective-permute-start.3 = (f32[192,128]{1,0:T(8,128)}, f32[192,128]{1,0:T(8,128)S(1)}, u32[]{:S(2)}, u32[]{:S(2)}) collective-permute-start(f32[192,128]{1,0:T(8,128)} %get-tuple-element.19), channel_id=1, source_target_pairs={{0,62},{1,63},{2,0},{3,1},{4,2},{5,3},{6,4},{7,5},{8,6},{9,7},{10,... | collective-permute-start | bytes 294920 | tf_op jit(solution)/shard_map/ppermute | solution.py:595
  24.9 2.5 %collective-permute-start.2 = (f32[192,128]{1,0:T(8,128)}, f32[192,128]{1,0:T(8,128)S(1)}, u32[]{:S(2)}, u32[]{:S(2)}) collective-permute-start(f32[192,128]{1,0:T(8,128)} %get-tuple-element.19), channel_id=1, source_target_pairs={{0,63},{1,0},{2,1},{3,2},{4,3},{5,4},{6,5},{7,6},{8,7},{9,8},{10,9... | collective-permute-start | bytes 294920 | tf_op jit(solution)/shard_map/ppermute | solution.py:595
  27.4 1.9 %collective-permute-start.1 = (f32[192,128]{1,0:T(8,128)}, f32[192,128]{1,0:T(8,128)S(1)}, u32[]{:S(2)}, u32[]{:S(2)}) collective-permute-start(f32[192,128]{1,0:T(8,128)} %get-tuple-element.19), channel_id=1, source_target_pairs={{0,2},{1,3},{2,4},{3,5},{4,6},{5,7},{6,8},{7,9},{8,10},{9,11},{10,... | collective-permute-start | bytes 294920 | tf_op jit(solution)/shard_map/ppermute | solution.py:595
  29.3 3.0 %collective-permute-start = (f32[192,128]{1,0:T(8,128)}, f32[192,128]{1,0:T(8,128)S(1)}, u32[]{:S(2)}, u32[]{:S(2)}) collective-permute-start(f32[192,128]{1,0:T(8,128)} %get-tuple-element.19), channel_id=1, source_target_pairs={{0,1},{1,2},{2,3},{3,4},{4,5},{5,6},{6,7},{7,8},{8,9},{9,10},{10,1... | collective-permute-start | bytes 294920 | tf_op jit(solution)/shard_map/ppermute | solution.py:595
  32.4 0.0 copy-start
  32.4 0.9 %copy-done = f32[456,128]{1,0:T(8,128)S(1)} copy-done((f32[456,128]{1,0:T(8,128)S(1)}, f32[456,128]{1,0:T(8,128)}, u32[]{:S(2)}) %copy-start) | copy-done | bytes 233496
  33.3 1.2 %shard_map.123 = (bf16[384,256]{1,0:T(8,128)(2,1)S(1)}, bf16[384,128]{1,0:T(8,128)(2,1)S(1)}, bf16[1152,128]{1,0:T(8,128)(2,1)S(1)}, f32[8,128]{1,0:T(8,128)S(1)...) custom-call(f32[456,128]{1,0:T(8,128)S(1)} %copy-done), custom_call_target="tpu_custom_call" | custom-call | tf_op jit(solution)/shard_map/pallas_call | solution.py:578
  34.5 0.0 all-to-all-done.arrived_ref
  34.5 0.6 shard_map.124
  35.1 0.0 copy-start.1
  35.1 0.0 copy-start.2
  35.1 0.0 collective-permute-done.3.p2_ref
  35.1 0.0 collective-permute-done.2.p1_ref
  35.2 1.1 %collective-permute-done.1.m2_ref = f32[192,128]{1,0:T(8,128)S(1)} collective-permute-done((f32[192,128]{1,0:T(8,128)}, f32[192,128]{1,0:T(8,128)S(1)}, u32[]{:S(2)}, u32[]{:S(2)}) %collective-permute-start.1) | collective-permute-done | bytes 98336 | tf_op jit(solution)/shard_map/ppermute | solution.py:595
  36.3 0.0 collective-permute-done.m1_ref
  36.3 4.2 %shard_map.125 = (f32[4,192,128]{2,1,0:T(8,128)S(1)}, f32[32,1,512]{2,1,0:T(1,128)S(1)}) custom-call(f32[192,128]{1,0:T(8,128)S(1)} %get-tuple-element.18.own_ref, f32[192,128]{1,0:T(8,128)S(1)} %collective-permute-done.m1_ref, f32[192,128]{1,0:T(8,128)S(1)} %collective-permute-done.1.m2_ref, f32[192,128]{1,0:T(8,128)S(1)} %collective-permute-done.2.p1_ref, ...), custom_call_target="tpu_custom_call" | custom-call | tf_op jit(solution)/shard_map/pallas_call | solution.py:578
  40.6 15.2 %all_to_all.15.arrived_ref = f32[32,1,512]{2,1,0:T(1,128)S(1)} all-to-all(f32[32,1,512]{2,1,0:T(1,128)S(1)} %get-tuple-element.27), channel_id=1, replica_groups={{0,2,4,6,8,10,12,14,16,18,20,22,24,26,28,30,32,34,36,38,40,42,44,46,48,..., dimensions={0} | all-to-all | bytes 131072 | tf_op jit(solution)/shard_map/all_to_all | solution.py:599
  55.8 1.0 %shard_map.126 = f32[16,1,1152]{2,1,0:T(1,128)} custom-call(f32[32,1,512]{2,1,0:T(1,128)S(1)} %all_to_all.15.arrived_ref), custom_call_target="tpu_custom_call" | custom-call | tf_op jit(solution)/shard_map/pallas_call | solution.py:578
  56.8 8.8 %all-to-all-start.2 = ((f32[16,1,1152]{2,1,0:T(1,128)}), f32[16,1,1152]{2,1,0:T(1,128)S(1)}, u32[]{:S(2)}, u32[]{:S(2)}) async-start(f32[16,1,1152]{2,1,0:T(1,128)} %shard_map.126), calls=%async_computation.2 | async-start | bytes 147456 | tf_op jit(solution)/shard_map/all_to_all | solution.py:599
  65.6 0.6 shard_map.127.refs_5_
  66.3 7.3 %all-to-all-done.2.refs_0_ = f32[16,1,1152]{2,1,0:T(1,128)S(1)} async-done(((f32[16,1,1152]{2,1,0:T(1,128)}), f32[16,1,1152]{2,1,0:T(1,128)S(1)}, u32[]{:S(2)}, u32[]{:S(2)}) %all-to-all-start.2) | async-done | bytes 73760 | tf_op jit(solution)/shard_map/all_to_all | solution.py:599
  73.6 0.0 copy-done.1
  73.6 0.0 copy-done.2
  73.6 2.1 %shard_map.128 = (f32[6,64]{1,0:T(8,128)}, f32[3072,128]{1,0:T(8,128)}) custom-call(f32[16,1,1152]{2,1,0:T(1,128)S(1)} %all-to-all-done.2.refs_0_, f32[8,64]{1,0:T(8,128)S(1)} %get-tuple-element.28.refs_1_, s32[1,64]{1,0:T(1,128)S(1)} %bitcast.6, f32[6,6]{1,0:T(8,128)S(1)} %copy-done.1, f32[8,128]{1,0:T(8,128)S(1)} %get-tuple-element.23.basis_ref.refs_4_, ...), custom_call_target="tpu_custom_call" | custom-call | tf_op jit(solution)/shard_map/pallas_call | solution.py:578
Async XLA Ops:
  3.1 31.5 %all-to-all-start = ((f32[64,1,128]{2,1,0:T(1,128)}), f32[64,1,128]{2,1,0:T(1,128)S(1)}, u32[]{:S(2)}, u32[]{:S(2)}) async-start(f32[64,1,128]{2,1,0:T(1,128)} %get-tuple-element.25), calls=%async_computation | async-start | bytes 65536 | tf_op jit(solution)/shard_map/all_to_all | solution.py:599
  17.9 17.2 %collective-permute-start.3 = (f32[192,128]{1,0:T(8,128)}, f32[192,128]{1,0:T(8,128)S(1)}, u32[]{:S(2)}, u32[]{:S(2)}) collective-permute-start(f32[192,128]{1,0:T(8,128)} %get-tuple-element.19), channel_id=1, source_target_pairs={{0,62},{1,63},{2,0},{3,1},{4,2},{5,3},{6,4},{7,5},{8,6},{9,7},{10,... | collective-permute-start | bytes 294920 | tf_op jit(solution)/shard_map/ppermute | solution.py:595
  24.9 10.3 %collective-permute-start.2 = (f32[192,128]{1,0:T(8,128)}, f32[192,128]{1,0:T(8,128)S(1)}, u32[]{:S(2)}, u32[]{:S(2)}) collective-permute-start(f32[192,128]{1,0:T(8,128)} %get-tuple-element.19), channel_id=1, source_target_pairs={{0,63},{1,0},{2,1},{3,2},{4,3},{5,4},{6,5},{7,6},{8,7},{9,8},{10,9... | collective-permute-start | bytes 294920 | tf_op jit(solution)/shard_map/ppermute | solution.py:595
  27.4 8.9 %collective-permute-start.1 = (f32[192,128]{1,0:T(8,128)}, f32[192,128]{1,0:T(8,128)S(1)}, u32[]{:S(2)}, u32[]{:S(2)}) collective-permute-start(f32[192,128]{1,0:T(8,128)} %get-tuple-element.19), channel_id=1, source_target_pairs={{0,2},{1,3},{2,4},{3,5},{4,6},{5,7},{6,8},{7,9},{8,10},{9,11},{10,... | collective-permute-start | bytes 294920 | tf_op jit(solution)/shard_map/ppermute | solution.py:595
  29.3 7.0 %collective-permute-start = (f32[192,128]{1,0:T(8,128)}, f32[192,128]{1,0:T(8,128)S(1)}, u32[]{:S(2)}, u32[]{:S(2)}) collective-permute-start(f32[192,128]{1,0:T(8,128)} %get-tuple-element.19), channel_id=1, source_target_pairs={{0,1},{1,2},{2,3},{3,4},{4,5},{5,6},{6,7},{7,8},{8,9},{9,10},{10,1... | collective-permute-start | bytes 294920 | tf_op jit(solution)/shard_map/ppermute | solution.py:595
  32.4 0.9 %copy-start = (f32[456,128]{1,0:T(8,128)S(1)}, f32[456,128]{1,0:T(8,128)}, u32[]{:S(2)}) copy-start(f32[456,128]{1,0:T(8,128)} %get-tuple-element.17.rest_ref) | copy-start | bytes 700420
  35.1 38.5 %copy-start.1 = (f32[6,6]{1,0:T(8,128)S(1)}, f32[6,6]{1,0:T(8,128)}, u32[]{:S(2)}) copy-start(f32[6,6]{1,0:T(8,128)} %refs_3_.1) | copy-start | bytes 436
  35.1 38.5 %copy-start.2 = (s32[64]{0:T(128)S(1)}, s32[64]{0:T(128)}, u32[]{:S(2)}) copy-start(s32[64]{0:T(128)} %param.15) | copy-start | bytes 772
  56.8 16.8 %all-to-all-start.2 = ((f32[16,1,1152]{2,1,0:T(1,128)}), f32[16,1,1152]{2,1,0:T(1,128)S(1)}, u32[]{:S(2)}, u32[]{:S(2)}) async-start(f32[16,1,1152]{2,1,0:T(1,128)} %shard_map.126), calls=%async_computation.2 | async-start | bytes 147456 | tf_op jit(solution)/shard_map/all_to_all | solution.py:599

commit v5 on v4

--- a/solution.py
+++ b/solution.py
@@ -127,6 +127,29 @@
         copy.wait()
 
 
+QUARTER = ROWS // 4
+
+
+def edge_rows(x):
+    lane = iota((QUARTER, LANES), 1) // IFACE
+    out = jnp.zeros((QUARTER, LANES), F32)
+    for q in range(4):
+        rows = x[QUARTER * q : QUARTER * (q + 1)]
+        out = jnp.where(lane == 2 * q, pltpu.roll(rows, (32 * q - 48) % LANES, 1), out)
+        out = jnp.where(lane == 2 * q + 1, pltpu.roll(rows, (32 * q - 96) % LANES, 1), out)
+    return out
+
+
+def spread_edge(x):
+    lane = iota((QUARTER, LANES), 1) // IFACE
+    out = []
+    for q in range(4):
+        first = pltpu.roll(x, (48 - 32 * q) % LANES, 1)
+        second = pltpu.roll(x, (96 - 32 * q) % LANES, 1)
+        out.append(jnp.where(lane == 3, first, jnp.where(lane == 7, second, 0.0)))
+    return jnp.concatenate(out, axis=0)
+
+
 def own_nodes(disp, conn):
     nodes, points = disp.shape[1], conn.shape[1]
     index = side_by_side(conn[...])
@@ -148,11 +171,12 @@
 
 
 def first_kernel(*refs):
-    face_ref, pack_ref, rest_ref, *held, sems = refs[10:]
+    face_ref, pack_ref, edge_ref, rest_ref, *held, sems = refs[10:]
     fetch(refs[:10], held, sems)
     disp, listed, load, phase, conn, maps, assign, root, chain, bridge = held
     faces(disp, listed, face_ref)
     pack(load, phase, pack_ref)
+    edge_ref[...] = edge_rows(pack_ref[...])
     points = conn.shape[1]
     blank = jnp.zeros((7, points), F32)
     for c in range(6):
@@ -277,7 +301,7 @@
     w = jnp.concatenate([weights_of(x) for x in near], axis=0)
 
     x0 = jnp.concatenate(near, axis=0)
-    known = jnp.concatenate([m2_ref[...], x0[: 3 * ROWS]], axis=0)
+    known = jnp.concatenate([spread_edge(m2_ref[...]), x0[: 3 * ROWS]], axis=0)
     split = parts(x0)
     f = jnp.concatenate([face(known, bdot(split, wb[...])), zero], axis=0)
     image = apply(x0, w, split, f[ROWS:], f[: 4 * ROWS])
@@ -624,14 +648,14 @@
     labels = jnp.transpose(phases, (0, 2, 1))
     sources = [displacement, listed, load, labels, connectivity, strain_map, assign]
     sources += [stiff_root, chain_map, bridge_map]
-    outgoing, packed, rest = call(
+    outgoing, packed, edge, rest = call(
         first_kernel,
-        [arr(devs, 1, LANES), arr(ROWS, LANES), arr(264 + ROWS, LANES)],
+        [arr(devs, 1, LANES), arr(ROWS, LANES), arr(QUARTER, LANES), arr(264 + ROWS, LANES)],
         *sources,
         own_copies=len(sources),
     )
     arrived = exchange(outgoing, "dev")
-    near = [shifted(packed, 1), shifted(packed, 2), shifted(packed, -1), shifted(packed, -2)]
+    near = [shifted(packed, 1), shifted(edge, 2), shifted(packed, -1), shifted(packed, -2)]
     *weights, terms, strain_part, own_part = call(
         tables,
         [

time: 76.1 us -> 75.4 us (level)
  blocking collectives: 15.2 us -> 12.6 us
  waiting for transfers between devices: 8.47 us -> 10.7 us
    all_to_all x1, blocking collectives: 15.2 us -> 12.6 us  [exchange(): lax.all_to_all(x, axis, split_axis=0, concat_axis=0, tiled=True, axis_ind...]
    ppermute x4, waiting for transfers between devices: 1.15 us -> 3.4 us  [shifted(): lax.ppermute(x, 'dev', [(i, (i + by) % devices) for i in range(devices)])]
where the time goes in v5:
time: 75.4 us; the launch traced here: 75 us
  starting transfers between devices  37.7 us (50%)
  blocking collectives  12.6 us (17%)
  Pallas kernels  12.2 us (16%)
  waiting for transfers between devices  10.7 us (14%)
  local copies, waits for them, and re-layouts  0.97 us (1%)
    all_to_all x2, starting transfers between devices, exchange(): lax.all_to_all(x, axis, split_axis=0, concat_axis=0, tiled=True, axis_ind...  23.3 us
    ppermute x4, starting transfers between devices, shifted(): lax.ppermute(x, 'dev', [(i, (i + by) % devices) for i in range(devices)])  14.4 us
    all_to_all x1, blocking collectives, exchange(): lax.all_to_all(x, axis, split_axis=0, concat_axis=0, tiled=True, axis_ind...  12.6 us
    pallas_call x7, Pallas kernels, call(): pl.pallas_call(kernel, out_shape=outs, in_specs=spaces[:len(args)], out_s...  12.2 us
    all_to_all x2, waiting for transfers between devices, exchange(): lax.all_to_all(x, axis, split_axis=0, concat_axis=0, tiled=True, axis_ind...  7.32 us
    ppermute x4, waiting for transfers between devices, shifted(): lax.ppermute(x, 'dev', [(i, (i + by) % devices) for i in range(devices)])  3.4 us
  transfers between devices with their start and end apart: 6, of which 2 were waited for; matrix products, arithmetic and copies ran while one was open for 0% of the time, Pallas kernels for 3%

profile of v5, /device:TPU:1, one launch (start us, length us, event | category | flops | bytes accessed | tf_op | source)
XLA Modules:
  0.0 75.0 jit_solution(16997449628349359107)
XLA Ops:
  0.6 2.4 %shard_map.122 = (f32[64,1,128]{2,1,0:T(1,128)}, f32[192,128]{1,0:T(8,128)}, f32[48,128]{1,0:T(8,128)}, f32[456,128]{1,0:T(8,128)}) custom-call(f32[3,256]{1,0:T(4,128)} %refs_0_.1, s32[1,16,64]{2,1,0:T(8,128)} %bitcast.9, f32[6,48,64]{2,1,0:T(8,128)} %bitcast.7, s32[1,48,64]{2,1,0:T(8,128)} %bitcast.8, s32[8,64]{1,0:T(8,128)} %refs_4_.1, ...), custom_call_target="tpu_custom_call" | custom-call | tf_op jit(solution)/shard_map/pallas_call | solution.py:602
  3.1 14.8 %all-to-all-start = ((f32[64,1,128]{2,1,0:T(1,128)}), f32[64,1,128]{2,1,0:T(1,128)S(1)}, u32[]{:S(2)}, u32[]{:S(2)}) async-start(f32[64,1,128]{2,1,0:T(1,128)} %get-tuple-element.27), calls=%async_computation | async-start | bytes 65536 | tf_op jit(solution)/shard_map/all_to_all | solution.py:623
  17.9 6.9 %collective-permute-start.3 = (f32[192,128]{1,0:T(8,128)}, f32[192,128]{1,0:T(8,128)S(1)}, u32[]{:S(2)}, u32[]{:S(2)}) collective-permute-start(f32[192,128]{1,0:T(8,128)} %get-tuple-element.20), channel_id=1, source_target_pairs={{0,62},{1,63},{2,0},{3,1},{4,2},{5,3},{6,4},{7,5},{8,6},{9,7},{10,... | collective-permute-start | bytes 294920 | tf_op jit(solution)/shard_map/ppermute | solution.py:619
  24.8 2.5 %collective-permute-start.2 = (f32[192,128]{1,0:T(8,128)}, f32[192,128]{1,0:T(8,128)S(1)}, u32[]{:S(2)}, u32[]{:S(2)}) collective-permute-start(f32[192,128]{1,0:T(8,128)} %get-tuple-element.20), channel_id=1, source_target_pairs={{0,63},{1,0},{2,1},{3,2},{4,3},{5,4},{6,5},{7,6},{8,7},{9,8},{10,9... | collective-permute-start | bytes 294920 | tf_op jit(solution)/shard_map/ppermute | solution.py:619
  27.4 3.0 %collective-permute-start = (f32[192,128]{1,0:T(8,128)}, f32[192,128]{1,0:T(8,128)S(1)}, u32[]{:S(2)}, u32[]{:S(2)}) collective-permute-start(f32[192,128]{1,0:T(8,128)} %get-tuple-element.20), channel_id=1, source_target_pairs={{0,1},{1,2},{2,3},{3,4},{4,5},{5,6},{6,7},{7,8},{8,9},{9,10},{10,1... | collective-permute-start | bytes 294920 | tf_op jit(solution)/shard_map/ppermute | solution.py:619
  30.4 1.9 %collective-permute-start.1 = (f32[48,128]{1,0:T(8,128)}, f32[48,128]{1,0:T(8,128)S(1)}, u32[]{:S(2)}, u32[]{:S(2)}) collective-permute-start(f32[48,128]{1,0:T(8,128)} %get-tuple-element.21), channel_id=1, source_target_pairs={{0,2},{1,3},{2,4},{3,5},{4,6},{5,7},{6,8},{7,9},{8,10},{9,11},{10,... | collective-permute-start | bytes 73736 | tf_op jit(solution)/shard_map/ppermute | solution.py:619
  32.3 0.0 copy-start
  32.4 0.9 %copy-done = f32[456,128]{1,0:T(8,128)S(1)} copy-done((f32[456,128]{1,0:T(8,128)S(1)}, f32[456,128]{1,0:T(8,128)}, u32[]{:S(2)}) %copy-start) | copy-done | bytes 233496
  33.3 1.2 %shard_map.123 = (bf16[384,256]{1,0:T(8,128)(2,1)S(1)}, bf16[384,128]{1,0:T(8,128)(2,1)S(1)}, bf16[1152,128]{1,0:T(8,128)(2,1)S(1)}, f32[8,128]{1,0:T(8,128)S(1)...) custom-call(f32[456,128]{1,0:T(8,128)S(1)} %copy-done), custom_call_target="tpu_custom_call" | custom-call | tf_op jit(solution)/shard_map/pallas_call | solution.py:602
  34.5 0.0 all-to-all-done.arrived_ref
  34.5 0.6 shard_map.124
  35.1 0.0 copy-start.1
  35.1 0.0 copy-start.2
  35.1 3.4 %collective-permute-done.1.m2_ref = f32[48,128]{1,0:T(8,128)S(1)} collective-permute-done((f32[48,128]{1,0:T(8,128)}, f32[48,128]{1,0:T(8,128)S(1)}, u32[]{:S(2)}, u32[]{:S(2)}) %collective-permute-start.1) | collective-permute-done | bytes 24608 | tf_op jit(solution)/shard_map/ppermute | solution.py:619
  38.5 0.0 collective-permute-done.3.p2_ref
  38.5 0.0 collective-permute-done.2.p1_ref
  38.5 0.0 collective-permute-done.m1_ref
  38.5 4.2 %shard_map.125 = (f32[4,192,128]{2,1,0:T(8,128)S(1)}, f32[32,1,512]{2,1,0:T(1,128)S(1)}) custom-call(f32[192,128]{1,0:T(8,128)S(1)} %get-tuple-element.19.own_ref, f32[192,128]{1,0:T(8,128)S(1)} %collective-permute-done.m1_ref, f32[48,128]{1,0:T(8,128)S(1)} %collective-permute-done.1.m2_ref, f32[192,128]{1,0:T(8,128)S(1)} %collective-permute-done.2.p1_ref, ...), custom_call_target="tpu_custom_call" | custom-call | tf_op jit(solution)/shard_map/pallas_call | solution.py:602
  42.8 12.6 %all_to_all.15.arrived_ref = f32[32,1,512]{2,1,0:T(1,128)S(1)} all-to-all(f32[32,1,512]{2,1,0:T(1,128)S(1)} %get-tuple-element.29), channel_id=1, replica_groups={{0,2,4,6,8,10,12,14,16,18,20,22,24,26,28,30,32,34,36,38,40,42,44,46,48,..., dimensions={0} | all-to-all | bytes 131072 | tf_op jit(solution)/shard_map/all_to_all | solution.py:623
  55.4 1.0 %shard_map.126 = f32[16,1,1152]{2,1,0:T(1,128)} custom-call(f32[32,1,512]{2,1,0:T(1,128)S(1)} %all_to_all.15.arrived_ref), custom_call_target="tpu_custom_call" | custom-call | tf_op jit(solution)/shard_map/pallas_call | solution.py:602
  56.4 8.5 %all-to-all-start.2 = ((f32[16,1,1152]{2,1,0:T(1,128)}), f32[16,1,1152]{2,1,0:T(1,128)S(1)}, u32[]{:S(2)}, u32[]{:S(2)}) async-start(f32[16,1,1152]{2,1,0:T(1,128)} %shard_map.126), calls=%async_computation.2 | async-start | bytes 147456 | tf_op jit(solution)/shard_map/all_to_all | solution.py:623
  64.9 0.7 shard_map.127.refs_5_
  65.6 7.3 %all-to-all-done.2.refs_0_ = f32[16,1,1152]{2,1,0:T(1,128)S(1)} async-done(((f32[16,1,1152]{2,1,0:T(1,128)}), f32[16,1,1152]{2,1,0:T(1,128)S(1)}, u32[]{:S(2)}, u32[]{:S(2)}) %all-to-all-start.2) | async-done | bytes 73760 | tf_op jit(solution)/shard_map/all_to_all | solution.py:623
  72.9 0.0 copy-done.1
  72.9 0.0 copy-done.2
  72.9 2.1 %shard_map.128 = (f32[6,64]{1,0:T(8,128)}, f32[3072,128]{1,0:T(8,128)}) custom-call(f32[16,1,1152]{2,1,0:T(1,128)S(1)} %all-to-all-done.2.refs_0_, f32[8,64]{1,0:T(8,128)S(1)} %get-tuple-element.30.refs_1_, s32[1,64]{1,0:T(1,128)S(1)} %bitcast.6, f32[6,6]{1,0:T(8,128)S(1)} %copy-done.1, f32[8,128]{1,0:T(8,128)S(1)} %get-tuple-element.25.basis_ref.refs_4_, ...), custom_call_target="tpu_custom_call" | custom-call | tf_op jit(solution)/shard_map/pallas_call | solution.py:602
Async XLA Ops:
  3.1 31.5 %all-to-all-start = ((f32[64,1,128]{2,1,0:T(1,128)}), f32[64,1,128]{2,1,0:T(1,128)S(1)}, u32[]{:S(2)}, u32[]{:S(2)}) async-start(f32[64,1,128]{2,1,0:T(1,128)} %get-tuple-element.27), calls=%async_computation | async-start | bytes 65536 | tf_op jit(solution)/shard_map/all_to_all | solution.py:623
  17.9 20.6 %collective-permute-start.3 = (f32[192,128]{1,0:T(8,128)}, f32[192,128]{1,0:T(8,128)S(1)}, u32[]{:S(2)}, u32[]{:S(2)}) collective-permute-start(f32[192,128]{1,0:T(8,128)} %get-tuple-element.20), channel_id=1, source_target_pairs={{0,62},{1,63},{2,0},{3,1},{4,2},{5,3},{6,4},{7,5},{8,6},{9,7},{10,... | collective-permute-start | bytes 294920 | tf_op jit(solution)/shard_map/ppermute | solution.py:619
  24.8 13.7 %collective-permute-start.2 = (f32[192,128]{1,0:T(8,128)}, f32[192,128]{1,0:T(8,128)S(1)}, u32[]{:S(2)}, u32[]{:S(2)}) collective-permute-start(f32[192,128]{1,0:T(8,128)} %get-tuple-element.20), channel_id=1, source_target_pairs={{0,63},{1,0},{2,1},{3,2},{4,3},{5,4},{6,5},{7,6},{8,7},{9,8},{10,9... | collective-permute-start | bytes 294920 | tf_op jit(solution)/shard_map/ppermute | solution.py:619
  27.4 11.1 %collective-permute-start = (f32[192,128]{1,0:T(8,128)}, f32[192,128]{1,0:T(8,128)S(1)}, u32[]{:S(2)}, u32[]{:S(2)}) collective-permute-start(f32[192,128]{1,0:T(8,128)} %get-tuple-element.20), channel_id=1, source_target_pairs={{0,1},{1,2},{2,3},{3,4},{4,5},{5,6},{6,7},{7,8},{8,9},{9,10},{10,1... | collective-permute-start | bytes 294920 | tf_op jit(solution)/shard_map/ppermute | solution.py:619
  30.4 8.1 %collective-permute-start.1 = (f32[48,128]{1,0:T(8,128)}, f32[48,128]{1,0:T(8,128)S(1)}, u32[]{:S(2)}, u32[]{:S(2)}) collective-permute-start(f32[48,128]{1,0:T(8,128)} %get-tuple-element.21), channel_id=1, source_target_pairs={{0,2},{1,3},{2,4},{3,5},{4,6},{5,7},{6,8},{7,9},{8,10},{9,11},{10,... | collective-permute-start | bytes 73736 | tf_op jit(solution)/shard_map/ppermute | solution.py:619
  32.3 0.9 %copy-start = (f32[456,128]{1,0:T(8,128)S(1)}, f32[456,128]{1,0:T(8,128)}, u32[]{:S(2)}) copy-start(f32[456,128]{1,0:T(8,128)} %get-tuple-element.18.rest_ref) | copy-start | bytes 700420
  35.1 37.8 %copy-start.1 = (f32[6,6]{1,0:T(8,128)S(1)}, f32[6,6]{1,0:T(8,128)}, u32[]{:S(2)}) copy-start(f32[6,6]{1,0:T(8,128)} %refs_3_.1) | copy-start | bytes 436
  35.1 37.8 %copy-start.2 = (s32[64]{0:T(128)S(1)}, s32[64]{0:T(128)}, u32[]{:S(2)}) copy-start(s32[64]{0:T(128)} %param.15) | copy-start | bytes 772
  56.4 16.5 %all-to-all-start.2 = ((f32[16,1,1152]{2,1,0:T(1,128)}), f32[16,1,1152]{2,1,0:T(1,128)S(1)}, u32[]{:S(2)}, u32[]{:S(2)}) async-start(f32[16,1,1152]{2,1,0:T(1,128)} %shard_map.126), calls=%async_computation.2 | async-start | bytes 147456 | tf_op jit(solution)/shard_map/all_to_all | solution.py:623

commit v6 on v5

--- a/solution.py
+++ b/solution.py
@@ -123,8 +123,7 @@
     ]
     for copy in copies:
         copy.start()
-    for copy in copies:
-        copy.wait()
+    return copies
 
 
 QUARTER = ROWS // 4
@@ -172,9 +171,13 @@
 
 def first_kernel(*refs):
     face_ref, pack_ref, edge_ref, rest_ref, *held, sems = refs[10:]
-    fetch(refs[:10], held, sems)
+    copies = fetch(refs[:10], held, sems)
     disp, listed, load, phase, conn, maps, assign, root, chain, bridge = held
+    for copy in copies[:2]:
+        copy.wait()
     faces(disp, listed, face_ref)
+    for copy in copies[2:]:
+        copy.wait()
     pack(load, phase, pack_ref)
     edge_ref[...] = edge_rows(pack_ref[...])
     points = conn.shape[1]
@@ -410,7 +413,8 @@
     cand_ref[...] = line
 
 
-def section_kernel(arrived_ref, send_ref):
+def section_kernel(arrived_ref, turned_ref, send_ref):
+    del turned_ref
     devs = arrived_ref.shape[0]
     groups = send_ref.shape[0] // 2
     total = jnp.sum(arrived_ref[:, 0, : 3 * LANES], axis=0, keepdims=True)
@@ -696,7 +700,7 @@
         vectors,
         scratch=[pltpu.VMEM((BLOCK * BLOCKS, LANES), F32)],
     )
-    across = call(section_kernel, arr(2 * groups, 1, 9 * LANES), section)
+    across = call(section_kernel, arr(2 * groups, 1, 9 * LANES), section, turned)
     gathered = exchange(across, ("group", "dev"), same_chip)
     scale = math.sqrt(BLOCK * devs * BLOCKS)
     stress, fluctuation = call(

time: 75.4 us -> 76.1 us (level)
  starting transfers between devices: 37.7 us -> 33.2 us
  blocking collectives: 12.6 us -> 16.9 us
  waiting for transfers between devices: 10.7 us -> 11.6 us
    all_to_all x2, starting transfers between devices: 23.3 us -> 18.8 us  [exchange(): lax.all_to_all(x, axis, split_axis=0, concat_axis=0, tiled=True, axis_ind...]
    all_to_all x1, blocking collectives: 12.6 us -> 16.9 us  [exchange(): lax.all_to_all(x, axis, split_axis=0, concat_axis=0, tiled=True, axis_ind...]
    all_to_all x2, waiting for transfers between devices: 7.32 us -> 8.2 us  [exchange(): lax.all_to_all(x, axis, split_axis=0, concat_axis=0, tiled=True, axis_ind...]
where the time goes in v6:
time: 76.1 us; the launch traced here: 75.7 us
  starting transfers between devices  33.2 us (44%)
  blocking collectives  16.9 us (22%)
  Pallas kernels  12.2 us (16%)
  waiting for transfers between devices  11.6 us (15%)
  local copies, waits for them, and re-layouts  0.95 us (1%)
    all_to_all x2, starting transfers between devices, exchange(): lax.all_to_all(x, axis, split_axis=0, concat_axis=0, tiled=True, axis_ind...  18.8 us
    all_to_all x1, blocking collectives, exchange(): lax.all_to_all(x, axis, split_axis=0, concat_axis=0, tiled=True, axis_ind...  16.9 us
    ppermute x4, starting transfers between devices, shifted(): lax.ppermute(x, 'dev', [(i, (i + by) % devices) for i in range(devices)])  14.4 us
    pallas_call x7, Pallas kernels, call(): pl.pallas_call(kernel, out_shape=outs, in_specs=spaces[:len(args)], out_s...  12.2 us
    all_to_all x2, waiting for transfers between devices, exchange(): lax.all_to_all(x, axis, split_axis=0, concat_axis=0, tiled=True, axis_ind...  8.2 us
    ppermute x4, waiting for transfers between devices, shifted(): lax.ppermute(x, 'dev', [(i, (i + by) % devices) for i in range(devices)])  3.44 us
  transfers between devices with their start and end apart: 6, of which 2 were waited for; matrix products, arithmetic and copies ran while one was open for 0% of the time, Pallas kernels for 3%

profile of v6, /device:TPU:1, one launch (start us, length us, event | category | flops | bytes accessed | tf_op | source)
XLA Modules:
  0.0 75.7 jit_solution(394056000228809031)
XLA Ops:
  0.6 2.4 %shard_map.122 = (f32[64,1,128]{2,1,0:T(1,128)}, f32[192,128]{1,0:T(8,128)}, f32[48,128]{1,0:T(8,128)}, f32[456,128]{1,0:T(8,128)}) custom-call(f32[3,256]{1,0:T(4,128)} %refs_0_.1, s32[1,16,64]{2,1,0:T(8,128)} %bitcast.9, f32[6,48,64]{2,1,0:T(8,128)} %bitcast.7, s32[1,48,64]{2,1,0:T(8,128)} %bitcast.8, s32[8,64]{1,0:T(8,128)} %refs_4_.1, ...), custom_call_target="tpu_custom_call" | custom-call | tf_op jit(solution)/shard_map/pallas_call | solution.py:606
  3.1 14.8 %all-to-all-start = ((f32[64,1,128]{2,1,0:T(1,128)}), f32[64,1,128]{2,1,0:T(1,128)S(1)}, u32[]{:S(2)}, u32[]{:S(2)}) async-start(f32[64,1,128]{2,1,0:T(1,128)} %get-tuple-element.27), calls=%async_computation | async-start | bytes 65536 | tf_op jit(solution)/shard_map/all_to_all | solution.py:627
  17.9 6.9 %collective-permute-start.3 = (f32[192,128]{1,0:T(8,128)}, f32[192,128]{1,0:T(8,128)S(1)}, u32[]{:S(2)}, u32[]{:S(2)}) collective-permute-start(f32[192,128]{1,0:T(8,128)} %get-tuple-element.20), channel_id=1, source_target_pairs={{0,62},{1,63},{2,0},{3,1},{4,2},{5,3},{6,4},{7,5},{8,6},{9,7},{10,... | collective-permute-start | bytes 294920 | tf_op jit(solution)/shard_map/ppermute | solution.py:623
  24.9 2.5 %collective-permute-start.2 = (f32[192,128]{1,0:T(8,128)}, f32[192,128]{1,0:T(8,128)S(1)}, u32[]{:S(2)}, u32[]{:S(2)}) collective-permute-start(f32[192,128]{1,0:T(8,128)} %get-tuple-element.20), channel_id=1, source_target_pairs={{0,63},{1,0},{2,1},{3,2},{4,3},{5,4},{6,5},{7,6},{8,7},{9,8},{10,9... | collective-permute-start | bytes 294920 | tf_op jit(solution)/shard_map/ppermute | solution.py:623
  27.4 3.0 %collective-permute-start = (f32[192,128]{1,0:T(8,128)}, f32[192,128]{1,0:T(8,128)S(1)}, u32[]{:S(2)}, u32[]{:S(2)}) collective-permute-start(f32[192,128]{1,0:T(8,128)} %get-tuple-element.20), channel_id=1, source_target_pairs={{0,1},{1,2},{2,3},{3,4},{4,5},{5,6},{6,7},{7,8},{8,9},{9,10},{10,1... | collective-permute-start | bytes 294920 | tf_op jit(solution)/shard_map/ppermute | solution.py:623
  30.4 1.9 %collective-permute-start.1 = (f32[48,128]{1,0:T(8,128)}, f32[48,128]{1,0:T(8,128)S(1)}, u32[]{:S(2)}, u32[]{:S(2)}) collective-permute-start(f32[48,128]{1,0:T(8,128)} %get-tuple-element.21), channel_id=1, source_target_pairs={{0,2},{1,3},{2,4},{3,5},{4,6},{5,7},{6,8},{7,9},{8,10},{9,11},{10,... | collective-permute-start | bytes 73736 | tf_op jit(solution)/shard_map/ppermute | solution.py:623
  32.4 0.0 copy-start
  32.4 0.9 %copy-done = f32[456,128]{1,0:T(8,128)S(1)} copy-done((f32[456,128]{1,0:T(8,128)S(1)}, f32[456,128]{1,0:T(8,128)}, u32[]{:S(2)}) %copy-start) | copy-done | bytes 233496
  33.3 1.2 %shard_map.123 = (bf16[384,256]{1,0:T(8,128)(2,1)S(1)}, bf16[384,128]{1,0:T(8,128)(2,1)S(1)}, bf16[1152,128]{1,0:T(8,128)(2,1)S(1)}, f32[8,128]{1,0:T(8,128)S(1)...) custom-call(f32[456,128]{1,0:T(8,128)S(1)} %copy-done), custom_call_target="tpu_custom_call" | custom-call | tf_op jit(solution)/shard_map/pallas_call | solution.py:606
  34.5 0.0 all-to-all-done.arrived_ref
  34.6 0.6 shard_map.124
  35.1 3.4 %collective-permute-done.1.m2_ref = f32[48,128]{1,0:T(8,128)S(1)} collective-permute-done((f32[48,128]{1,0:T(8,128)}, f32[48,128]{1,0:T(8,128)S(1)}, u32[]{:S(2)}, u32[]{:S(2)}) %collective-permute-start.1) | collective-permute-done | bytes 24608 | tf_op jit(solution)/shard_map/ppermute | solution.py:623
  38.5 0.0 collective-permute-done.3.p2_ref
  38.5 0.0 collective-permute-done.2.p1_ref
  38.5 0.0 collective-permute-done.m1_ref
  38.5 0.0 copy-start.1
  38.6 0.0 copy-start.2
  38.6 4.9 %shard_map.125 = (f32[4,192,128]{2,1,0:T(8,128)S(1)}, f32[32,1,512]{2,1,0:T(1,128)}) custom-call(f32[192,128]{1,0:T(8,128)S(1)} %get-tuple-element.19.own_ref, f32[192,128]{1,0:T(8,128)S(1)} %collective-permute-done.m1_ref, f32[48,128]{1,0:T(8,128)S(1)} %collective-permute-done.1.m2_ref, f32[192,128]{1,0:T(8,128)S(1)} %collective-permute-done.2.p1_ref, ...), custom_call_target="tpu_custom_call" | custom-call | tf_op jit(solution)/shard_map/pallas_call | solution.py:606
  43.5 3.9 %all-to-all-start.1 = ((f32[32,1,512]{2,1,0:T(1,128)}), f32[32,1,512]{2,1,0:T(1,128)S(1)}, u32[]{:S(2)}, u32[]{:S(2)}) async-start(f32[32,1,512]{2,1,0:T(1,128)} %get-tuple-element.29), calls=%async_computation.1 | async-start | bytes 131072 | tf_op jit(solution)/shard_map/all_to_all | solution.py:627
  47.4 0.7 shard_map.126.turned_ref.refs_5_
  48.1 8.2 %all-to-all-done.1.arrived_ref = f32[32,1,512]{2,1,0:T(1,128)S(1)} async-done(((f32[32,1,512]{2,1,0:T(1,128)}), f32[32,1,512]{2,1,0:T(1,128)S(1)}, u32[]{:S(2)}, u32[]{:S(2)}) %all-to-all-start.1) | async-done | bytes 65568 | tf_op jit(solution)/shard_map/all_to_all | solution.py:627
  56.3 0.4 shard_map.127
  56.7 16.9 %all_to_all.15.refs_0_ = f32[16,1,1152]{2,1,0:T(1,128)S(1)} all-to-all(f32[16,1,1152]{2,1,0:T(1,128)S(1)} %shard_map.127), channel_id=1, replica_groups={{0,1,64,65,128,129,192,193,256,257,320,321,384,385,448,449},{2,3,66,67,..., dimensions={0} | all-to-all | bytes 147456 | tf_op jit(solution)/shard_map/all_to_all | solution.py:627
  73.6 0.0 copy-done.1
  73.6 0.0 copy-done.2
  73.6 2.1 %shard_map.128 = (f32[6,64]{1,0:T(8,128)}, f32[3072,128]{1,0:T(8,128)}) custom-call(f32[16,1,1152]{2,1,0:T(1,128)S(1)} %all_to_all.15.refs_0_, f32[8,64]{1,0:T(8,128)S(1)} %get-tuple-element.31.refs_1_, s32[1,64]{1,0:T(1,128)S(1)} %bitcast.6, f32[6,6]{1,0:T(8,128)S(1)} %copy-done.1, f32[8,128]{1,0:T(8,128)S(1)} %get-tuple-element.25.basis_ref.refs_4_, ...), custom_call_target="tpu_custom_call" | custom-call | tf_op jit(solution)/shard_map/pallas_call | solution.py:606
Async XLA Ops:
  3.1 31.5 %all-to-all-start = ((f32[64,1,128]{2,1,0:T(1,128)}), f32[64,1,128]{2,1,0:T(1,128)S(1)}, u32[]{:S(2)}, u32[]{:S(2)}) async-start(f32[64,1,128]{2,1,0:T(1,128)} %get-tuple-element.27), calls=%async_computation | async-start | bytes 65536 | tf_op jit(solution)/shard_map/all_to_all | solution.py:627
  17.9 20.6 %collective-permute-start.3 = (f32[192,128]{1,0:T(8,128)}, f32[192,128]{1,0:T(8,128)S(1)}, u32[]{:S(2)}, u32[]{:S(2)}) collective-permute-start(f32[192,128]{1,0:T(8,128)} %get-tuple-element.20), channel_id=1, source_target_pairs={{0,62},{1,63},{2,0},{3,1},{4,2},{5,3},{6,4},{7,5},{8,6},{9,7},{10,... | collective-permute-start | bytes 294920 | tf_op jit(solution)/shard_map/ppermute | solution.py:623
  24.9 13.7 %collective-permute-start.2 = (f32[192,128]{1,0:T(8,128)}, f32[192,128]{1,0:T(8,128)S(1)}, u32[]{:S(2)}, u32[]{:S(2)}) collective-permute-start(f32[192,128]{1,0:T(8,128)} %get-tuple-element.20), channel_id=1, source_target_pairs={{0,63},{1,0},{2,1},{3,2},{4,3},{5,4},{6,5},{7,6},{8,7},{9,8},{10,9... | collective-permute-start | bytes 294920 | tf_op jit(solution)/shard_map/ppermute | solution.py:623
  27.4 11.1 %collective-permute-start = (f32[192,128]{1,0:T(8,128)}, f32[192,128]{1,0:T(8,128)S(1)}, u32[]{:S(2)}, u32[]{:S(2)}) collective-permute-start(f32[192,128]{1,0:T(8,128)} %get-tuple-element.20), channel_id=1, source_target_pairs={{0,1},{1,2},{2,3},{3,4},{4,5},{5,6},{6,7},{7,8},{8,9},{9,10},{10,1... | collective-permute-start | bytes 294920 | tf_op jit(solution)/shard_map/ppermute | solution.py:623
  30.4 8.1 %collective-permute-start.1 = (f32[48,128]{1,0:T(8,128)}, f32[48,128]{1,0:T(8,128)S(1)}, u32[]{:S(2)}, u32[]{:S(2)}) collective-permute-start(f32[48,128]{1,0:T(8,128)} %get-tuple-element.21), channel_id=1, source_target_pairs={{0,2},{1,3},{2,4},{3,5},{4,6},{5,7},{6,8},{7,9},{8,10},{9,11},{10,... | collective-permute-start | bytes 73736 | tf_op jit(solution)/shard_map/ppermute | solution.py:623
  32.4 0.9 %copy-start = (f32[456,128]{1,0:T(8,128)S(1)}, f32[456,128]{1,0:T(8,128)}, u32[]{:S(2)}) copy-start(f32[456,128]{1,0:T(8,128)} %get-tuple-element.18.rest_ref) | copy-start | bytes 700420
  38.5 35.0 %copy-start.1 = (f32[6,6]{1,0:T(8,128)S(1)}, f32[6,6]{1,0:T(8,128)}, u32[]{:S(2)}) copy-start(f32[6,6]{1,0:T(8,128)} %refs_3_.1) | copy-start | bytes 436
  38.6 35.0 %copy-start.2 = (s32[64]{0:T(128)S(1)}, s32[64]{0:T(128)}, u32[]{:S(2)}) copy-start(s32[64]{0:T(128)} %param.15) | copy-start | bytes 772
  43.5 12.8 %all-to-all-start.1 = ((f32[32,1,512]{2,1,0:T(1,128)}), f32[32,1,512]{2,1,0:T(1,128)S(1)}, u32[]{:S(2)}, u32[]{:S(2)}) async-start(f32[32,1,512]{2,1,0:T(1,128)} %get-tuple-element.29), calls=%async_computation.1 | async-start | bytes 131072 | tf_op jit(solution)/shard_map/all_to_all | solution.py:627

commit v7 on v5

--- a/solution.py
+++ b/solution.py
@@ -85,15 +85,15 @@
     return bdot(a.astype(BF16), b.astype(BF16))
 
 
-def pack(load, phase, out_ref):
+def pack(load, phase, out_ref, base):
     for c in range(6):
-        out_ref[pl.ds(c, HALF, stride=8), :] = jnp.concatenate(
+        out_ref[pl.ds(base + c, HALF, stride=8), :] = jnp.concatenate(
             [load[pl.ds(c, 1), pl.ds(par, HALF, stride=2), :][0] for par in range(2)], axis=1
         )
     labels = [phase[pl.ds(0, 1), pl.ds(par, HALF, stride=2), :][0] for par in range(2)]
     weights = 1.0 + 2.0 * jnp.concatenate(labels, axis=1).astype(F32)
-    out_ref[pl.ds(6, HALF, stride=8), :] = weights
-    out_ref[pl.ds(7, HALF, stride=8), :] = jnp.zeros((HALF, LANES), F32)
+    out_ref[pl.ds(base + 6, HALF, stride=8), :] = weights
+    out_ref[pl.ds(base + 7, HALF, stride=8), :] = jnp.zeros((HALF, LANES), F32)
 
 
 def faces(disp, listed, out_ref):
@@ -171,12 +171,11 @@
 
 
 def first_kernel(*refs):
-    face_ref, pack_ref, edge_ref, rest_ref, *held, sems = refs[10:]
+    face_ref, rest_ref, *held, sems = refs[10:]
     fetch(refs[:10], held, sems)
     disp, listed, load, phase, conn, maps, assign, root, chain, bridge = held
     faces(disp, listed, face_ref)
-    pack(load, phase, pack_ref)
-    edge_ref[...] = edge_rows(pack_ref[...])
+    pack(load, phase, rest_ref, 264)
     points = conn.shape[1]
     blank = jnp.zeros((7, points), F32)
     for c in range(6):
@@ -188,12 +187,12 @@
     rest_ref[184:248, :] = jnp.concatenate([root[...], chain[...]], axis=1)
     wide = jnp.concatenate([bridge[...], jnp.zeros((IFACE, LANES - IFACE), F32)], axis=1)
     rest_ref[248:264, :] = wide
-    rest_ref[264:, :] = pack_ref[...]
-
-
-def tables(rest_ref, w1, wb, w2, basis_ref, strain_part, own_part):
+
+
+def tables(rest_ref, w1, wb, w2, basis_ref, strain_part, own_part, edge_ref):
     strain_part[...] = rest_ref[:184]
     own_part[...] = rest_ref[264:]
+    edge_ref[...] = edge_rows(rest_ref[264:])
     root, chain = rest_ref[184:248, :BLOCK], rest_ref[184:248, BLOCK:]
     bridge = rest_ref[248:264, :IFACE]
     zero = jnp.zeros((BLOCK, BLOCK), F32)
@@ -648,15 +647,14 @@
     labels = jnp.transpose(phases, (0, 2, 1))
     sources = [displacement, listed, load, labels, connectivity, strain_map, assign]
     sources += [stiff_root, chain_map, bridge_map]
-    outgoing, packed, edge, rest = call(
+    outgoing, rest = call(
         first_kernel,
-        [arr(devs, 1, LANES), arr(ROWS, LANES), arr(QUARTER, LANES), arr(264 + ROWS, LANES)],
+        [arr(devs, 1, LANES), arr(264 + ROWS, LANES)],
         *sources,
         own_copies=len(sources),
     )
     arrived = exchange(outgoing, "dev")
-    near = [shifted(packed, 1), shifted(edge, 2), shifted(packed, -1), shifted(packed, -2)]
-    *weights, terms, strain_part, own_part = call(
+    *weights, terms, strain_part, packed, edge = call(
         tables,
         [
             arr(3 * LANES, 2 * LANES, dtype=BF16),
@@ -665,9 +663,11 @@
             arr(8, LANES),
             arr(184, LANES),
             arr(ROWS, LANES),
+            arr(QUARTER, LANES),
         ],
         rest,
     )
+    near = [shifted(packed, 1), shifted(edge, 2), shifted(packed, -1), shifted(packed, -2)]
     cand, strain = call(
         strain_kernel,
         [arr(1, LANES), arr(8, points)],
@@ -678,7 +678,7 @@
     vectors, send = call(
         krylov_kernel,
         [arr(4, ROWS, LANES), arr(devs // 2, 1, 4 * LANES)],
-        own_part,
+        packed,
         *near,
         *weights,
         terms,

time: 75.4 us -> 77.3 us (1.025)
  waiting for transfers between devices: 10.7 us -> 12.7 us
  blocking collectives: 12.6 us -> 11.8 us
  starting transfers between devices: 37.7 us -> 38.5 us
    ppermute x4, waiting for transfers between devices: 3.4 us -> 5.37 us  [shifted(): lax.ppermute(x, 'dev', [(i, (i + by) % devices) for i in range(devices)])]
    all_to_all x1, blocking collectives: 12.6 us -> 11.8 us  [exchange(): lax.all_to_all(x, axis, split_axis=0, concat_axis=0, tiled=True, axis_ind...]
where the time goes in v7:
time: 77.3 us; the launch traced here: 76.9 us
  starting transfers between devices  38.5 us (50%)
  waiting for transfers between devices  12.7 us (16%)
  Pallas kernels  12.2 us (16%)
  blocking collectives  11.8 us (15%)
  local copies, waits for them, and re-layouts  0.97 us (1%)
    all_to_all x2, starting transfers between devices, exchange(): lax.all_to_all(x, axis, split_axis=0, concat_axis=0, tiled=True, axis_ind...  24.1 us
    ppermute x4, starting transfers between devices, shifted(): lax.ppermute(x, 'dev', [(i, (i + by) % devices) for i in range(devices)])  14.4 us
    pallas_call x7, Pallas kernels, call(): pl.pallas_call(kernel, out_shape=outs, in_specs=spaces[:len(args)], out_s...  12.2 us
    all_to_all x1, blocking collectives, exchange(): lax.all_to_all(x, axis, split_axis=0, concat_axis=0, tiled=True, axis_ind...  11.8 us
    all_to_all x2, waiting for transfers between devices, exchange(): lax.all_to_all(x, axis, split_axis=0, concat_axis=0, tiled=True, axis_ind...  7.32 us
    ppermute x4, waiting for transfers between devices, shifted(): lax.ppermute(x, 'dev', [(i, (i + by) % devices) for i in range(devices)])  5.37 us
  transfers between devices with their start and end apart: 6, of which 2 were waited for; matrix products, arithmetic and copies ran while one was open for 0% of the time, Pallas kernels for 3%

profile of v7, /device:TPU:1, one launch (start us, length us, event | category | flops | bytes accessed | tf_op | source)
XLA Modules:
  0.0 76.9 jit_solution(17499408855867576399)
XLA Ops:
  0.6 2.4 %shard_map.122 = (f32[64,1,128]{2,1,0:T(1,128)}, f32[456,128]{1,0:T(8,128)}) custom-call(f32[3,256]{1,0:T(4,128)} %refs_0_.1, s32[1,16,64]{2,1,0:T(8,128)} %bitcast.9, f32[6,48,64]{2,1,0:T(8,128)} %bitcast.7, s32[1,48,64]{2,1,0:T(8,128)} %bitcast.8, s32[8,64]{1,0:T(8,128)} %refs_4_.1, f32[6,24,64]{2,1,0:T(8,128)} %refs_5_.1, s32[1,64]{1,0:T(1,128)} %bitcast.5, ...), custom_call_target="tpu_custom_call" | custom-call | tf_op jit(solution)/shard_map/pallas_call | solution.py:601
  3.1 14.8 %all-to-all-start = ((f32[64,1,128]{2,1,0:T(1,128)}), f32[64,1,128]{2,1,0:T(1,128)S(1)}, u32[]{:S(2)}, u32[]{:S(2)}) async-start(f32[64,1,128]{2,1,0:T(1,128)} %get-tuple-element.25), calls=%async_computation | async-start | bytes 65536 | tf_op jit(solution)/shard_map/all_to_all | solution.py:622
  17.9 0.0 copy-start
  17.9 0.9 %copy-done = f32[456,128]{1,0:T(8,128)S(1)} copy-done((f32[456,128]{1,0:T(8,128)S(1)}, f32[456,128]{1,0:T(8,128)}, u32[]{:S(2)}) %copy-start) | copy-done | bytes 233496
  18.9 1.2 %shard_map.123 = (bf16[384,256]{1,0:T(8,128)(2,1)S(1)}, bf16[384,128]{1,0:T(8,128)(2,1)S(1)}, bf16[1152,128]{1,0:T(8,128)(2,1)S(1)}, f32[8,128]{1,0:T(8,128)S(1)...) custom-call(f32[456,128]{1,0:T(8,128)S(1)} %copy-done), custom_call_target="tpu_custom_call" | custom-call | tf_op jit(solution)/shard_map/pallas_call | solution.py:601
  20.1 6.9 %collective-permute-start.3 = (f32[192,128]{1,0:T(8,128)S(1)}, f32[192,128]{1,0:T(8,128)S(1)}, u32[]{:S(2)}, u32[]{:S(2)}) collective-permute-start(f32[192,128]{1,0:T(8,128)S(1)} %get-tuple-element.18.own_ref), channel_id=1, source_target_pairs={{0,62},{1,63},{2,0},{3,1},{4,2},{5,3},{6,4},{7,5},{8,6},{9,7},{10,... | collective-permute-start | bytes 294920 | tf_op jit(solution)/shard_map/ppermute | solution.py:618
  27.0 2.5 %collective-permute-start.2 = (f32[192,128]{1,0:T(8,128)S(1)}, f32[192,128]{1,0:T(8,128)S(1)}, u32[]{:S(2)}, u32[]{:S(2)}) collective-permute-start(f32[192,128]{1,0:T(8,128)S(1)} %get-tuple-element.18.own_ref), channel_id=1, source_target_pairs={{0,63},{1,0},{2,1},{3,2},{4,3},{5,4},{6,5},{7,6},{8,7},{9,8},{10,9... | collective-permute-start | bytes 294920 | tf_op jit(solution)/shard_map/ppermute | solution.py:618
  29.6 3.0 %collective-permute-start = (f32[192,128]{1,0:T(8,128)S(1)}, f32[192,128]{1,0:T(8,128)S(1)}, u32[]{:S(2)}, u32[]{:S(2)}) collective-permute-start(f32[192,128]{1,0:T(8,128)S(1)} %get-tuple-element.18.own_ref), channel_id=1, source_target_pairs={{0,1},{1,2},{2,3},{3,4},{4,5},{5,6},{6,7},{7,8},{8,9},{9,10},{10,1... | collective-permute-start | bytes 294920 | tf_op jit(solution)/shard_map/ppermute | solution.py:618
  32.6 1.9 %collective-permute-start.1 = (f32[48,128]{1,0:T(8,128)S(1)}, f32[48,128]{1,0:T(8,128)S(1)}, u32[]{:S(2)}, u32[]{:S(2)}) collective-permute-start(f32[48,128]{1,0:T(8,128)S(1)} %get-tuple-element.19), channel_id=1, source_target_pairs={{0,2},{1,3},{2,4},{3,5},{4,6},{5,7},{6,8},{7,9},{8,10},{9,11},{10,... | collective-permute-start | bytes 73736 | tf_op jit(solution)/shard_map/ppermute | solution.py:618
  34.5 0.0 all-to-all-done.arrived_ref
  34.6 0.6 shard_map.124
  35.1 0.0 copy-start.1
  35.1 0.0 copy-start.2
  35.1 5.4 %collective-permute-done.1.m2_ref = f32[48,128]{1,0:T(8,128)S(1)} collective-permute-done((f32[48,128]{1,0:T(8,128)S(1)}, f32[48,128]{1,0:T(8,128)S(1)}, u32[]{:S(2)}, u32[]{:S(2)}) %collective-permute-start.1) | collective-permute-done | bytes 24608 | tf_op jit(solution)/shard_map/ppermute | solution.py:618
  40.5 0.0 collective-permute-done.3.p2_ref
  40.5 0.0 collective-permute-done.2.p1_ref
  40.5 0.0 collective-permute-done.m1_ref
  40.5 4.2 %shard_map.125 = (f32[4,192,128]{2,1,0:T(8,128)S(1)}, f32[32,1,512]{2,1,0:T(1,128)S(1)}) custom-call(f32[192,128]{1,0:T(8,128)S(1)} %get-tuple-element.18.own_ref, f32[192,128]{1,0:T(8,128)S(1)} %collective-permute-done.m1_ref, f32[48,128]{1,0:T(8,128)S(1)} %collective-permute-done.1.m2_ref, f32[192,128]{1,0:T(8,128)S(1)} %collective-permute-done.2.p1_ref, ...), custom_call_target="tpu_custom_call" | custom-call | tf_op jit(solution)/shard_map/pallas_call | solution.py:601
  44.8 11.8 %all_to_all.15.arrived_ref = f32[32,1,512]{2,1,0:T(1,128)S(1)} all-to-all(f32[32,1,512]{2,1,0:T(1,128)S(1)} %get-tuple-element.27), channel_id=1, replica_groups={{0,2,4,6,8,10,12,14,16,18,20,22,24,26,28,30,32,34,36,38,40,42,44,46,48,..., dimensions={0} | all-to-all | bytes 131072 | tf_op jit(solution)/shard_map/all_to_all | solution.py:622
  56.6 1.0 %shard_map.126 = f32[16,1,1152]{2,1,0:T(1,128)} custom-call(f32[32,1,512]{2,1,0:T(1,128)S(1)} %all_to_all.15.arrived_ref), custom_call_target="tpu_custom_call" | custom-call | tf_op jit(solution)/shard_map/pallas_call | solution.py:601
  57.6 9.2 %all-to-all-start.2 = ((f32[16,1,1152]{2,1,0:T(1,128)}), f32[16,1,1152]{2,1,0:T(1,128)S(1)}, u32[]{:S(2)}, u32[]{:S(2)}) async-start(f32[16,1,1152]{2,1,0:T(1,128)} %shard_map.126), calls=%async_computation.2 | async-start | bytes 147456 | tf_op jit(solution)/shard_map/all_to_all | solution.py:622
  66.8 0.7 shard_map.127.refs_5_
  67.5 7.3 %all-to-all-done.2.refs_0_ = f32[16,1,1152]{2,1,0:T(1,128)S(1)} async-done(((f32[16,1,1152]{2,1,0:T(1,128)}), f32[16,1,1152]{2,1,0:T(1,128)S(1)}, u32[]{:S(2)}, u32[]{:S(2)}) %all-to-all-start.2) | async-done | bytes 73760 | tf_op jit(solution)/shard_map/all_to_all | solution.py:622
  74.8 0.0 copy-done.1
  74.8 0.0 copy-done.2
  74.8 2.1 %shard_map.128 = (f32[6,64]{1,0:T(8,128)}, f32[3072,128]{1,0:T(8,128)}) custom-call(f32[16,1,1152]{2,1,0:T(1,128)S(1)} %all-to-all-done.2.refs_0_, f32[8,64]{1,0:T(8,128)S(1)} %get-tuple-element.28.refs_1_, s32[1,64]{1,0:T(1,128)S(1)} %bitcast.6, f32[6,6]{1,0:T(8,128)S(1)} %copy-done.1, f32[8,128]{1,0:T(8,128)S(1)} %get-tuple-element.23.basis_ref.refs_4_, ...), custom_call_target="tpu_custom_call" | custom-call | tf_op jit(solution)/shard_map/pallas_call | solution.py:601
Async XLA Ops:
  3.1 31.5 %all-to-all-start = ((f32[64,1,128]{2,1,0:T(1,128)}), f32[64,1,128]{2,1,0:T(1,128)S(1)}, u32[]{:S(2)}, u32[]{:S(2)}) async-start(f32[64,1,128]{2,1,0:T(1,128)} %get-tuple-element.25), calls=%async_computation | async-start | bytes 65536 | tf_op jit(solution)/shard_map/all_to_all | solution.py:622
  17.9 0.9 %copy-start = (f32[456,128]{1,0:T(8,128)S(1)}, f32[456,128]{1,0:T(8,128)}, u32[]{:S(2)}) copy-start(f32[456,128]{1,0:T(8,128)} %get-tuple-element.17.rest_ref) | copy-start | bytes 700420
  20.1 20.4 %collective-permute-start.3 = (f32[192,128]{1,0:T(8,128)S(1)}, f32[192,128]{1,0:T(8,128)S(1)}, u32[]{:S(2)}, u32[]{:S(2)}) collective-permute-start(f32[192,128]{1,0:T(8,128)S(1)} %get-tuple-element.18.own_ref), channel_id=1, source_target_pairs={{0,62},{1,63},{2,0},{3,1},{4,2},{5,3},{6,4},{7,5},{8,6},{9,7},{10,... | collective-permute-start | bytes 294920 | tf_op jit(solution)/shard_map/ppermute | solution.py:618
  27.0 13.5 %collective-permute-start.2 = (f32[192,128]{1,0:T(8,128)S(1)}, f32[192,128]{1,0:T(8,128)S(1)}, u32[]{:S(2)}, u32[]{:S(2)}) collective-permute-start(f32[192,128]{1,0:T(8,128)S(1)} %get-tuple-element.18.own_ref), channel_id=1, source_target_pairs={{0,63},{1,0},{2,1},{3,2},{4,3},{5,4},{6,5},{7,6},{8,7},{9,8},{10,9... | collective-permute-start | bytes 294920 | tf_op jit(solution)/shard_map/ppermute | solution.py:618
  29.6 10.9 %collective-permute-start = (f32[192,128]{1,0:T(8,128)S(1)}, f32[192,128]{1,0:T(8,128)S(1)}, u32[]{:S(2)}, u32[]{:S(2)}) collective-permute-start(f32[192,128]{1,0:T(8,128)S(1)} %get-tuple-element.18.own_ref), channel_id=1, source_target_pairs={{0,1},{1,2},{2,3},{3,4},{4,5},{5,6},{6,7},{7,8},{8,9},{9,10},{10,1... | collective-permute-start | bytes 294920 | tf_op jit(solution)/shard_map/ppermute | solution.py:618
  32.6 7.9 %collective-permute-start.1 = (f32[48,128]{1,0:T(8,128)S(1)}, f32[48,128]{1,0:T(8,128)S(1)}, u32[]{:S(2)}, u32[]{:S(2)}) collective-permute-start(f32[48,128]{1,0:T(8,128)S(1)} %get-tuple-element.19), channel_id=1, source_target_pairs={{0,2},{1,3},{2,4},{3,5},{4,6},{5,7},{6,8},{7,9},{8,10},{9,11},{10,... | collective-permute-start | bytes 73736 | tf_op jit(solution)/shard_map/ppermute | solution.py:618
  35.1 39.7 %copy-start.1 = (f32[6,6]{1,0:T(8,128)S(1)}, f32[6,6]{1,0:T(8,128)}, u32[]{:S(2)}) copy-start(f32[6,6]{1,0:T(8,128)} %refs_3_.1) | copy-start | bytes 436
  35.1 39.7 %copy-start.2 = (s32[64]{0:T(128)S(1)}, s32[64]{0:T(128)}, u32[]{:S(2)}) copy-start(s32[64]{0:T(128)} %param.15) | copy-start | bytes 772
  57.6 17.2 %all-to-all-start.2 = ((f32[16,1,1152]{2,1,0:T(1,128)}), f32[16,1,1152]{2,1,0:T(1,128)S(1)}, u32[]{:S(2)}, u32[]{:S(2)}) async-start(f32[16,1,1152]{2,1,0:T(1,128)} %shard_map.126), calls=%async_computation.2 | async-start | bytes 147456 | tf_op jit(solution)/shard_map/all_to_all | solution.py:622
